TPU v7x, 256 devices: a whole 4x4x8 slice. The times are simulated.
256 devices in a mesh: lat: 16 (over z, x_hi), lon: 16 (over x_lo, y, core).
Axes of the slice: x: 4 (x_hi: 2, x_lo: 2; x = x_hi * 2 + x_lo), y: 4, z: 8, core: 2. Of those that a mesh axis runs over, the one named last changes fastest.
Arguments:
- latents: bfloat16 [4, 96, 384, 512], P(None, 'lat', 'lon'), may hold values from -6 to 6
- mask_ids: int32 [96, 384], P('lat', 'lon'), may hold values from 0 to 3
- w_qkv: bfloat16 [512, 1536], replicated, may hold values from -0.35355339 to 0.35355339
- w_out: bfloat16 [512, 512], replicated, may hold values from -0.25 to 0.25
- w_kv: bfloat16 [512, 1024], replicated, may hold values from -0.25 to 0.25
- level_queries: bfloat16 [13, 512], replicated, may hold values from -12 to 12
- w_o: bfloat16 [512, 512], replicated, may hold values from -0.25 to 0.25
- w_head: bfloat16 [512, 80], replicated, may hold values from -0.25 to 0.25
- field_cotangent: bfloat16 [96, 384, 1040], P('lat', 'lon'), may hold values from -6 to 6
Outputs:
- mixed_latents: bfloat16 [4, 96, 384, 512], P(None, 'lat', 'lon')
- decoded: bfloat16 [96, 384, 1040], P('lat', 'lon')
- grad_kv: float32 [512, 1024], replicated
- grad_queries: float32 [13, 512], replicated
- grad_o: float32 [512, 512], replicated
- grad_head: float32 [512, 80], replicated
All inputs are finite; a program needn't handle non-finite values.
Results may differ from a plain program's by a relative error of at most 0.025.
Values may be sent and summed in bfloat16 or wider, within the bound.
No kernel may reach another device: no remote copies, remote signals or barrier semaphores. Data moves between devices by JAX's collectives and lax.ppermute only.
A program may use at most 128 MiB of HBM per device.

v0:
```python
import math

import jax
import jax.numpy as jnp
from jax import lax
from jax.sharding import PartitionSpec as P

HEADS = 8
PLEV = 13
OUTS = 80
WL = 2
WH = 6
WW = 12


norm_eps = 1e-05
clip_eps = 1e-06


def shifted_2(block, axis, distance):
    devices = range(lax.axis_size(axis))
    route = [((i - distance) % len(devices), i) for i in devices]
    return lax.ppermute(block, axis, route)


def layer_norm(values):
    wide = values.astype(jnp.float32)
    center = wide - jnp.mean(wide, axis=-1, keepdims=True)
    spread = jnp.mean(center * center, axis=-1, keepdims=True)
    return (center * lax.rsqrt(spread + norm_eps)).astype(jnp.bfloat16)


def window_attention(block_tile, region, w_qkv, w_out):
    levels, height, across, features = block_tile.shape
    head_size = features // HEADS
    normed = layer_norm(block_tile).reshape(-1, features)
    projected = jnp.dot(normed, w_qkv, preferred_element_type=jnp.float32).astype(jnp.bfloat16)
    grid_shape = (levels // WL, WL, height // WH, WH, across // WW, WW)
    grouped = projected.reshape(grid_shape + (3, HEADS, head_size)).transpose(
        0, 2, 4, 1, 3, 5, 6, 7, 8
    )
    grouped = grouped.reshape(-1, WL * WH * WW, 3, HEADS, head_size)
    labels = region.reshape(grid_shape).transpose(0, 2, 4, 1, 3, 5).reshape(-1, WL * WH * WW)
    scores = jnp.einsum(
        "wqhe,wkhe->whqk", grouped[:, :, 0], grouped[:, :, 1], preferred_element_type=jnp.float32
    ) / math.sqrt(head_size)
    allowed = labels[:, None, :, None] == labels[:, None, None, :]
    scores = jnp.where(allowed, scores, -jnp.inf)
    weights = jax.nn.softmax(scores, axis=-1).astype(jnp.bfloat16)
    context = jnp.einsum(
        "whqk,wkhe->wqhe", weights, grouped[:, :, 2], preferred_element_type=jnp.float32
    ).astype(jnp.bfloat16)
    context = context.reshape(levels // WL, height // WH, across // WW, WL, WH, WW, features)
    context = context.transpose(0, 3, 1, 4, 2, 5, 6).reshape(-1, features)
    mixed = block_tile.reshape(-1, features).astype(jnp.float32) + jnp.dot(
        context, w_out, preferred_element_type=jnp.float32
    )
    return mixed.astype(jnp.bfloat16).reshape(levels, height, across, features)


def decode_block(latent_block, cot_block, w_kv, level_queries, w_o, w_head):
    levels, patches, features = latent_block.shape
    head_size = features // HEADS
    scale = 1.0 / math.sqrt(head_size)
    normed = layer_norm(latent_block).reshape(levels * patches, features)
    projected = jnp.dot(normed, w_kv, preferred_element_type=jnp.float32).astype(jnp.bfloat16)
    split_kv = projected.reshape(levels, patches, 2, HEADS, head_size).astype(jnp.float32)
    key_vecs = split_kv[:, :, 0]
    value_vecs = split_kv[:, :, 1]
    query_vecs = level_queries.astype(jnp.float32).reshape(PLEV, HEADS, head_size)
    scores = jnp.einsum("ahe,lphe->phal", query_vecs, key_vecs) * scale
    weights = jax.nn.softmax(scores, axis=-1)
    context = (
        jnp.einsum("phal,lphe->pahe", weights, value_vecs)
        .astype(jnp.bfloat16)
        .reshape(patches * PLEV, features)
    )
    hidden = jnp.dot(context, w_o, preferred_element_type=jnp.float32).reshape(
        patches, PLEV, features
    )
    hidden = (
        (hidden + level_queries.astype(jnp.float32)[None])
        .astype(jnp.bfloat16)
        .reshape(patches * PLEV, features)
    )
    fields = jnp.dot(hidden, w_head, preferred_element_type=jnp.float32).astype(jnp.bfloat16)
    upstream = cot_block.reshape(patches * PLEV, OUTS)
    grad_head = jnp.dot(hidden.T, upstream, preferred_element_type=jnp.float32)
    d_hidden = jnp.dot(upstream, w_head.T, preferred_element_type=jnp.float32).astype(jnp.bfloat16)
    grad_out = jnp.dot(context.T, d_hidden, preferred_element_type=jnp.float32)
    d_context = jnp.dot(d_hidden, w_o.T, preferred_element_type=jnp.float32).reshape(
        patches, PLEV, HEADS, head_size
    )
    d_weights = jnp.einsum("pahe,lphe->phal", d_context, value_vecs)
    d_scores = weights * (d_weights - jnp.sum(weights * d_weights, axis=-1, keepdims=True)) * scale
    d_values = jnp.einsum("phal,pahe->lphe", weights, d_context)
    d_keys = jnp.einsum("phal,ahe->lphe", d_scores, query_vecs)
    grad_query = jnp.einsum("phal,lphe->ahe", d_scores, key_vecs).reshape(PLEV, features)
    grad_query = grad_query + jnp.sum(
        d_hidden.astype(jnp.float32).reshape(patches, PLEV, features), axis=0
    )
    d_pair = (
        jnp.stack([d_keys, d_values], axis=2)
        .astype(jnp.bfloat16)
        .reshape(levels * patches, 2 * features)
    )
    grad_kv = jnp.dot(normed.T, d_pair, preferred_element_type=jnp.float32)
    return (fields.reshape(patches, PLEV * OUTS), grad_kv, grad_query, grad_out, grad_head)


def per_device(latents, mask_ids, w_qkv, w_out, w_kv, level_queries, w_o, w_head, field_cotangent):
    levels, height, across, features = latents.shape
    shift_levels = WL // 2
    shift_rows = WH // 2
    shift_cols = WW // 2
    lat_count = lax.axis_size("lat")
    strip, strip_ids = shifted_2((latents[:, :shift_rows], mask_ids[:shift_rows]), "lat", -1)
    framed = jnp.concatenate([latents[:, shift_rows:], strip], axis=1)
    framed_ids = jnp.concatenate([mask_ids[shift_rows:], strip_ids], axis=0)
    side, side_ids = shifted_2((framed[:, :, :shift_cols], framed_ids[:, :shift_cols]), "lon", -1)
    shifted = jnp.concatenate([framed[:, :, shift_cols:], side], axis=2)
    shifted_ids = jnp.concatenate([framed_ids[:, shift_cols:], side_ids], axis=1).astype(jnp.int32)
    shifted = jnp.roll(shifted, -shift_levels, axis=0)
    row_position = lax.axis_index("lat") * height + shift_rows + jnp.arange(height)
    lat_flag = (row_position >= height * lat_count).astype(jnp.int32)
    lev_flag = (jnp.arange(levels) + shift_levels >= levels).astype(jnp.int32)
    region = shifted_ids[None] + 4 * lat_flag[None, :, None] + 8 * lev_flag[:, None, None]
    mixed = window_attention(shifted, region, w_qkv, w_out)
    mixed = jnp.roll(mixed, shift_levels, axis=0)
    returned_cols = shifted_2(mixed[:, :, across - shift_cols :], "lon", 1)
    row_frame = jnp.concatenate([returned_cols, mixed[:, :, : across - shift_cols]], axis=2)
    returned_rows = shifted_2(row_frame[:, height - shift_rows :], "lat", 1)
    owned = jnp.concatenate([returned_rows, row_frame[:, : height - shift_rows]], axis=1)
    fields, grad_kv, grad_query, grad_out, grad_head = decode_block(
        owned.reshape(levels, height * across, features),
        field_cotangent.reshape(height * across, PLEV * OUTS),
        w_kv,
        level_queries,
        w_o,
        w_head,
    )
    decoded = fields.reshape(height, across, PLEV * OUTS)
    query_columns = grad_query.T
    entries = features * 2 * features + PLEV * features + features * features + features * OUTS
    limit = math.sqrt(entries)
    totals = lax.psum((grad_kv, query_columns, grad_out, grad_head), ("lat", "lon"))
    squares = (
        jnp.sum(totals[0] * totals[0])
        + jnp.sum(totals[1] * totals[1])
        + jnp.sum(totals[2] * totals[2])
        + jnp.sum(totals[3] * totals[3])
    )
    factor = jnp.minimum(1.0, limit * lax.rsqrt(squares + clip_eps))
    clipped = (totals[0] * factor, totals[1] * factor, totals[2] * factor, totals[3] * factor)
    return (owned, decoded, clipped[0], clipped[1].T, clipped[2], clipped[3])


def solution(mesh):
    in_specs = (
        P(None, "lat", "lon", None),
        P("lat", "lon"),
        P(),
        P(),
        P(),
        P(),
        P(),
        P(),
        P("lat", "lon", None),
    )
    out_specs = (P(None, "lat", "lon", None), P("lat", "lon", None), P(), P(), P(), P())
    return jax.shard_map(
        per_device, mesh=mesh, in_specs=in_specs, out_specs=out_specs, check_vma=False
    )
```

profile of v0, /device:TPU:1, one launch (start us, length us, event | category | flops | bytes accessed | tf_op | source)
XLA Modules:
  0.0 443.0 jit_solution(5873666083806617494)
XLA Ops:
  8.4 8.9 %collective-permute-start = (bf16[4,3,24,512]{3,2,1,0:T(8,128)(2,1)S(1)}, bf16[4,3,24,512]{3,2,1,0:T(8,128)(2,1)S(1)}, u32[]{:S(2)}, u32[]{:S(2)}) collective-permute-start(bf16[4,3,24,512]{3,2,1,0:T(8,128)(2,1)S(1)} %get-tuple-element.23), channel_id=1, source_target_pairs={{16,0},{32,16},{48,32},{64,48},{80,64},{96,80},{112,96},{128,112},... | collective-permute-start | bytes 884744 | tf_op jit(solution)/shard_map/ppermute | solution.py:23
  19.9 2.5 reshape_reshape.7
  24.7 2.4 collective-permute-done.3
  29.3 4.0 collective-permute-done.1
  36.6 5.6 %reshape.247 = bf16[2,2,1,6,2,12,3,8,64]{8,7,6,5,4,3,1,0,2:T(8,128)(2,1)} reshape(bf16[576,1536]{1,0:T(8,128)(2,1)} %convolution_convert_fusion) | data formatting | bytes 3538944 | tf_op jit(solution)/shard_map/reshape | solution.py:39
  42.1 2.6 copy.29
  46.6 2.6 copy.64
  60.6 2.6 collective-permute-done.4
  63.5 2.7 collective-permute-start.5
  67.4 3.4 reshape.254
  70.8 3.2 collective-permute-done.5
  81.9 3.3 fusion.40
  85.2 3.1 copy.66
  88.3 6.1 %fusion.3 = f32[144,8,13,4]{2,3,1,0:T(4,128)} fusion(bf16[144,13,8,64]{3,2,1,0:T(8,128)(2,1)} %reshape.254, bf16[4,144,1,8,64]{4,0,3,1,2:T(4,128)(2,1)S(1)} %copy.66), kind=kOutput, calls=%fused_computation.3 | convolution fusion | flops 7667712 | bytes 2746368 | tf_op jit(solution)/shard_map/pahe,lphe->phal/dot_general | solution.py:94
  94.4 2.6 copy.47
  99.5 4.9 %fusion.1 = bf16[144,8,64,4]{2,3,1,0:T(4,128)(2,1)} fusion(bf16[144,8,13,4]{2,3,1,0:T(4,128)(2,1)} %copy.41, bf16[144,13,8,64]{3,2,1,0:T(8,128)(2,1)} %reshape.254), kind=kOutput, calls=%fused_computation.1 | convolution fusion | flops 7667712 | bytes 2626560 | tf_op jit(solution)/shard_map/phal,pahe->lphe/dot_general | solution.py:96
  106.5 2.9 copy.42
  109.4 3.8 copy.54
  113.7 2.8 copy.51
  116.9 3.1 copy.52
  120.0 3.9 convert_element_type.123
  123.9 5.1 %dot_general.63 = bf16[144,13,512]{2,0,1:T(8,128)(2,1)S(1)} reshape(bf16[144,13,8,64]{3,2,0,1:T(8,128)(2,1)} %copy.42) | data formatting | bytes 3833856 | tf_op jit(solution)/shard_map/dot_general | solution.py:78
  131.2 2.5 copy.43
  133.7 2.7 reshape.253
  138.6 6.3 %reshape.258 = bf16[1872,512]{1,0:T(8,128)(2,1)} reshape(bf16[144,13,8,64]{3,2,1,0:T(8,128)(2,1)} %copy.54) | data formatting | bytes 3833856 | tf_op jit(solution)/shard_map/reshape | solution.py:76
  144.9 4.4 fusion.48
  151.7 4.3 reshape.262
  156.0 2.8 reduce_sum.116
  163.3 87.0 %psum.29 = f32[512,13]{0,1:T(8,128)S(1)} all-reduce(f32[512,13]{0,1:T(8,128)S(1)} %add_bitcast_fusion), channel_id=1, replica_groups=mesh['lat'=16,'lon'=16] {'lat','lon'}, use_global_device_ids=true, to_apply=%region_12.13 | all-reduce | flops 6656 | bytes 53248 | tf_op jit(solution)/shard_map/psum | solution.py:146
  250.9 172.5 %all-reduce.3.cloned.1.call-done = (f32[512,1024]{1,0:T(8,128)}, f32[512,512]{1,0:T(8,128)}, f32[512,80]{0,1:T(8,128)}) async-done(((f32[512,1024]{1,0:T(8,128)}, f32[512,512]{1,0:T(8,128)}, f32[512,80]{0,1:T(8,128)}), (f32[512,1024]{1,0:T(8,128)}, f32[512,512]{1,0:T(8,128)}, f32[512,80]{0,1:T(8,128)})) %all-reduce.3.cloned.1.call-update) | async-done | bytes 3309584 | tf_op jit(solution)/shard_map/psum | solution.py:146
  423.4 2.8 multiply_reduce_fusion
  432.7 3.2 broadcast_multiply_fusion
  (128 shorter events, 55.0 us)
Async XLA Ops:
  7.2 27.1 %copy-start = (bf16[512,1536]{1,0:T(8,128)(2,1)S(1)}, bf16[512,1536]{1,0:T(8,128)(2,1)}, u32[]{:S(2)}) copy-start(bf16[512,1536]{1,0:T(8,128)(2,1)} %param.11) | copy-start | bytes 4718596
  7.2 416.2 %all-reduce.3.cloned.1.call-start = ((), (), s32[]{:S(2)}) async-start(), calls=%async_computation | async-start | bytes 6619136 | tf_op jit(solution)/shard_map/psum | solution.py:146
  8.4 19.1 %collective-permute-start = (bf16[4,3,24,512]{3,2,1,0:T(8,128)(2,1)S(1)}, bf16[4,3,24,512]{3,2,1,0:T(8,128)(2,1)S(1)}, u32[]{:S(2)}, u32[]{:S(2)}) collective-permute-start(bf16[4,3,24,512]{3,2,1,0:T(8,128)(2,1)S(1)} %get-tuple-element.23), channel_id=1, source_target_pairs={{16,0},{32,16},{48,32},{64,48},{80,64},{96,80},{112,96},{128,112},... | collective-permute-start | bytes 884744 | tf_op jit(solution)/shard_map/ppermute | solution.py:23
  18.2 5.0 %collective-permute-start.2 = (s32[3,24]{1,0:T(4,128)S(1)}, s32[3,24]{1,0:T(4,128)S(1)}, u32[]{:S(2)}, u32[]{:S(2)}) collective-permute-start(s32[3,24]{1,0:T(4,128)S(1)} %get-tuple-element.25), channel_id=1, source_target_pairs={{16,0},{32,16},{48,32},{64,48},{80,64},{96,80},{112,96},{128,112},... | collective-permute-start | bytes 872 | tf_op jit(solution)/shard_map/ppermute | solution.py:23
  23.1 4.0 collective-permute-start.3
  27.6 5.7 %collective-permute-start.1 = (bf16[4,6,6,512]{3,2,1,0:T(8,128)(2,1)S(1)}, bf16[4,6,6,512]{3,2,1,0:T(8,128)(2,1)S(1)}, u32[]{:S(2)}, u32[]{:S(2)}) collective-permute-start(bf16[4,6,6,512]{3,2,1,0:T(8,128)(2,1)S(1)} %pad_maximum_fusion.5), channel_id=1, source_target_pairs={{1,0},{2,1},{3,2},{4,3},{5,4},{6,5},{7,6},{8,7},{9,8},{10,9},{11,1... | collective-permute-start | bytes 442376 | tf_op jit(solution)/shard_map/ppermute | solution.py:23
  50.8 1.6 copy-start.12
  54.5 1.7 copy-start.15
  57.9 1.0 copy-start.17
  58.9 1.0 copy-start.10
  59.0 1.0 copy-start.18
  59.5 6.7 %copy-start.20 = (bf16[512,512]{1,0:T(8,128)(2,1)S(1)}, bf16[512,512]{1,0:T(8,128)(2,1)}, u32[]{:S(2)}) copy-start(bf16[512,512]{1,0:T(8,128)(2,1)} %param.15) | copy-start | bytes 1572868
  59.6 3.7 collective-permute-start.4
  60.6 5.6 %copy-start.2 = (bf16[1872,512]{1,0:T(8,128)(2,1)}, bf16[1872,512]{1,0:T(8,128)(2,1)S(1)}, u32[]{:S(2)}) copy-start(bf16[1872,512]{1,0:T(8,128)(2,1)S(1)} %convolution_convert_fusion.1) | copy-start | bytes 5750788
  63.5 10.6 %collective-permute-start.5 = (bf16[4,3,24,512]{3,2,1,0:T(8,128)(2,1)S(1)}, bf16[4,3,24,512]{3,2,1,0:T(8,128)(2,1)S(1)}, u32[]{:S(2)}, u32[]{:S(2)}) collective-permute-start(bf16[4,3,24,512]{3,2,1,0:T(8,128)(2,1)S(1)} %get-tuple-element.20), channel_id=1, source_target_pairs={{240,0},{0,16},{16,32},{32,48},{48,64},{64,80},{80,96},{96,112},{1... | collective-permute-start | bytes 884744 | tf_op jit(solution)/shard_map/ppermute | solution.py:23
  74.0 2.0 copy-start.19
  74.2 3.6 copy-start.3
  85.2 11.8 %copy-start.4 = (bf16[4,144,1,8,64]{1,0,4,3,2:T(4,128)(2,1)}, bf16[4,144,1,8,64]{1,0,4,3,2:T(4,128)(2,1)S(1)}, u32[]{:S(2)}) copy-start(bf16[4,144,1,8,64]{1,0,4,3,2:T(4,128)(2,1)S(1)} %get-tuple-element.18) | copy-start | bytes 1769476
  96.9 16.3 %copy-start.8 = (f32[144,8,13,4]{0,2,3,1:T(8,128)}, f32[144,8,13,4]{0,2,3,1:T(8,128)S(1)}, u32[]{:S(2)}) copy-start(f32[144,8,13,4]{0,2,3,1:T(8,128)S(1)} %copy.47) | copy-start | bytes 718852
  97.5 15.7 %copy-start.6 = (f32[144,8,13,4]{0,2,3,1:T(8,128)}, f32[144,8,13,4]{0,2,3,1:T(8,128)S(1)}, u32[]{:S(2)}) copy-start(f32[144,8,13,4]{0,2,3,1:T(8,128)S(1)} %get-tuple-element.10) | copy-start | bytes 718852
  97.5 15.7 %copy-start.14 = (f32[144,8,13]{0,2,1:T(8,128)}, f32[144,8,13]{0,2,1:T(8,128)S(1)}, u32[]{:S(2)}) copy-start(f32[144,8,13]{0,2,1:T(8,128)S(1)} %get-tuple-element.9) | copy-start | bytes 179716
  99.5 4.9 %copy-start.9 = (bf16[144,8,13,4]{2,3,1,0:T(4,128)(2,1)S(1)}, bf16[144,8,13,4]{2,3,1,0:T(4,128)(2,1)}, u32[]{:S(2)}) copy-start(bf16[144,8,13,4]{2,3,1,0:T(4,128)(2,1)} %copy.41) | copy-start | bytes 359428
  144.9 4.4 copy-start.13
  156.0 2.8 copy-start.5
  156.0 2.8 copy-start.7
  423.4 2.8 copy-start.11
  423.4 3.7 copy-start.16
  432.1 3.8 copy-start.1
Sparse Core Ops, SparseCore 0:
  151.8 271.5 all-reduce.2
where the time goes:
time: 449 us; the launch traced here: 443 us
  waiting for transfers between devices  185 us (41%)
  blocking collectives  87 us (19%)
  local copies, waits for them, and re-layouts  81.6 us (18%)
  matrix products  37 us (8%)
  other arithmetic  19.7 us (4%)
  between operations  17.5 us (4%)
  starting transfers between devices  14.9 us (3%)
    psum x1, waiting for transfers between devices, per_device(): lax.psum((grad_kv, query_columns, grad_out, grad_head), ('lat', 'lon'))  172 us
    psum x1, blocking collectives, per_device(): lax.psum((grad_kv, query_columns, grad_out, grad_head), ('lat', 'lon'))  87 us
    ppermute x6, starting transfers between devices, shifted_2(): return lax.ppermute(block, axis, route)  14.9 us
    ppermute x6, waiting for transfers between devices, shifted_2(): return lax.ppermute(block, axis, route)  12.9 us
    unnamed x46, local copies, waits for them, and re-layouts  9.48 us
  transfers between devices with their start and end apart: 7, of which 6 were waited for; matrix products, arithmetic and copies ran while one was open for 5% of the time, Pallas kernels for 0%

commit v1 on v0

v1 whole, which is shorter than its diff:
```python
import math

import jax
import jax.numpy as jnp
import numpy as np
from jax import lax
from jax.experimental import pallas as pl
from jax.experimental.pallas import tpu as pltpu
from jax.sharding import PartitionSpec as P

D = 512
HEADS = 8
LEV = 4
PLEV = 13
OUTS = 80
WL = 2
WH = 6
WW = 12
PATCHES = WH * 2 * WW
TOKENS = LEV * PATCHES
MAIN = 224
SIDE = 80
PACKED = 2 * MAIN + 2 * SIDE
ROWS = 768
LANES = 128

norm_eps = 1e-05
clip_eps = 1e-06
BF = jnp.bfloat16
F32 = jnp.float32


def window_order():
    level_pairs = ((1, 2), (3, 0))

    def rows_of(levels, rows, cols):
        return [(l * WH + r) * 2 * WW + c for l in levels for r in rows for c in cols]

    order = []
    for rows in ((3, 4, 5), (0, 1, 2)):
        for pair in level_pairs:
            order += rows_of(pair, rows, range(6, 18))
        for pair in level_pairs:
            order += rows_of(pair, rows, range(18, 24)) + [-1] * 4
    for rows in ((3, 4, 5), (0, 1, 2)):
        for pair in level_pairs:
            order += rows_of(pair, rows, range(0, 6)) + [-1] * 4
    return np.array(order)


def pack_matrix():
    order = window_order()
    return (order[:, None] == np.arange(TOKENS)[None, :]).astype(np.float32)


def dot(a, b, contract):
    return lax.dot_general(a, b, (contract, ((), ())), preferred_element_type=F32)


def mm(a, b):
    return dot(a, b, ((1,), (0,)))


def layer_norm(wide):
    center = wide - jnp.mean(wide, axis=-1, keepdims=True)
    spread = jnp.mean(center * center, axis=-1, keepdims=True)
    return (center * lax.rsqrt(spread + norm_eps)).astype(BF)


def pack_kernel(x_ref, perm_ref, main_ref, north_ref, west_ref, corner_ref):
    x = x_ref[...]
    north_ref[...] = mm(perm_ref[MAIN : 2 * MAIN], x).astype(BF)
    west_ref[...] = mm(perm_ref[2 * MAIN : 2 * MAIN + SIDE], x).astype(BF)
    corner_ref[...] = mm(perm_ref[2 * MAIN + SIDE :], x).astype(BF)
    main_ref[...] = mm(perm_ref[:MAIN], x).astype(BF)


def attention_kernel(
    main_ref, north_ref, west_ref, corner_ref, row_ref, col_ref, wqkv_ref, wout_ref,
    main_out, north_out, west_out, corner_out, proj, context,
):
    pieces = (main_ref, north_ref, west_ref, corner_ref)
    wide = jnp.concatenate([ref[...].astype(F32) for ref in pieces], axis=0)
    proj[...] = mm(layer_norm(wide), wqkv_ref[...])
    n, w, c = MAIN, 2 * MAIN, 2 * MAIN + SIDE
    windows = (
        (0, 144, ((0, 72), (n, 72))),
        (1, 144, ((72, 72), (n + 72, 72))),
        (2, 160, ((144, 40), (n + 144, 40), (w, 40), (c, 40))),
        (3, 160, ((184, 40), (n + 184, 40), (w + 40, 40), (c + 40, 40))),
    )
    low = lax.broadcasted_iota(jnp.int32, (1, LANES), 1) < D // HEADS
    for index, size, parts in windows:
        allowed = col_ref[:size, index : index + 1] == row_ref[index : index + 1, :size]
        bias = jnp.where(allowed, 0.0, -jnp.inf)
        bias = jnp.concatenate([bias, bias], axis=0)

        def take(start):
            return jnp.concatenate([proj[at : at + count, start : start + LANES] for at, count in parts], axis=0)

        for pair in range(HEADS // 2):
            lane = pair * LANES
            query = take(lane).astype(BF).astype(F32) * 0.125
            key = take(D + lane).astype(BF)
            value = take(2 * D + lane).astype(BF)
            both = jnp.concatenate([jnp.where(low, query, 0.0), jnp.where(low, 0.0, query)], axis=0).astype(BF)
            scores = dot(both, key, ((1,), (1,))) + bias
            weights = jnp.exp(scores - jnp.max(scores, axis=-1, keepdims=True))
            scale = 1.0 / jnp.sum(weights, axis=-1, keepdims=True)
            mixed = mm(weights.astype(BF), value) * scale
            result = jnp.where(low, mixed[:size], mixed[size:])
            start = 0
            for at, count in parts:
                context[at : at + count, lane : lane + LANES] = result[start : start + count]
                start += count
    mixed = wide + mm(context[...].astype(BF), wout_ref[...])
    mixed = mixed.astype(BF)
    main_out[...] = mixed[:n]
    north_out[...] = mixed[n:w]
    west_out[...] = mixed[w:c]
    corner_out[...] = mixed[c:]


def expand_matrix(level):
    c = lax.broadcasted_iota(jnp.int32, (LANES, D), 0)
    j = lax.broadcasted_iota(jnp.int32, (LANES, D), 1)
    return (c == level * HEADS + j // (D // HEADS)).astype(F32).astype(BF)


def shift_matrix(offset, width):
    i = lax.broadcasted_iota(jnp.int32, (width, LANES), 0)
    j = lax.broadcasted_iota(jnp.int32, (width, LANES), 1)
    return ((i - offset == j) & (j < OUTS)).astype(F32).astype(BF)


def spot(level):
    first = level * OUTS // LANES * LANES
    return first, level * OUTS - first, min(2 * LANES, PLEV * OUTS - first)


def spread_queries(queries):
    parts = [jnp.broadcast_to(queries[a : a + 1], (HEADS, D)) for a in range(PLEV)]
    parts.append(jnp.zeros((LANES - HEADS * PLEV, D), F32))
    tall = jnp.concatenate(parts, axis=0)
    c = lax.broadcasted_iota(jnp.int32, (LANES, D), 0)
    j = lax.broadcasted_iota(jnp.int32, (LANES, D), 1)
    return jnp.where(c % HEADS == j // (D // HEADS), tall, 0.0)


def pre_kernel(cot_ref, queries_ref, wo_ref, whead_ref, up_ref, dctx_ref, map_ref, base_ref):
    head = whead_ref[...]
    both = mm(wo_ref[...], head).astype(BF)
    map_ref[...] = both
    base_ref[...] = jnp.concatenate(
        [mm(queries_ref[...], head), jnp.zeros((16 - PLEV, LANES), F32)], axis=0
    )
    for level in range(PLEV):
        first, offset, width = spot(level)
        up = mm(cot_ref[:, first : first + width], shift_matrix(offset, width)).astype(BF)
        up_ref[level] = up
        dctx_ref[level] = dot(up, both, ((1,), (1,))).astype(BF)


def decode_kernel(
    main_ref, north_ref, west_ref, corner_ref, perm_ref, wkv_ref, queries_ref, up_ref, dctx_ref, map_ref, base_ref,
    owned_ref, fields_ref, sums_ref,
    pair, weights, dweights, dvalues, context, fields,
):
    pieces = (main_ref, north_ref, west_ref, corner_ref)
    packed = jnp.concatenate([ref[...] for ref in pieces], axis=0)
    wide = dot(perm_ref[...], packed, ((0,), (0,)))
    owned_ref[...] = wide.astype(BF)
    normed = layer_norm(wide)
    pair[...] = mm(normed, wkv_ref[...]).astype(BF).astype(F32)
    queries = spread_queries(queries_ref[...].astype(F32)).astype(BF)
    scores = dot(pair[:, :D].astype(BF), queries, ((1,), (1,))) * 0.125
    slabs = [scores[l * PATCHES : (l + 1) * PATCHES] for l in range(LEV)]
    top = jnp.maximum(jnp.maximum(slabs[0], slabs[1]), jnp.maximum(slabs[2], slabs[3]))
    slabs = [jnp.exp(s - top) for s in slabs]
    scale = 1.0 / (slabs[0] + slabs[1] + slabs[2] + slabs[3])
    for l in range(LEV):
        weights[l * PATCHES : (l + 1) * PATCHES] = slabs[l] * scale
    dweights[...] = jnp.zeros_like(dweights)
    dvalues[...] = jnp.zeros_like(dvalues)
    fields[...] = jnp.zeros_like(fields)
    narrow = weights[...].astype(BF)
    for level in range(PLEV):
        expand = expand_matrix(level)
        spread = mm(narrow, expand)
        upstream = dctx_ref[level].astype(F32)
        total = jnp.zeros((PATCHES, D), F32)
        for l in range(LEV):
            at = slice(l * PATCHES, (l + 1) * PATCHES)
            value = pair[at, D:]
            part = spread[at]
            total += part * value
            dvalues[at] += part * upstream
            dweights[at] += dot((upstream * value).astype(BF), expand, ((1,), (1,)))
        total = total.astype(BF)
        context[level * PATCHES : (level + 1) * PATCHES] = total
        first, offset, width = spot(level)
        decoded = (mm(total, map_ref[...]) + base_ref[level : level + 1]).astype(BF)
        fields[:, first : first + width] += dot(decoded, shift_matrix(offset, width), ((1,), (1,)))
    fields_ref[...] = fields[...].astype(BF)
    parts = [weights[l * PATCHES : (l + 1) * PATCHES] for l in range(LEV)]
    slopes = [dweights[l * PATCHES : (l + 1) * PATCHES] for l in range(LEV)]
    mean = sum(p * d for p, d in zip(parts, slopes))
    dscores = jnp.concatenate([p * (d - mean) * 0.125 for p, d in zip(parts, slopes)], axis=0).astype(BF)
    sums_ref[:D] = dot(normed, dvalues[...].astype(BF), ((0,), (0,))).astype(BF)
    sums_ref[D : D + LANES] = dot(dscores, normed, ((0,), (0,))).astype(BF)
    up = jnp.concatenate([up_ref[a] for a in range(PLEV)], axis=0)
    outer = dot(up, context[...], ((0,), (0,)))
    sums_ref[D + LANES : D + LANES + OUTS] = outer[:OUTS].astype(BF)
    totals = [jnp.sum(up_ref[a].astype(F32), axis=0, keepdims=True) for a in range(PLEV)]
    totals.append(jnp.zeros((LANES - OUTS - PLEV, LANES), F32))
    totals = jnp.concatenate(totals, axis=0)
    totals = jnp.concatenate([totals, jnp.zeros((LANES - OUTS, D - LANES), F32)], axis=1)
    sums_ref[D + LANES + OUTS :] = totals.astype(BF)


def final_kernel(gathered_ref, order_ref, wkv_ref, queries_ref, wo_ref, whead_ref, kv_ref, query_ref, o_ref, head_ref):
    sums = mm(order_ref[...], gathered_ref[...]).astype(BF)
    queries = queries_ref[...]
    head = whead_ref[...]
    keyed = sums[D : D + LANES]
    outer = sums[D + LANES :]
    level_sums = outer[OUTS : OUTS + 16, :LANES]
    spread = spread_queries(queries.astype(F32)).astype(BF)
    values = sums[:D].astype(F32)
    keys = dot(keyed, spread, ((0,), (0,)))
    c = lax.broadcasted_iota(jnp.int32, (LANES, D), 0)
    j = lax.broadcasted_iota(jnp.int32, (LANES, D), 1)
    grouped = jnp.where(c % HEADS == j // (D // HEADS), mm(keyed, wkv_ref[:, :D]), 0.0)
    grouped = jnp.sum(grouped.reshape(LANES // HEADS, HEADS, D), axis=1)
    level = grouped[:PLEV] + dot(level_sums, head, ((1,), (1,)))[:PLEV]
    clean = outer[:OUTS]
    out = dot(clean, head[:, :OUTS], ((0,), (1,)))
    pixels = dot(wo_ref[...], clean, ((0,), (1,)))
    pixels = pixels + dot(queries, level_sums[:PLEV, :OUTS], ((0,), (0,)))
    squares = jnp.sum(values * values) + jnp.sum(keys * keys) + jnp.sum(level * level)
    squares = squares + jnp.sum(out * out) + jnp.sum(pixels * pixels)
    limit = math.sqrt(2 * D * D + PLEV * D + D * D + D * OUTS)
    factor = jnp.minimum(1.0, limit * lax.rsqrt(jnp.full((1, 1), squares + clip_eps, F32)))
    kv_ref[:, :D] = keys * factor
    kv_ref[:, D:] = values * factor
    query_ref[...] = level * factor
    o_ref[...] = out * factor
    head_ref[...] = pixels * factor


def call(kernel, outs, scratch=()):
    return pl.pallas_call(
        kernel,
        out_shape=outs,
        scratch_shapes=list(scratch),
        compiler_params=pltpu.CompilerParams(vmem_limit_bytes=56 * 2**20),
    )


def struct(shape, dtype=BF):
    return jax.ShapeDtypeStruct(shape, dtype)


def move(array, lat_step, lon_step):
    lats, lons = lax.axis_size("lat"), lax.axis_size("lon")
    route = [
        (i * lons + j, (i + lat_step) % lats * lons + (j + lon_step) % lons)
        for i in range(lats)
        for j in range(lons)
    ]
    return lax.ppermute(array, ("lat", "lon"), route)


def sum_over_all(packed):
    rows, width = packed.shape
    lats, lons = lax.axis_size("lat"), lax.axis_size("lon")
    part = rows // lons
    chunks = lax.all_to_all(packed.reshape(lons, part, width), "lon", 0, 0, tiled=True)
    mine = jnp.sum(chunks.astype(F32), axis=0).astype(BF)
    chunks = lax.all_to_all(mine.reshape(lats, part // lats, width), "lat", 0, 0, tiled=True)
    mine = jnp.sum(chunks.astype(F32), axis=0).astype(BF)
    return lax.all_gather(mine, ("lat", "lon")).reshape(rows, width)


def gathered_order():
    lats, lons = lax.axis_size("lat"), lax.axis_size("lon")
    count = ROWS // lats // lons
    row = np.arange(ROWS)
    lon, lat, at = row // (lats * count), row // count % lats, row % count
    return ((lat * lons + lon) * count + at)[:, None] == row[None, :]


def window_labels(own, north, west, corner):
    lat_flag = jnp.where(lax.axis_index("lat") == lax.axis_size("lat") - 1, 4, 0)
    own, west = own.astype(jnp.int32), west.astype(jnp.int32)
    north, corner = north.astype(jnp.int32) + lat_flag, corner.astype(jnp.int32) + lat_flag

    def flat(block, jump, pad):
        block = block.reshape(-1)
        return jnp.concatenate([block, block + jump, jnp.full((pad,), -1, jnp.int32)])

    rows = []
    for jump in (0, 8):
        pieces = [flat(own[:, :WW], jump, 0), flat(north[:, :WW], jump, 0), jnp.full((16,), -1, jnp.int32)]
        rows.append(jnp.concatenate(pieces))
    for jump in (0, 8):
        pieces = (own[:, WW:], north[:, WW:], west, corner)
        rows.append(jnp.concatenate([flat(piece, jump, 4) for piece in pieces]))
    return jnp.stack(rows)


def per_device(latents, mask_ids, w_qkv, w_out, w_kv, level_queries, w_o, w_head, field_cotangent):
    perm = jnp.asarray(pack_matrix(), BF)
    shapes = [struct((MAIN, D)), struct((MAIN, D)), struct((SIDE, D)), struct((SIDE, D))]
    main, north, west, corner = call(pack_kernel, shapes)(latents.reshape(TOKENS, D), perm)
    north, west, corner = move(north, -1, 0), move(west, 0, -1), move(corner, -1, -1)
    labels = window_labels(
        mask_ids[3:, 6:],
        move(mask_ids[:3, 6:], -1, 0),
        move(mask_ids[3:, :6], 0, -1),
        move(mask_ids[:3, :6], -1, -1),
    )
    head = jnp.pad(w_head, ((0, 0), (0, LANES - OUTS)))
    up, dctx, both, base = call(
        pre_kernel,
        [
            struct((PLEV, PATCHES, LANES)),
            struct((PLEV, PATCHES, D)),
            struct((D, LANES)),
            struct((16, LANES), F32),
        ],
    )(field_cotangent.reshape(PATCHES, PLEV * OUTS), level_queries, w_o, head)
    main, north, west, corner = call(
        attention_kernel,
        shapes,
        [pltpu.VMEM((PACKED, 3 * D), F32), pltpu.VMEM((PACKED, D), F32)],
    )(main, north, west, corner, labels, labels.T, w_qkv, w_out)
    north, west, corner = move(north, 1, 0), move(west, 0, 1), move(corner, 1, 1)
    owned, fields, sums = call(
        decode_kernel,
        [struct((TOKENS, D)), struct((PATCHES, PLEV * OUTS)), struct((ROWS, D))],
        [
            pltpu.VMEM((TOKENS, 2 * D), F32),
            pltpu.VMEM((TOKENS, LANES), F32),
            pltpu.VMEM((TOKENS, LANES), F32),
            pltpu.VMEM((TOKENS, D), F32),
            pltpu.VMEM((PLEV * PATCHES, D), BF),
            pltpu.VMEM((PATCHES, PLEV * OUTS), F32),
        ],
    )(main, north, west, corner, perm, w_kv, level_queries, up, dctx, both, base)
    sums = sum_over_all(sums)
    grads = call(
        final_kernel,
        [struct((D, 2 * D), F32), struct((PLEV, D), F32), struct((D, D), F32), struct((D, OUTS), F32)],
    )(sums, jnp.asarray(gathered_order(), BF), w_kv, level_queries, w_o, head)
    shape = latents.shape
    return (owned.reshape(shape), fields.reshape(shape[1], shape[2], PLEV * OUTS), *grads)


def solution(mesh):
    in_specs = (
        P(None, "lat", "lon", None),
        P("lat", "lon"),
        P(),
        P(),
        P(),
        P(),
        P(),
        P(),
        P("lat", "lon", None),
    )
    out_specs = (P(None, "lat", "lon", None), P("lat", "lon", None), P(), P(), P(), P())
    return jax.shard_map(per_device, mesh=mesh, in_specs=in_specs, out_specs=out_specs, check_vma=False)
```

time: 449 us -> 166 us (0.37); the launches traced: 443 us -> 165 us
  waiting for transfers between devices: 185 us -> 8.62 us
  local copies, waits for them, and re-layouts: 81.6 us -> 9.44 us
  matrix products: 37 us -> 0 us
  Pallas kernels: 0 us -> 32.5 us
  other arithmetic: 19.7 us -> 0.2 us
  between operations: 17.5 us -> 0.71 us
  starting transfers between devices: 14.9 us -> 22.1 us
  blocking collectives: 87 us -> 91.5 us
    psum x1 -> x0, waiting for transfers between devices: 172 us -> none  [per_device(): lax.psum((grad_kv, query_columns, grad_out, grad_head), ('lat', 'lon'))]
    psum x1 -> x0, blocking collectives: 87 us -> none  [per_device(): lax.psum((grad_kv, query_columns, grad_out, grad_head), ('lat', 'lon'))]
    all_gather x0 -> x1, blocking collectives: none -> 61.1 us  [sum_over_all(): return lax.all_gather(mine, ('lat', 'lon')).reshape(rows, width)]
    dot_general x18 -> x0, matrix products: 37 us -> none  [the longest x1 6.05 us: decode_block(): d_weights = jnp.einsum('pahe,lphe->phal', d_context, value_vecs)]
    pallas_call x0 -> x5, Pallas kernels: none -> 32.5 us  [the longest x1 12.9 us: per_device(): call(decode_kernel, [struct((TOKENS, D)), struct((PATCHES, PLEV * OUTS)),...]
    all_to_all x0 -> x2, blocking collectives: none -> 30.4 us  [the longest x1 16 us: sum_over_all(): lax.all_to_all(packed.reshape(lons, part, width), 'lon', 0, 0, tiled=True)]
    reshape x11 -> x7, local copies, waits for them, and re-layouts: 28.9 us -> 0.53 us  [the longest x6 0.5 us: flat(): block = block.reshape(-1)]
    convert_element_type x7 -> x0, local copies, waits for them, and re-layouts: 16.2 us -> none  [the longest x2 6.69 us: decode_block(): context = jnp.einsum('phal,lphe->pahe', weights, value_vecs).astype(jnp.b...]
  transfers between devices with their start and end apart: 7 -> 9, of which waited for: 6 -> 3; matrix products, arithmetic and copies ran while one was open for 5% -> 2% of each run, Pallas kernels for 0% -> 5%
where the time goes in v1:
time: 166 us; the launch traced here: 165 us
  blocking collectives  91.5 us (55%)
  Pallas kernels  32.5 us (20%)
  starting transfers between devices  22.1 us (13%)
  local copies, waits for them, and re-layouts  9.44 us (6%)
  waiting for transfers between devices  8.62 us (5%)
    all_gather x1, blocking collectives, sum_over_all(): return lax.all_gather(mine, ('lat', 'lon')).reshape(rows, width)  61.1 us
    ppermute x9, starting transfers between devices, move(): return lax.ppermute(array, ('lat', 'lon'), route)  22.1 us
    all_to_all x1, blocking collectives, sum_over_all(): lax.all_to_all(packed.reshape(lons, part, width), 'lon', 0, 0, tiled=True)  16 us
    all_to_all x1, blocking collectives, sum_over_all(): lax.all_to_all(mine.reshape(lats, part // lats, width), 'lat', 0, 0, tile...  14.3 us
    pallas_call x1, Pallas kernels, per_device(): call(decode_kernel, [struct((TOKENS, D)), struct((PATCHES, PLEV * OUTS)),...  12.9 us
    ppermute x9, waiting for transfers between devices, move(): return lax.ppermute(array, ('lat', 'lon'), route)  8.62 us
    pallas_call x1, Pallas kernels, per_device(): call(attention_kernel, shapes, [pltpu.VMEM((PACKED, 3 * D), F32), pltpu.V...  6.07 us
    pallas_call x1, Pallas kernels, per_device(): call(final_kernel, [struct((D, 2 * D), F32), struct((PLEV, D), F32), stru...  5.52 us
  transfers between devices with their start and end apart: 9, of which 3 were waited for; matrix products, arithmetic and copies ran while one was open for 2% of the time, Pallas kernels for 5%

profile of v1, /device:TPU:1, one launch (start us, length us, event | category | flops | bytes accessed | tf_op | source)
XLA Modules:
  0.0 165.1 jit_solution(16328959868085199706)
XLA Ops:
  0.6 0.9 fusion
  1.5 9.4 %collective-permute-start.5 = (s32[3,6]{1,0:T(4,128)S(1)}, s32[3,6]{1,0:T(4,128)S(1)}, u32[]{:S(2)}, u32[]{:S(2)}) collective-permute-start(s32[3,6]{1,0:T(4,128)S(1)} %get-tuple-element.62), channel_id=1, source_target_pairs={{0,255},{1,240},{2,241},{3,242},{4,243},{5,244},{6,245},{7,246},{8... | collective-permute-start | bytes 224 | tf_op jit(solution)/shard_map/ppermute | solution.py:271
  10.9 2.0 %collective-permute-start.4 = (s32[3,6]{1,0:T(4,128)S(1)}, s32[3,6]{1,0:T(4,128)S(1)}, u32[]{:S(2)}, u32[]{:S(2)}) collective-permute-start(s32[3,6]{1,0:T(4,128)S(1)} %get-tuple-element.64), channel_id=1, source_target_pairs={{0,15},{1,0},{2,1},{3,2},{4,3},{5,4},{6,5},{7,6},{8,7},{9,8},{10,9... | collective-permute-start | bytes 224 | tf_op jit(solution)/shard_map/ppermute | solution.py:271
  12.9 0.8 slice.29
  13.7 0.5 collective-permute-start.3
  14.2 2.8 %shard_map.154 = (bf16[224,512]{1,0:T(8,128)(2,1)}, bf16[224,512]{1,0:T(8,128)(2,1)}, bf16[80,512]{1,0:T(8,128)(2,1)}, bf16[80,512]{1,0:T(8,128)(2,1)}) custom-call(bf16[576,512]{1,0:T(8,128)(2,1)} %bitcast.13, bf16[608,576]{1,0:T(8,128)(2,1)} %constant.26.clone.perm_ref), custom_call_target="tpu_custom_call" | custom-call | tf_op jit(solution)/shard_map/pallas_call | solution.py:315
  17.0 2.6 %collective-permute-start.1 = (bf16[80,512]{1,0:T(8,128)(2,1)}, bf16[80,512]{1,0:T(8,128)(2,1)S(1)}, u32[]{:S(2)}, u32[]{:S(2)}) collective-permute-start(bf16[80,512]{1,0:T(8,128)(2,1)} %get-tuple-element.27), channel_id=1, source_target_pairs={{0,15},{1,0},{2,1},{3,2},{4,3},{5,4},{6,5},{7,6},{8,7},{9,8},{10,9... | collective-permute-start | bytes 245768 | tf_op jit(solution)/shard_map/ppermute | solution.py:271
  19.7 1.9 %collective-permute-start.2 = (bf16[80,512]{1,0:T(8,128)(2,1)}, bf16[80,512]{1,0:T(8,128)(2,1)S(1)}, u32[]{:S(2)}, u32[]{:S(2)}) collective-permute-start(bf16[80,512]{1,0:T(8,128)(2,1)} %get-tuple-element.28), channel_id=1, source_target_pairs={{0,255},{1,240},{2,241},{3,242},{4,243},{5,244},{6,245},{7,246},{8... | collective-permute-start | bytes 245768 | tf_op jit(solution)/shard_map/ppermute | solution.py:271
  21.6 0.8 slice.28
  22.5 1.4 collective-permute-start
  24.7 0.7 copy.27
  25.5 0.7 collective-permute-done.2.corner_ref
  26.1 5.3 %collective-permute-done.north_ref = bf16[224,512]{1,0:T(8,128)(2,1)S(1)} collective-permute-done((bf16[224,512]{1,0:T(8,128)(2,1)}, bf16[224,512]{1,0:T(8,128)(2,1)S(1)}, u32[]{:S(2)}, u32[]{:S(2)}) %collective-permute-start) | collective-permute-done | bytes 229408 | tf_op jit(solution)/shard_map/ppermute | solution.py:271
  31.4 0.7 copy-done
  32.1 6.1 %shard_map.155 = (bf16[224,512]{1,0:T(8,128)(2,1)}, bf16[224,512]{1,0:T(8,128)(2,1)}, bf16[80,512]{1,0:T(8,128)(2,1)}, bf16[80,512]{1,0:T(8,128)(2,1)}) custom-call(bf16[224,512]{1,0:T(8,128)(2,1)} %get-tuple-element.25.main_ref, bf16[224,512]{1,0:T(8,128)(2,1)} %copy-done, bf16[80,512]{1,0:T(8,128)(2,1)} %copy-done.2, bf16[80,512]{1,0:T(8,128)(2,1)} %copy-done.3, ...), custom_call_target="tpu_custom_call" | custom-call | tf_op jit(solution)/shard_map/pallas_call | solution.py:333
  38.2 1.7 %collective-permute-start.6 = (bf16[224,512]{1,0:T(8,128)(2,1)}, bf16[224,512]{1,0:T(8,128)(2,1)S(1)}, u32[]{:S(2)}, u32[]{:S(2)}) collective-permute-start(bf16[224,512]{1,0:T(8,128)(2,1)} %get-tuple-element.30), channel_id=1, source_target_pairs={{0,16},{1,17},{2,18},{3,19},{4,20},{5,21},{6,22},{7,23},{8,24},{9,... | collective-permute-start | bytes 688136 | tf_op jit(solution)/shard_map/ppermute | solution.py:271
  39.8 1.3 collective-permute-start.7
  41.1 1.3 collective-permute-start.8
  42.4 0.1 copy.28
  42.5 0.7 pad.4.whead_ref
  43.2 5.2 %shard_map.156 = (bf16[13,144,128]{2,1,0:T(8,128)(2,1)}, bf16[13,144,512]{2,1,0:T(8,128)(2,1)}, bf16[512,128]{1,0:T(8,128)(2,1)}, f32[16,128]{1,0:T(8,128)}) custom-call(bf16[144,1040]{1,0:T(8,128)(2,1)} %bitcast.14, bf16[13,512]{1,0:T(8,128)(2,1)} %queries_ref.5, bf16[512,512]{1,0:T(8,128)(2,1)} %wo_ref.3, bf16[512,128]{1,0:T(8,128)(2,1)} %pad.4.whead_ref), custom_call_target="tpu_custom_call" | custom-call | tf_op jit(solution)/shard_map/pallas_call | solution.py:324
  48.4 2.7 %collective-permute-done.8.corner_ref = bf16[80,512]{1,0:T(8,128)(2,1)S(1)} collective-permute-done((bf16[80,512]{1,0:T(8,128)(2,1)}, bf16[80,512]{1,0:T(8,128)(2,1)S(1)}, u32[]{:S(2)}, u32[]{:S(2)}) %collective-permute-start.8) | collective-permute-done | bytes 81952 | tf_op jit(solution)/shard_map/ppermute | solution.py:271
  51.1 0.6 copy-done.6
  51.7 0.1 copy-done.1
  51.8 12.9 %shard_map.157 = (bf16[576,512]{1,0:T(8,128)(2,1)}, bf16[144,1040]{1,0:T(8,128)(2,1)}, bf16[768,512]{1,0:T(8,128)(2,1)}) custom-call(bf16[224,512]{1,0:T(8,128)(2,1)} %get-tuple-element.29.main_ref, bf16[224,512]{1,0:T(8,128)(2,1)} %copy-done.1, bf16[80,512]{1,0:T(8,128)(2,1)} %copy-done.5, bf16[80,512]{1,0:T(8,128)(2,1)} %copy-done.6, ...), custom_call_target="tpu_custom_call" | custom-call | tf_op jit(solution)/shard_map/pallas_call | solution.py:339
  64.7 16.0 %all_to_all.10 = bf16[16,48,512]{2,1,0:T(8,128)(2,1)S(1)} all-to-all(bf16[16,48,512]{2,1,0:T(8,128)(2,1)} %bitcast.12), channel_id=1, replica_groups=mesh['lat'=16,'lon'=16] {'lon'}, dimensions={0} | all-to-all | bytes 1572864 | tf_op jit(solution)/shard_map/all_to_all | solution.py:278
  80.7 0.1 reduce_sum.24
  80.9 14.3 %all_to_all.11 = bf16[16,3,512]{2,1,0:T(4,128)(2,1)S(1)} all-to-all(bf16[16,3,512]{2,1,0:T(4,128)(2,1)S(1)} %reshape.68), channel_id=1, replica_groups=mesh['lat'=16,'lon'=16] {'lat'}, dimensions={0} | all-to-all | bytes 98304 | tf_op jit(solution)/shard_map/all_to_all | solution.py:280
  95.3 61.1 %all-gather.1 = bf16[256,3,512]{2,1,0:T(4,128)(2,1)S(1)} all-gather(bf16[1,3,512]{2,1,0:T(4,128)(2,1)S(1)} %bitcast.17), channel_id=2, replica_groups=mesh['lat'=16,'lon'=16] {'lat','lon'}, dimensions={0}, use_global_device_ids=true | all-gather | bytes 789504 | tf_op jit(solution)/shard_map/all_gather | solution.py:282
  156.4 1.4 reshape.73.gathered_ref
  157.8 5.5 %shard_map.158 = (f32[512,1024]{1,0:T(8,128)}, f32[13,512]{1,0:T(8,128)}, f32[512,512]{1,0:T(8,128)}, f32[512,80]{1,0:T(8,128)}) custom-call(bf16[768,512]{1,0:T(8,128)(2,1)} %reshape.73.gathered_ref, bf16[768,768]{1,0:T(8,128)(2,1)} %constant.27.clone.order_ref, bf16[512,1024]{1,0:T(8,128)(2,1)} %wkv_ref.3, bf16[13,512]{1,0:T(8,128)(2,1)} %queries_ref.5, ...), custom_call_target="tpu_custom_call" | custom-call | tf_op jit(solution)/shard_map/pallas_call | solution.py:352
  163.3 1.7 %copy.29 = f32[512,80]{0,1:T(8,128)} copy(f32[512,80]{1,0:T(8,128)} %get-tuple-element.61) | data formatting | bytes 327680
  (41 shorter events, 1.1 us)
Async XLA Ops:
  1.5 21.0 %collective-permute-start.5 = (s32[3,6]{1,0:T(4,128)S(1)}, s32[3,6]{1,0:T(4,128)S(1)}, u32[]{:S(2)}, u32[]{:S(2)}) collective-permute-start(s32[3,6]{1,0:T(4,128)S(1)} %get-tuple-element.62), channel_id=1, source_target_pairs={{0,255},{1,240},{2,241},{3,242},{4,243},{5,244},{6,245},{7,246},{8... | collective-permute-start | bytes 224 | tf_op jit(solution)/shard_map/ppermute | solution.py:271
  10.9 13.1 %collective-permute-start.4 = (s32[3,6]{1,0:T(4,128)S(1)}, s32[3,6]{1,0:T(4,128)S(1)}, u32[]{:S(2)}, u32[]{:S(2)}) collective-permute-start(s32[3,6]{1,0:T(4,128)S(1)} %get-tuple-element.64), channel_id=1, source_target_pairs={{0,15},{1,0},{2,1},{3,2},{4,3},{5,4},{6,5},{7,6},{8,7},{9,8},{10,9... | collective-permute-start | bytes 224 | tf_op jit(solution)/shard_map/ppermute | solution.py:271
  13.7 10.4 %collective-permute-start.3 = (s32[3,18]{1,0:T(4,128)S(1)}, s32[3,18]{1,0:T(4,128)S(1)}, u32[]{:S(2)}, u32[]{:S(2)}) collective-permute-start(s32[3,18]{1,0:T(4,128)S(1)} %slice.29), channel_id=1, source_target_pairs={{0,240},{1,241},{2,242},{3,243},{4,244},{5,245},{6,246},{7,247},{8... | collective-permute-start | bytes 656 | tf_op jit(solution)/shard_map/ppermute | solution.py:271
  14.2 28.2 %copy-start.4 = (bf16[512,80]{0,1:T(8,128)(2,1)S(1)}, bf16[512,80]{0,1:T(8,128)(2,1)}, u32[]{:S(2)}) copy-start(bf16[512,80]{0,1:T(8,128)(2,1)} %param.18) | copy-start | bytes 245764
  17.0 8.4 %collective-permute-start.1 = (bf16[80,512]{1,0:T(8,128)(2,1)}, bf16[80,512]{1,0:T(8,128)(2,1)S(1)}, u32[]{:S(2)}, u32[]{:S(2)}) collective-permute-start(bf16[80,512]{1,0:T(8,128)(2,1)} %get-tuple-element.27), channel_id=1, source_target_pairs={{0,15},{1,0},{2,1},{3,2},{4,3},{5,4},{6,5},{7,6},{8,7},{9,8},{10,9... | collective-permute-start | bytes 245768 | tf_op jit(solution)/shard_map/ppermute | solution.py:271
  19.7 6.5 %collective-permute-start.2 = (bf16[80,512]{1,0:T(8,128)(2,1)}, bf16[80,512]{1,0:T(8,128)(2,1)S(1)}, u32[]{:S(2)}, u32[]{:S(2)}) collective-permute-start(bf16[80,512]{1,0:T(8,128)(2,1)} %get-tuple-element.28), channel_id=1, source_target_pairs={{0,255},{1,240},{2,241},{3,242},{4,243},{5,244},{6,245},{7,246},{8... | collective-permute-start | bytes 245768 | tf_op jit(solution)/shard_map/ppermute | solution.py:271
  22.5 8.9 %collective-permute-start = (bf16[224,512]{1,0:T(8,128)(2,1)}, bf16[224,512]{1,0:T(8,128)(2,1)S(1)}, u32[]{:S(2)}, u32[]{:S(2)}) collective-permute-start(bf16[224,512]{1,0:T(8,128)(2,1)} %get-tuple-element.26), channel_id=1, source_target_pairs={{0,240},{1,241},{2,242},{3,243},{4,244},{5,245},{6,246},{7,247},{8... | collective-permute-start | bytes 688136 | tf_op jit(solution)/shard_map/ppermute | solution.py:271
  24.7 6.7 %copy-start.7 = (s32[4,160]{1,0:T(4,128)}, s32[4,160]{1,0:T(4,128)S(1)}, u32[]{:S(2)}) copy-start(s32[4,160]{1,0:T(4,128)S(1)} %pad_add_fusion.row_ref) | copy-start | bytes 7684
  25.5 5.9 %copy-start.2 = (bf16[80,512]{1,0:T(8,128)(2,1)}, bf16[80,512]{1,0:T(8,128)(2,1)S(1)}, u32[]{:S(2)}) copy-start(bf16[80,512]{1,0:T(8,128)(2,1)S(1)} %collective-permute-done.1.west_ref) | copy-start | bytes 245764
  26.1 5.3 %copy-start.3 = (bf16[80,512]{1,0:T(8,128)(2,1)}, bf16[80,512]{1,0:T(8,128)(2,1)S(1)}, u32[]{:S(2)}) copy-start(bf16[80,512]{1,0:T(8,128)(2,1)S(1)} %collective-permute-done.2.corner_ref) | copy-start | bytes 245764
  31.4 0.7 copy-start
  38.2 12.9 %collective-permute-start.6 = (bf16[224,512]{1,0:T(8,128)(2,1)}, bf16[224,512]{1,0:T(8,128)(2,1)S(1)}, u32[]{:S(2)}, u32[]{:S(2)}) collective-permute-start(bf16[224,512]{1,0:T(8,128)(2,1)} %get-tuple-element.30), channel_id=1, source_target_pairs={{0,16},{1,17},{2,18},{3,19},{4,20},{5,21},{6,22},{7,23},{8,24},{9,... | collective-permute-start | bytes 688136 | tf_op jit(solution)/shard_map/ppermute | solution.py:271
  39.8 8.6 %collective-permute-start.7 = (bf16[80,512]{1,0:T(8,128)(2,1)}, bf16[80,512]{1,0:T(8,128)(2,1)S(1)}, u32[]{:S(2)}, u32[]{:S(2)}) collective-permute-start(bf16[80,512]{1,0:T(8,128)(2,1)} %get-tuple-element.31), channel_id=1, source_target_pairs={{0,1},{1,2},{2,3},{3,4},{4,5},{5,6},{6,7},{7,8},{8,9},{9,10},{10,1... | collective-permute-start | bytes 245768 | tf_op jit(solution)/shard_map/ppermute | solution.py:271
  41.1 10.0 %collective-permute-start.8 = (bf16[80,512]{1,0:T(8,128)(2,1)}, bf16[80,512]{1,0:T(8,128)(2,1)S(1)}, u32[]{:S(2)}, u32[]{:S(2)}) collective-permute-start(bf16[80,512]{1,0:T(8,128)(2,1)} %get-tuple-element.32), channel_id=1, source_target_pairs={{0,17},{1,18},{2,19},{3,20},{4,21},{5,22},{6,23},{7,24},{8,25},{9,... | collective-permute-start | bytes 245768 | tf_op jit(solution)/shard_map/ppermute | solution.py:271
  48.4 2.7 %copy-start.5 = (bf16[80,512]{1,0:T(8,128)(2,1)}, bf16[80,512]{1,0:T(8,128)(2,1)S(1)}, u32[]{:S(2)}) copy-start(bf16[80,512]{1,0:T(8,128)(2,1)S(1)} %collective-permute-done.7.west_ref) | copy-start | bytes 245764
  51.1 0.6 copy-start.6
  51.1 0.7 copy-start.1

commit v2 on v1

--- a/solution.py
+++ b/solution.py
@@ -24,6 +24,14 @@
 ROWS = 768
 LANES = 128
 
+SPAN = 256
+PIECES = (
+    {0: (0, 72, 0), 1: (72, 72, 0), 2: (144, 40, 0), 3: (184, 40, 0)},
+    {0: (224, 72, 72), 1: (296, 72, 72), 2: (368, 40, 40), 3: (408, 40, 40)},
+    {2: (448, 40, 80), 3: (488, 40, 80)},
+    {2: (528, 40, 120), 3: (568, 40, 120)},
+)
+
 norm_eps = 1e-05
 clip_eps = 1e-06
 BF = jnp.bfloat16
@@ -53,6 +61,28 @@
     return (order[:, None] == np.arange(TOKENS)[None, :]).astype(np.float32)
 
 
+def label_tables():
+    order = window_order()
+    row, col, level = order // (2 * WW) % WH, order % (2 * WW), order // PATCHES
+    columns = np.zeros((2 * WW, 12 * SPAN), np.float32)
+    rows = np.zeros((8, 12 * SPAN), np.float32)
+    extra = np.zeros((8, SPAN), np.float32)
+    segment = 0
+    for starts, far in zip(PIECES, (False, True, False, True)):
+        for window, (at, count, place) in starts.items():
+            for i in range(count):
+                lane, token = place + i, at + i
+                if order[token] < 0:
+                    extra[window, lane] = -1
+                    continue
+                columns[col[token], segment * SPAN + lane] = 1
+                rows[row[token], segment * SPAN + lane] = 1
+                extra[window, lane] = 8 * (level[token] == 0)
+                extra[4 + window, lane] = 4 * far
+            segment += 1
+    return columns, rows, extra
+
+
 def dot(a, b, contract):
     return lax.dot_general(a, b, (contract, ((), ())), preferred_element_type=F32)
 
@@ -67,21 +97,41 @@
     return (center * lax.rsqrt(spread + norm_eps)).astype(BF)
 
 
-def pack_kernel(x_ref, perm_ref, main_ref, north_ref, west_ref, corner_ref):
+def pack_kernel(x_ref, ids_ref, perm_ref, columns_ref, rows_ref, main_ref, north_ref, west_ref, corner_ref):
+    ids = ids_ref[...].astype(F32).astype(BF)
+    lines = jnp.sum(mm(ids, columns_ref[...]) * rows_ref[:WH], axis=0, keepdims=True)
     x = x_ref[...]
-    north_ref[...] = mm(perm_ref[MAIN : 2 * MAIN], x).astype(BF)
-    west_ref[...] = mm(perm_ref[2 * MAIN : 2 * MAIN + SIDE], x).astype(BF)
-    corner_ref[...] = mm(perm_ref[2 * MAIN + SIDE :], x).astype(BF)
-    main_ref[...] = mm(perm_ref[:MAIN], x).astype(BF)
+    segment = 0
+    for ref, windows in zip((main_ref, north_ref, west_ref, corner_ref), PIECES):
+        height = ref.shape[0]
+        first = min(at for at, _, _ in windows.values())
+        packed = mm(perm_ref[first : first + height], x)
+        bottom = [jnp.zeros((12, SPAN), F32)]
+        for window in range(4):
+            if window in windows:
+                bottom.append(lines[:, segment * SPAN : (segment + 1) * SPAN])
+                segment += 1
+            else:
+                bottom.append(jnp.zeros((1, SPAN), F32))
+        bottom = jnp.concatenate(bottom, axis=0)
+        bottom = jnp.concatenate([bottom, jnp.zeros((16, D - SPAN), F32)], axis=1)
+        ref[: height - 16] = packed[: height - 16].astype(BF)
+        ref[height - 16 :] = (packed[height - 16 :] + bottom).astype(BF)
 
 
 def attention_kernel(
-    main_ref, north_ref, west_ref, corner_ref, row_ref, col_ref, wqkv_ref, wout_ref,
+    flag_ref, main_ref, north_ref, west_ref, corner_ref, extra_ref, wqkv_ref, wout_ref,
     main_out, north_out, west_out, corner_out, proj, context,
 ):
     pieces = (main_ref, north_ref, west_ref, corner_ref)
     wide = jnp.concatenate([ref[...].astype(F32) for ref in pieces], axis=0)
     proj[...] = mm(layer_norm(wide), wqkv_ref[...])
+    lines = sum(ref[ref.shape[0] - 16 :, :SPAN].astype(F32) for ref in pieces)[12:]
+    lines = lines + extra_ref[:4] + jnp.where(flag_ref[0, 0] > 0, extra_ref[4:], 0.0)
+    lines = jnp.concatenate([lines, lines], axis=0)
+    i = lax.broadcasted_iota(jnp.int32, (SPAN, SPAN), 0)
+    j = lax.broadcasted_iota(jnp.int32, (SPAN, SPAN), 1)
+    standing = dot((i == j).astype(F32).astype(BF), lines.astype(BF), ((1,), (1,)))
     n, w, c = MAIN, 2 * MAIN, 2 * MAIN + SIDE
     windows = (
         (0, 144, ((0, 72), (n, 72))),
@@ -91,7 +141,7 @@
     )
     low = lax.broadcasted_iota(jnp.int32, (1, LANES), 1) < D // HEADS
     for index, size, parts in windows:
-        allowed = col_ref[:size, index : index + 1] == row_ref[index : index + 1, :size]
+        allowed = standing[:size, index : index + 1] == lines[index : index + 1, :size]
         bias = jnp.where(allowed, 0.0, -jnp.inf)
         bias = jnp.concatenate([bias, bias], axis=0)
 
@@ -149,10 +199,10 @@
 
 def pre_kernel(cot_ref, queries_ref, wo_ref, whead_ref, up_ref, dctx_ref, map_ref, base_ref):
     head = whead_ref[...]
-    both = mm(wo_ref[...], head).astype(BF)
+    both = dot(wo_ref[...], head, ((1,), (1,))).astype(BF)
     map_ref[...] = both
     base_ref[...] = jnp.concatenate(
-        [mm(queries_ref[...], head), jnp.zeros((16 - PLEV, LANES), F32)], axis=0
+        [dot(queries_ref[...], head, ((1,), (1,))), jnp.zeros((16 - PLEV, LANES), F32)], axis=0
     )
     for level in range(PLEV):
         first, offset, width = spot(level)
@@ -218,8 +268,8 @@
     sums_ref[D + LANES + OUTS :] = totals.astype(BF)
 
 
-def final_kernel(gathered_ref, order_ref, wkv_ref, queries_ref, wo_ref, whead_ref, kv_ref, query_ref, o_ref, head_ref):
-    sums = mm(order_ref[...], gathered_ref[...]).astype(BF)
+def final_kernel(sums_ref, wkv_ref, queries_ref, wo_ref, whead_ref, kv_ref, query_ref, o_ref, head_ref):
+    sums = sums_ref[...]
     queries = queries_ref[...]
     head = whead_ref[...]
     keyed = sums[D : D + LANES]
@@ -232,11 +282,11 @@
     j = lax.broadcasted_iota(jnp.int32, (LANES, D), 1)
     grouped = jnp.where(c % HEADS == j // (D // HEADS), mm(keyed, wkv_ref[:, :D]), 0.0)
     grouped = jnp.sum(grouped.reshape(LANES // HEADS, HEADS, D), axis=1)
-    level = grouped[:PLEV] + dot(level_sums, head, ((1,), (1,)))[:PLEV]
+    level = grouped[:PLEV] + mm(level_sums, head)[:PLEV]
     clean = outer[:OUTS]
-    out = dot(clean, head[:, :OUTS], ((0,), (1,)))
-    pixels = dot(wo_ref[...], clean, ((0,), (1,)))
-    pixels = pixels + dot(queries, level_sums[:PLEV, :OUTS], ((0,), (0,)))
+    out = dot(clean, head[:OUTS], ((0,), (0,)))
+    pixels = mm(clean, wo_ref[...])
+    pixels = pixels + dot(level_sums[:PLEV, :OUTS], queries, ((0,), (0,)))
     squares = jnp.sum(values * values) + jnp.sum(keys * keys) + jnp.sum(level * level)
     squares = squares + jnp.sum(out * out) + jnp.sum(pixels * pixels)
     limit = math.sqrt(2 * D * D + PLEV * D + D * D + D * OUTS)
@@ -248,9 +298,14 @@
     head_ref[...] = pixels * factor
 
 
-def call(kernel, outs, scratch=()):
+def call(kernel, outs, scratch=(), smem=False):
+    more = {}
+    if smem:
+        whole = pl.BlockSpec(memory_space=pltpu.VMEM)
+        more["in_specs"] = [pl.BlockSpec(memory_space=pltpu.SMEM)] + [whole] * 7
     return pl.pallas_call(
         kernel,
+        **more,
         out_shape=outs,
         scratch_shapes=list(scratch),
         compiler_params=pltpu.CompilerParams(vmem_limit_bytes=56 * 2**20),
@@ -271,56 +326,46 @@
     return lax.ppermute(array, ("lat", "lon"), route)
 
 
+def lat_groups(count, stride):
+    lats = lax.axis_size("lat")
+    return [
+        [first + stride * i for i in range(count)]
+        for first in range(lats)
+        if first // stride % count == 0
+    ]
+
+
+def sum_over_lat(mine):
+    lats = lax.axis_size("lat")
+    low = min(4, lats)
+    high = lats // low
+    copies = jnp.broadcast_to(mine[None], (low,) + mine.shape)
+    copies = lax.all_to_all(copies, "lat", 0, 0, axis_index_groups=lat_groups(low, 1), tiled=True)
+    mine = jnp.sum(copies.astype(F32), axis=0).astype(BF)
+    others = [move(mine, low * step, 0) for step in range(1, high)]
+    return sum((other.astype(F32) for other in others), mine.astype(F32)).astype(BF)
+
+
 def sum_over_all(packed):
     rows, width = packed.shape
-    lats, lons = lax.axis_size("lat"), lax.axis_size("lon")
+    lons = lax.axis_size("lon")
     part = rows // lons
     chunks = lax.all_to_all(packed.reshape(lons, part, width), "lon", 0, 0, tiled=True)
-    mine = jnp.sum(chunks.astype(F32), axis=0).astype(BF)
-    chunks = lax.all_to_all(mine.reshape(lats, part // lats, width), "lat", 0, 0, tiled=True)
-    mine = jnp.sum(chunks.astype(F32), axis=0).astype(BF)
-    return lax.all_gather(mine, ("lat", "lon")).reshape(rows, width)
-
-
-def gathered_order():
-    lats, lons = lax.axis_size("lat"), lax.axis_size("lon")
-    count = ROWS // lats // lons
-    row = np.arange(ROWS)
-    lon, lat, at = row // (lats * count), row // count % lats, row % count
-    return ((lat * lons + lon) * count + at)[:, None] == row[None, :]
-
-
-def window_labels(own, north, west, corner):
-    lat_flag = jnp.where(lax.axis_index("lat") == lax.axis_size("lat") - 1, 4, 0)
-    own, west = own.astype(jnp.int32), west.astype(jnp.int32)
-    north, corner = north.astype(jnp.int32) + lat_flag, corner.astype(jnp.int32) + lat_flag
-
-    def flat(block, jump, pad):
-        block = block.reshape(-1)
-        return jnp.concatenate([block, block + jump, jnp.full((pad,), -1, jnp.int32)])
-
-    rows = []
-    for jump in (0, 8):
-        pieces = [flat(own[:, :WW], jump, 0), flat(north[:, :WW], jump, 0), jnp.full((16,), -1, jnp.int32)]
-        rows.append(jnp.concatenate(pieces))
-    for jump in (0, 8):
-        pieces = (own[:, WW:], north[:, WW:], west, corner)
-        rows.append(jnp.concatenate([flat(piece, jump, 4) for piece in pieces]))
-    return jnp.stack(rows)
+    mine = sum_over_lat(jnp.sum(chunks.astype(F32), axis=0).astype(BF))
+    copies = jnp.broadcast_to(mine[None], (lons, part, width))
+    return lax.all_to_all(copies, "lon", 0, 0, tiled=True).reshape(rows, width)
 
 
 def per_device(latents, mask_ids, w_qkv, w_out, w_kv, level_queries, w_o, w_head, field_cotangent):
     perm = jnp.asarray(pack_matrix(), BF)
+    columns, rows, extra = label_tables()
+    flag = (lax.axis_index("lat") == lax.axis_size("lat") - 1).astype(jnp.int32).reshape(1, 1)
     shapes = [struct((MAIN, D)), struct((MAIN, D)), struct((SIDE, D)), struct((SIDE, D))]
-    main, north, west, corner = call(pack_kernel, shapes)(latents.reshape(TOKENS, D), perm)
+    main, north, west, corner = call(pack_kernel, shapes)(
+        latents.reshape(TOKENS, D), mask_ids, perm, jnp.asarray(columns, BF), jnp.asarray(rows)
+    )
     north, west, corner = move(north, -1, 0), move(west, 0, -1), move(corner, -1, -1)
-    labels = window_labels(
-        mask_ids[3:, 6:],
-        move(mask_ids[:3, 6:], -1, 0),
-        move(mask_ids[3:, :6], 0, -1),
-        move(mask_ids[:3, :6], -1, -1),
-    )
-    head = jnp.pad(w_head, ((0, 0), (0, LANES - OUTS)))
+    head = jnp.pad(w_head.T, ((0, LANES - OUTS), (0, 0)))
     up, dctx, both, base = call(
         pre_kernel,
         [
@@ -334,7 +379,8 @@
         attention_kernel,
         shapes,
         [pltpu.VMEM((PACKED, 3 * D), F32), pltpu.VMEM((PACKED, D), F32)],
-    )(main, north, west, corner, labels, labels.T, w_qkv, w_out)
+        smem=True,
+    )(flag, main, north, west, corner, jnp.asarray(extra), w_qkv, w_out)
     north, west, corner = move(north, 1, 0), move(west, 0, 1), move(corner, 1, 1)
     owned, fields, sums = call(
         decode_kernel,
@@ -349,12 +395,12 @@
         ],
     )(main, north, west, corner, perm, w_kv, level_queries, up, dctx, both, base)
     sums = sum_over_all(sums)
-    grads = call(
+    kv, query, out, pixels = call(
         final_kernel,
-        [struct((D, 2 * D), F32), struct((PLEV, D), F32), struct((D, D), F32), struct((D, OUTS), F32)],
-    )(sums, jnp.asarray(gathered_order(), BF), w_kv, level_queries, w_o, head)
+        [struct((D, 2 * D), F32), struct((PLEV, D), F32), struct((D, D), F32), struct((OUTS, D), F32)],
+    )(sums, w_kv, level_queries, w_o, head)
     shape = latents.shape
-    return (owned.reshape(shape), fields.reshape(shape[1], shape[2], PLEV * OUTS), *grads)
+    return (owned.reshape(shape), fields.reshape(shape[1], shape[2], PLEV * OUTS), kv, query, out, pixels.T)
 
 
 def solution(mesh):

time: 166 us -> 116 us (0.70)
  blocking collectives: 91.5 us -> 45.6 us
  local copies, waits for them, and re-layouts: 9.44 us -> 2.17 us
  waiting for transfers between devices: 8.62 us -> 14.4 us
    all_gather x1 -> x0, blocking collectives: 61.1 us -> none  [sum_over_all(): return lax.all_gather(mine, ('lat', 'lon')).reshape(rows, width)]
    all_to_all x1 -> x2, blocking collectives: 14.3 us -> 28 us  [the longest x1 19.7 us: sum_over_all(): return lax.all_to_all(copies, 'lon', 0, 0, tiled=True).reshape(rows, width)]
    ppermute x9, waiting for transfers between devices: 8.62 us -> 14.4 us  [move(): return lax.ppermute(array, ('lat', 'lon'), route)]
    unnamed x19 -> x14, local copies, waits for them, and re-layouts: 4.68 us -> 1.42 us
    slice x4 -> x0, local copies, waits for them, and re-layouts: 2.46 us -> none  [the longest x1 0.87 us: per_device(): mask_ids[:3, :6]]
  transfers between devices with their start and end apart: 9 -> 9, of which waited for: 3 -> 4; matrix products, arithmetic and copies ran while one was open for 2% -> 1% of each run, Pallas kernels for 5% -> 4%
where the time goes in v2:
time: 116 us; the launch traced here: 115 us
  blocking collectives  45.6 us (39%)
  Pallas kernels  31.3 us (27%)
  starting transfers between devices  21.1 us (18%)
  waiting for transfers between devices  14.4 us (12%)
  local copies, waits for them, and re-layouts  2.17 us (2%)
    ppermute x9, starting transfers between devices, move(): return lax.ppermute(array, ('lat', 'lon'), route)  21.1 us
    all_to_all x1, blocking collectives, sum_over_all(): return lax.all_to_all(copies, 'lon', 0, 0, tiled=True).reshape(rows, width)  19.7 us
    all_to_all x1, blocking collectives, sum_over_all(): lax.all_to_all(packed.reshape(lons, part, width), 'lon', 0, 0, tiled=True)  17.6 us
    ppermute x9, waiting for transfers between devices, move(): return lax.ppermute(array, ('lat', 'lon'), route)  14.4 us
    pallas_call x1, Pallas kernels, per_device(): call(decode_kernel, [struct((TOKENS, D)), struct((PATCHES, PLEV * OUTS)),...  12.9 us
    all_to_all x1, blocking collectives, sum_over_lat(): lax.all_to_all(copies, 'lat', 0, 0, axis_index_groups=lat_groups(low, 1),...  8.37 us
    pallas_call x1, Pallas kernels, per_device(): call(attention_kernel, shapes, [pltpu.VMEM((PACKED, 3 * D), F32), pltpu.V...  6.09 us
    pallas_call x1, Pallas kernels, per_device(): call(pre_kernel, [struct((PLEV, PATCHES, LANES)), struct((PLEV, PATCHES,...  5.07 us
  transfers between devices with their start and end apart: 9, of which 4 were waited for; matrix products, arithmetic and copies ran while one was open for 1% of the time, Pallas kernels for 4%

profile of v2, /device:TPU:1, one launch (start us, length us, event | category | flops | bytes accessed | tf_op | source)
XLA Modules:
  0.0 115.4 jit_solution(15166011172167657167)
XLA Ops:
  0.6 2.9 %shard_map.172 = (bf16[224,512]{1,0:T(8,128)(2,1)}, bf16[224,512]{1,0:T(8,128)(2,1)}, bf16[80,512]{1,0:T(8,128)(2,1)}, bf16[80,512]{1,0:T(8,128)(2,1)}) custom-call(bf16[576,512]{1,0:T(8,128)(2,1)} %bitcast.11, s32[6,24]{1,0:T(8,128)} %ids_ref.1, bf16[608,576]{1,0:T(8,128)(2,1)} %constant.21.clone.perm_ref, bf16[24,3072]{1,0:T(8,128)(2,1)} %constant.22.clone.columns_ref, ...), custom_call_target="tpu_custom_call" | custom-call | tf_op jit(solution)/shard_map/pallas_call | solution.py:364
  3.5 8.9 %collective-permute-start = (bf16[224,512]{1,0:T(8,128)(2,1)}, bf16[224,512]{1,0:T(8,128)(2,1)S(1)}, u32[]{:S(2)}, u32[]{:S(2)}) collective-permute-start(bf16[224,512]{1,0:T(8,128)(2,1)} %get-tuple-element.26), channel_id=1, source_target_pairs={{0,240},{1,241},{2,242},{3,243},{4,244},{5,245},{6,246},{7,247},{8... | collective-permute-start | bytes 688136 | tf_op jit(solution)/shard_map/ppermute | solution.py:326
  12.4 1.0 collective-permute-start.1
  13.3 3.8 %collective-permute-start.2 = (bf16[80,512]{1,0:T(8,128)(2,1)}, bf16[80,512]{1,0:T(8,128)(2,1)S(1)}, u32[]{:S(2)}, u32[]{:S(2)}) collective-permute-start(bf16[80,512]{1,0:T(8,128)(2,1)} %get-tuple-element.28), channel_id=1, source_target_pairs={{0,255},{1,240},{2,241},{3,242},{4,243},{5,244},{6,245},{7,246},{8... | collective-permute-start | bytes 245768 | tf_op jit(solution)/shard_map/ppermute | solution.py:326
  17.1 0.0 collective-permute-done.1.west_ref
  17.1 3.0 %collective-permute-done.2.corner_ref = bf16[80,512]{1,0:T(8,128)(2,1)S(1)} collective-permute-done((bf16[80,512]{1,0:T(8,128)(2,1)}, bf16[80,512]{1,0:T(8,128)(2,1)S(1)}, u32[]{:S(2)}, u32[]{:S(2)}) %collective-permute-start.2) | collective-permute-done | bytes 81952 | tf_op jit(solution)/shard_map/ppermute | solution.py:326
  20.1 0.0 collective-permute-done.north_ref
  20.1 0.6 copy-done.3
  20.7 0.1 copy-done
  20.8 6.1 %shard_map.173 = (bf16[224,512]{1,0:T(8,128)(2,1)}, bf16[224,512]{1,0:T(8,128)(2,1)}, bf16[80,512]{1,0:T(8,128)(2,1)}, bf16[80,512]{1,0:T(8,128)(2,1)}) custom-call(s32[1,1]{1,0:T(1,128)} %bitcast.flag_ref, bf16[224,512]{1,0:T(8,128)(2,1)} %get-tuple-element.25.main_ref, bf16[224,512]{1,0:T(8,128)(2,1)} %copy-done, bf16[80,512]{1,0:T(8,128)(2,1)} %copy-done.2, ...), custom_call_target="tpu_custom_call" | custom-call | tf_op jit(solution)/shard_map/pallas_call | solution.py:378
  26.9 0.1 collective-permute-start.3
  27.0 1.3 %collective-permute-start.4 = (bf16[80,512]{1,0:T(8,128)(2,1)}, bf16[80,512]{1,0:T(8,128)(2,1)S(1)}, u32[]{:S(2)}, u32[]{:S(2)}) collective-permute-start(bf16[80,512]{1,0:T(8,128)(2,1)} %get-tuple-element.31), channel_id=1, source_target_pairs={{0,1},{1,2},{2,3},{3,4},{4,5},{5,6},{6,7},{7,8},{8,9},{9,10},{10,1... | collective-permute-start | bytes 245768 | tf_op jit(solution)/shard_map/ppermute | solution.py:326
  28.3 0.4 collective-permute-start.5
  28.7 0.7 pad.4.whead_ref
  29.4 5.1 %shard_map.174 = (bf16[13,144,128]{2,1,0:T(8,128)(2,1)}, bf16[13,144,512]{2,1,0:T(8,128)(2,1)}, bf16[512,128]{1,0:T(8,128)(2,1)}, f32[16,128]{1,0:T(8,128)}) custom-call(bf16[144,1040]{1,0:T(8,128)(2,1)} %bitcast.12, bf16[13,512]{1,0:T(8,128)(2,1)} %queries_ref.5, bf16[512,512]{1,0:T(8,128)(2,1)} %wo_ref.3, bf16[128,512]{1,0:T(8,128)(2,1)} %pad.4.whead_ref), custom_call_target="tpu_custom_call" | custom-call | tf_op jit(solution)/shard_map/pallas_call | solution.py:369
  34.4 0.0 collective-permute-done.4.west_ref
  34.4 6.8 %collective-permute-done.5.corner_ref = bf16[80,512]{1,0:T(8,128)(2,1)S(1)} collective-permute-done((bf16[80,512]{1,0:T(8,128)(2,1)}, bf16[80,512]{1,0:T(8,128)(2,1)S(1)}, u32[]{:S(2)}, u32[]{:S(2)}) %collective-permute-start.5) | collective-permute-done | bytes 81952 | tf_op jit(solution)/shard_map/ppermute | solution.py:326
  41.2 0.0 collective-permute-done.3.north_ref
  41.2 0.6 copy-done.6
  41.9 0.1 copy-done.1
  41.9 12.9 %shard_map.175 = (bf16[576,512]{1,0:T(8,128)(2,1)}, bf16[144,1040]{1,0:T(8,128)(2,1)}, bf16[768,512]{1,0:T(8,128)(2,1)}) custom-call(bf16[224,512]{1,0:T(8,128)(2,1)} %get-tuple-element.29.main_ref, bf16[224,512]{1,0:T(8,128)(2,1)} %copy-done.1, bf16[80,512]{1,0:T(8,128)(2,1)} %copy-done.5, bf16[80,512]{1,0:T(8,128)(2,1)} %copy-done.6, ...), custom_call_target="tpu_custom_call" | custom-call | tf_op jit(solution)/shard_map/pallas_call | solution.py:385
  54.8 17.6 %all_to_all.15 = bf16[16,48,512]{2,1,0:T(8,128)(2,1)S(1)} all-to-all(bf16[16,48,512]{2,1,0:T(8,128)(2,1)} %bitcast.10), channel_id=1, replica_groups=mesh['lat'=16,'lon'=16] {'lon'}, dimensions={0} | all-to-all | bytes 1572864 | tf_op jit(solution)/shard_map/all_to_all | solution.py:353
  72.4 0.1 reduce_sum.24
  72.6 8.4 %all_to_all.16 = bf16[4,48,512]{2,1,0:T(8,128)(2,1)S(1)} all-to-all(bf16[4,48,512]{2,1,0:T(8,128)(2,1)S(1)} %broadcast_in_dim.4), channel_id=1, replica_groups={{0,16,32,48},{64,80,96,112},{128,144,160,176},{192,208,224,240},{1,17,3..., dimensions={0} | all-to-all | bytes 393216 | tf_op jit(solution)/shard_map/all_to_all | solution.py:343
  81.0 2.8 %collective-permute-start.8 = (bf16[48,512]{1,0:T(8,128)(2,1)S(1)}, bf16[48,512]{1,0:T(8,128)(2,1)S(1)}, u32[]{:S(2)}, u32[]{:S(2)}) collective-permute-start(bf16[48,512]{1,0:T(8,128)(2,1)S(1)} %reduce_sum.25), channel_id=1, source_target_pairs={{0,192},{1,193},{2,194},{3,195},{4,196},{5,197},{6,198},{7,199},{8... | collective-permute-start | bytes 147464 | tf_op jit(solution)/shard_map/ppermute | solution.py:326
  83.7 1.5 %collective-permute-start.7 = (bf16[48,512]{1,0:T(8,128)(2,1)S(1)}, bf16[48,512]{1,0:T(8,128)(2,1)S(1)}, u32[]{:S(2)}, u32[]{:S(2)}) collective-permute-start(bf16[48,512]{1,0:T(8,128)(2,1)S(1)} %reduce_sum.25), channel_id=1, source_target_pairs={{0,128},{1,129},{2,130},{3,131},{4,132},{5,133},{6,134},{7,135},{8... | collective-permute-start | bytes 147464 | tf_op jit(solution)/shard_map/ppermute | solution.py:326
  85.2 1.4 %collective-permute-start.6 = (bf16[48,512]{1,0:T(8,128)(2,1)S(1)}, bf16[48,512]{1,0:T(8,128)(2,1)S(1)}, u32[]{:S(2)}, u32[]{:S(2)}) collective-permute-start(bf16[48,512]{1,0:T(8,128)(2,1)S(1)} %reduce_sum.25), channel_id=1, source_target_pairs={{0,64},{1,65},{2,66},{3,67},{4,68},{5,69},{6,70},{7,71},{8,72},{9,... | collective-permute-start | bytes 147464 | tf_op jit(solution)/shard_map/ppermute | solution.py:326
  86.6 4.0 %collective-permute-done.7 = bf16[48,512]{1,0:T(8,128)(2,1)S(1)} collective-permute-done((bf16[48,512]{1,0:T(8,128)(2,1)S(1)}, bf16[48,512]{1,0:T(8,128)(2,1)S(1)}, u32[]{:S(2)}, u32[]{:S(2)}) %collective-permute-start.7) | collective-permute-done | bytes 49184 | tf_op jit(solution)/shard_map/ppermute | solution.py:326
  90.6 0.6 collective-permute-done.6
  91.3 0.1 broadcast_in_dim.5
  91.4 19.7 %all_to_all.17 = bf16[16,48,512]{2,1,0:T(8,128)(2,1)} all-to-all(bf16[16,48,512]{2,1,0:T(8,128)(2,1)S(1)} %broadcast_in_dim.5), channel_id=1, replica_groups=mesh['lat'=16,'lon'=16] {'lon'}, dimensions={0} | all-to-all | bytes 1572864 | tf_op jit(solution)/shard_map/all_to_all | solution.py:356
  111.0 4.4 %shard_map.176 = (f32[512,1024]{1,0:T(8,128)}, f32[13,512]{1,0:T(8,128)}, f32[512,512]{1,0:T(8,128)}, f32[80,512]{1,0:T(8,128)}) custom-call(bf16[768,512]{1,0:T(8,128)(2,1)} %bitcast.9, bf16[512,1024]{1,0:T(8,128)(2,1)} %wkv_ref.3, bf16[13,512]{1,0:T(8,128)(2,1)} %queries_ref.5, bf16[512,512]{1,0:T(8,128)(2,1)} %wo_ref.3, bf16[128,512]{1,0:T(8,128)(2,1)} %pad.4.whead_ref), custom_call_target="tpu_custom_call" | custom-call | tf_op jit(solution)/shard_map/pallas_call | solution.py:398
  (14 shorter events, 0.1 us)
Async XLA Ops:
  0.6 28.1 %copy-start.4 = (bf16[512,80]{0,1:T(8,128)(2,1)S(1)}, bf16[512,80]{0,1:T(8,128)(2,1)}, u32[]{:S(2)}) copy-start(bf16[512,80]{0,1:T(8,128)(2,1)} %param.20) | copy-start | bytes 245764
  3.5 16.6 %collective-permute-start = (bf16[224,512]{1,0:T(8,128)(2,1)}, bf16[224,512]{1,0:T(8,128)(2,1)S(1)}, u32[]{:S(2)}, u32[]{:S(2)}) collective-permute-start(bf16[224,512]{1,0:T(8,128)(2,1)} %get-tuple-element.26), channel_id=1, source_target_pairs={{0,240},{1,241},{2,242},{3,243},{4,244},{5,245},{6,246},{7,247},{8... | collective-permute-start | bytes 688136 | tf_op jit(solution)/shard_map/ppermute | solution.py:326
  12.4 4.8 %collective-permute-start.1 = (bf16[80,512]{1,0:T(8,128)(2,1)}, bf16[80,512]{1,0:T(8,128)(2,1)S(1)}, u32[]{:S(2)}, u32[]{:S(2)}) collective-permute-start(bf16[80,512]{1,0:T(8,128)(2,1)} %get-tuple-element.27), channel_id=1, source_target_pairs={{0,15},{1,0},{2,1},{3,2},{4,3},{5,4},{6,5},{7,6},{8,7},{9,8},{10,9... | collective-permute-start | bytes 245768 | tf_op jit(solution)/shard_map/ppermute | solution.py:326
  13.3 6.8 %collective-permute-start.2 = (bf16[80,512]{1,0:T(8,128)(2,1)}, bf16[80,512]{1,0:T(8,128)(2,1)S(1)}, u32[]{:S(2)}, u32[]{:S(2)}) collective-permute-start(bf16[80,512]{1,0:T(8,128)(2,1)} %get-tuple-element.28), channel_id=1, source_target_pairs={{0,255},{1,240},{2,241},{3,242},{4,243},{5,244},{6,245},{7,246},{8... | collective-permute-start | bytes 245768 | tf_op jit(solution)/shard_map/ppermute | solution.py:326
  17.1 3.0 %copy-start.2 = (bf16[80,512]{1,0:T(8,128)(2,1)}, bf16[80,512]{1,0:T(8,128)(2,1)S(1)}, u32[]{:S(2)}) copy-start(bf16[80,512]{1,0:T(8,128)(2,1)S(1)} %collective-permute-done.1.west_ref) | copy-start | bytes 245764
  20.1 0.6 copy-start.3
  20.1 0.7 copy-start
  26.9 14.3 %collective-permute-start.3 = (bf16[224,512]{1,0:T(8,128)(2,1)}, bf16[224,512]{1,0:T(8,128)(2,1)S(1)}, u32[]{:S(2)}, u32[]{:S(2)}) collective-permute-start(bf16[224,512]{1,0:T(8,128)(2,1)} %get-tuple-element.30), channel_id=1, source_target_pairs={{0,16},{1,17},{2,18},{3,19},{4,20},{5,21},{6,22},{7,23},{8,24},{9,... | collective-permute-start | bytes 688136 | tf_op jit(solution)/shard_map/ppermute | solution.py:326
  27.0 7.4 %collective-permute-start.4 = (bf16[80,512]{1,0:T(8,128)(2,1)}, bf16[80,512]{1,0:T(8,128)(2,1)S(1)}, u32[]{:S(2)}, u32[]{:S(2)}) collective-permute-start(bf16[80,512]{1,0:T(8,128)(2,1)} %get-tuple-element.31), channel_id=1, source_target_pairs={{0,1},{1,2},{2,3},{3,4},{4,5},{5,6},{6,7},{7,8},{8,9},{9,10},{10,1... | collective-permute-start | bytes 245768 | tf_op jit(solution)/shard_map/ppermute | solution.py:326
  28.3 12.9 %collective-permute-start.5 = (bf16[80,512]{1,0:T(8,128)(2,1)}, bf16[80,512]{1,0:T(8,128)(2,1)S(1)}, u32[]{:S(2)}, u32[]{:S(2)}) collective-permute-start(bf16[80,512]{1,0:T(8,128)(2,1)} %get-tuple-element.32), channel_id=1, source_target_pairs={{0,17},{1,18},{2,19},{3,20},{4,21},{5,22},{6,23},{7,24},{8,25},{9,... | collective-permute-start | bytes 245768 | tf_op jit(solution)/shard_map/ppermute | solution.py:326
  34.4 6.8 %copy-start.5 = (bf16[80,512]{1,0:T(8,128)(2,1)}, bf16[80,512]{1,0:T(8,128)(2,1)S(1)}, u32[]{:S(2)}) copy-start(bf16[80,512]{1,0:T(8,128)(2,1)S(1)} %collective-permute-done.4.west_ref) | copy-start | bytes 245764
  41.2 0.6 copy-start.6
  41.2 0.7 copy-start.1
  81.0 5.7 %collective-permute-start.8 = (bf16[48,512]{1,0:T(8,128)(2,1)S(1)}, bf16[48,512]{1,0:T(8,128)(2,1)S(1)}, u32[]{:S(2)}, u32[]{:S(2)}) collective-permute-start(bf16[48,512]{1,0:T(8,128)(2,1)S(1)} %reduce_sum.25), channel_id=1, source_target_pairs={{0,192},{1,193},{2,194},{3,195},{4,196},{5,197},{6,198},{7,199},{8... | collective-permute-start | bytes 147464 | tf_op jit(solution)/shard_map/ppermute | solution.py:326
  83.7 6.9 %collective-permute-start.7 = (bf16[48,512]{1,0:T(8,128)(2,1)S(1)}, bf16[48,512]{1,0:T(8,128)(2,1)S(1)}, u32[]{:S(2)}, u32[]{:S(2)}) collective-permute-start(bf16[48,512]{1,0:T(8,128)(2,1)S(1)} %reduce_sum.25), channel_id=1, source_target_pairs={{0,128},{1,129},{2,130},{3,131},{4,132},{5,133},{6,134},{7,135},{8... | collective-permute-start | bytes 147464 | tf_op jit(solution)/shard_map/ppermute | solution.py:326
  85.2 6.0 %collective-permute-start.6 = (bf16[48,512]{1,0:T(8,128)(2,1)S(1)}, bf16[48,512]{1,0:T(8,128)(2,1)S(1)}, u32[]{:S(2)}, u32[]{:S(2)}) collective-permute-start(bf16[48,512]{1,0:T(8,128)(2,1)S(1)} %reduce_sum.25), channel_id=1, source_target_pairs={{0,64},{1,65},{2,66},{3,67},{4,68},{5,69},{6,70},{7,71},{8,72},{9,... | collective-permute-start | bytes 147464 | tf_op jit(solution)/shard_map/ppermute | solution.py:326

commit v3 on v2

--- a/solution.py
+++ b/solution.py
@@ -22,6 +22,7 @@
 SIDE = 80
 PACKED = 2 * MAIN + 2 * SIDE
 ROWS = 768
+BLOCK = 48
 LANES = 128
 
 SPAN = 256
@@ -31,6 +32,10 @@
     {2: (448, 40, 80), 3: (488, 40, 80)},
     {2: (528, 40, 120), 3: (568, 40, 120)},
 )
+
+LAT = ("z", "x_hi")
+LON = ("x_lo", "y", "core")
+PLANE = ("x_hi", "x_lo", "y")
 
 norm_eps = 1e-05
 clip_eps = 1e-06
@@ -171,10 +176,11 @@
     corner_out[...] = mixed[c:]
 
 
-def expand_matrix(level):
+def expand_matrices():
     c = lax.broadcasted_iota(jnp.int32, (LANES, D), 0)
     j = lax.broadcasted_iota(jnp.int32, (LANES, D), 1)
-    return (c == level * HEADS + j // (D // HEADS)).astype(F32).astype(BF)
+    gap = c - j // (D // HEADS)
+    return [jnp.where(gap == level * HEADS, 1.0, 0.0).astype(BF) for level in range(PLEV)]
 
 
 def shift_matrix(offset, width):
@@ -197,79 +203,101 @@
     return jnp.where(c % HEADS == j // (D // HEADS), tall, 0.0)
 
 
-def pre_kernel(cot_ref, queries_ref, wo_ref, whead_ref, up_ref, dctx_ref, map_ref, base_ref):
+def pre_kernel(cot_ref, queries_ref, wo_ref, whead_ref, up_ref, dctx_ref, dsum_ref, map_ref, base_ref):
     head = whead_ref[...]
     both = dot(wo_ref[...], head, ((1,), (1,))).astype(BF)
     map_ref[...] = both
     base_ref[...] = jnp.concatenate(
         [dot(queries_ref[...], head, ((1,), (1,))), jnp.zeros((16 - PLEV, LANES), F32)], axis=0
     )
+    dsum = jnp.zeros((PATCHES, D), F32)
     for level in range(PLEV):
         first, offset, width = spot(level)
         up = mm(cot_ref[:, first : first + width], shift_matrix(offset, width)).astype(BF)
         up_ref[level] = up
-        dctx_ref[level] = dot(up, both, ((1,), (1,))).astype(BF)
+        dctx = dot(up, both, ((1,), (1,))).astype(BF)
+        dctx_ref[level] = dctx
+        dsum = dsum + dctx.astype(F32)
+    dsum_ref[...] = dsum
 
 
 def decode_kernel(
-    main_ref, north_ref, west_ref, corner_ref, perm_ref, wkv_ref, queries_ref, up_ref, dctx_ref, map_ref, base_ref,
-    owned_ref, fields_ref, sums_ref,
-    pair, weights, dweights, dvalues, context, fields,
+    flag_ref, main_ref, north_ref, west_ref, corner_ref, perm_ref, wkv_ref, queries_ref, up_ref, dctx_ref, dsum_ref,
+    map_ref, base_ref,
+    owned_ref, fields_ref, keep_ref, send_ref,
+    value, weights, dvalues, context, products, fields, sums,
 ):
     pieces = (main_ref, north_ref, west_ref, corner_ref)
     packed = jnp.concatenate([ref[...] for ref in pieces], axis=0)
     wide = dot(perm_ref[...], packed, ((0,), (0,)))
     owned_ref[...] = wide.astype(BF)
     normed = layer_norm(wide)
-    pair[...] = mm(normed, wkv_ref[...]).astype(BF).astype(F32)
+    key = mm(normed, wkv_ref[:, :D]).astype(BF)
+    value[...] = mm(normed, wkv_ref[:, D:]).astype(BF).astype(F32)
     queries = spread_queries(queries_ref[...].astype(F32)).astype(BF)
-    scores = dot(pair[:, :D].astype(BF), queries, ((1,), (1,))) * 0.125
+    scores = dot(key, queries, ((1,), (1,))) * 0.125
     slabs = [scores[l * PATCHES : (l + 1) * PATCHES] for l in range(LEV)]
     top = jnp.maximum(jnp.maximum(slabs[0], slabs[1]), jnp.maximum(slabs[2], slabs[3]))
     slabs = [jnp.exp(s - top) for s in slabs]
     scale = 1.0 / (slabs[0] + slabs[1] + slabs[2] + slabs[3])
+    slabs = [s * scale for s in slabs]
     for l in range(LEV):
-        weights[l * PATCHES : (l + 1) * PATCHES] = slabs[l] * scale
-    dweights[...] = jnp.zeros_like(dweights)
-    dvalues[...] = jnp.zeros_like(dvalues)
+        weights[l * PATCHES : (l + 1) * PATCHES] = slabs[l]
+    half = lax.broadcasted_iota(jnp.int32, (BLOCK, LANES), 1) // (D // HEADS)
+    for tile in range(D // LANES):
+        lanes = slice(tile * LANES, (tile + 1) * LANES)
+        for start in range(0, PATCHES, BLOCK):
+            at = [slice(l * PATCHES + start, l * PATCHES + start + BLOCK) for l in range(LEV)]
+            last = value[at[LEV - 1], lanes]
+            gaps = [value[at[l], lanes] - last for l in range(LEV - 1)]
+            heads = [weights[at[l]] for l in range(LEV - 1)]
+            found = [jnp.zeros((BLOCK, LANES), F32) for _ in range(LEV - 1)]
+            for level in range(PLEV):
+                index = half + (level * HEADS + 2 * tile)
+                upstream = dctx_ref[level, start : start + BLOCK, lanes].astype(F32)
+                total = last
+                for l in range(LEV - 1):
+                    spread = jnp.take_along_axis(heads[l], index, axis=1)
+                    total = total + spread * gaps[l]
+                    found[l] = found[l] + spread * upstream
+                    products[level, at[l], lanes] = (upstream * gaps[l]).astype(BF)
+                context[level * PATCHES + start : level * PATCHES + start + BLOCK, lanes] = total.astype(BF)
+            for l in range(LEV - 1):
+                dvalues[at[l], lanes] = found[l]
+            dvalues[at[LEV - 1], lanes] = dsum_ref[start : start + BLOCK, lanes] - (found[0] + found[1] + found[2])
     fields[...] = jnp.zeros_like(fields)
-    narrow = weights[...].astype(BF)
+    slopes = jnp.zeros(((LEV - 1) * PATCHES, LANES), F32)
+    expand = expand_matrices()
     for level in range(PLEV):
-        expand = expand_matrix(level)
-        spread = mm(narrow, expand)
-        upstream = dctx_ref[level].astype(F32)
-        total = jnp.zeros((PATCHES, D), F32)
-        for l in range(LEV):
-            at = slice(l * PATCHES, (l + 1) * PATCHES)
-            value = pair[at, D:]
-            part = spread[at]
-            total += part * value
-            dvalues[at] += part * upstream
-            dweights[at] += dot((upstream * value).astype(BF), expand, ((1,), (1,)))
-        total = total.astype(BF)
-        context[level * PATCHES : (level + 1) * PATCHES] = total
+        slopes = slopes + dot(products[level], expand[level], ((1,), (1,)))
         first, offset, width = spot(level)
-        decoded = (mm(total, map_ref[...]) + base_ref[level : level + 1]).astype(BF)
-        fields[:, first : first + width] += dot(decoded, shift_matrix(offset, width), ((1,), (1,)))
+        decoded = mm(context[level * PATCHES : (level + 1) * PATCHES], map_ref[...]) + base_ref[level : level + 1]
+        fields[:, first : first + width] += dot(decoded.astype(BF), shift_matrix(offset, width), ((1,), (1,)))
     fields_ref[...] = fields[...].astype(BF)
-    parts = [weights[l * PATCHES : (l + 1) * PATCHES] for l in range(LEV)]
-    slopes = [dweights[l * PATCHES : (l + 1) * PATCHES] for l in range(LEV)]
-    mean = sum(p * d for p, d in zip(parts, slopes))
-    dscores = jnp.concatenate([p * (d - mean) * 0.125 for p, d in zip(parts, slopes)], axis=0).astype(BF)
-    sums_ref[:D] = dot(normed, dvalues[...].astype(BF), ((0,), (0,))).astype(BF)
-    sums_ref[D : D + LANES] = dot(dscores, normed, ((0,), (0,))).astype(BF)
+    slopes = [slopes[l * PATCHES : (l + 1) * PATCHES] for l in range(LEV - 1)]
+    mean = sum(p * d for p, d in zip(slabs, slopes))
+    dscores = [p * (d - mean) * 0.125 for p, d in zip(slabs, slopes)]
+    dscores.append(slabs[LEV - 1] * mean * -0.125)
+    dscores = jnp.concatenate(dscores, axis=0).astype(BF)
+    sums[:D] = dot(normed, dvalues[...].astype(BF), ((0,), (0,)))
+    sums[D : D + LANES] = dot(dscores, normed, ((0,), (0,)))
     up = jnp.concatenate([up_ref[a] for a in range(PLEV)], axis=0)
     outer = dot(up, context[...], ((0,), (0,)))
-    sums_ref[D + LANES : D + LANES + OUTS] = outer[:OUTS].astype(BF)
+    sums[D + LANES : D + LANES + OUTS] = outer[:OUTS]
     totals = [jnp.sum(up_ref[a].astype(F32), axis=0, keepdims=True) for a in range(PLEV)]
     totals.append(jnp.zeros((LANES - OUTS - PLEV, LANES), F32))
     totals = jnp.concatenate(totals, axis=0)
-    totals = jnp.concatenate([totals, jnp.zeros((LANES - OUTS, D - LANES), F32)], axis=1)
-    sums_ref[D + LANES + OUTS :] = totals.astype(BF)
-
-
-def final_kernel(sums_ref, wkv_ref, queries_ref, wo_ref, whead_ref, kv_ref, query_ref, o_ref, head_ref):
-    sums = sums_ref[...]
+    sums[D + LANES + OUTS :] = jnp.concatenate([totals, jnp.zeros((LANES - OUTS, D - LANES), F32)], axis=1)
+    second = flag_ref[0, 0] > 0
+    top, bottom = sums[: ROWS // 2], sums[ROWS // 2 :]
+    keep_ref[...] = jnp.where(second, bottom, top).astype(BF)
+    send_ref[...] = jnp.where(second, top, bottom).astype(BF)
+
+
+def final_kernel(flag_ref, mine_ref, other_ref, wkv_ref, queries_ref, wo_ref, whead_ref, kv_ref, query_ref, o_ref, head_ref):
+    second = flag_ref[0, 0] > 0
+    mine, other = mine_ref[...].astype(F32), other_ref[...].astype(F32)
+    sums = jnp.concatenate([jnp.where(second, other, mine), jnp.where(second, mine, other)], axis=0).astype(BF)
     queries = queries_ref[...]
     head = whead_ref[...]
     keyed = sums[D : D + LANES]
@@ -298,11 +326,11 @@
     head_ref[...] = pixels * factor
 
 
-def call(kernel, outs, scratch=(), smem=False):
+def call(kernel, outs, scratch=(), smem=0):
     more = {}
     if smem:
         whole = pl.BlockSpec(memory_space=pltpu.VMEM)
-        more["in_specs"] = [pl.BlockSpec(memory_space=pltpu.SMEM)] + [whole] * 7
+        more["in_specs"] = [pl.BlockSpec(memory_space=pltpu.SMEM)] + [whole] * smem
     return pl.pallas_call(
         kernel,
         **more,
@@ -317,60 +345,54 @@
 
 
 def move(array, lat_step, lon_step):
-    lats, lons = lax.axis_size("lat"), lax.axis_size("lon")
+    lats, lons = lax.axis_size(LAT), lax.axis_size(LON)
     route = [
         (i * lons + j, (i + lat_step) % lats * lons + (j + lon_step) % lons)
         for i in range(lats)
         for j in range(lons)
     ]
-    return lax.ppermute(array, ("lat", "lon"), route)
-
-
-def lat_groups(count, stride):
-    lats = lax.axis_size("lat")
-    return [
-        [first + stride * i for i in range(count)]
-        for first in range(lats)
-        if first // stride % count == 0
-    ]
-
-
-def sum_over_lat(mine):
-    lats = lax.axis_size("lat")
-    low = min(4, lats)
-    high = lats // low
-    copies = jnp.broadcast_to(mine[None], (low,) + mine.shape)
-    copies = lax.all_to_all(copies, "lat", 0, 0, axis_index_groups=lat_groups(low, 1), tiled=True)
-    mine = jnp.sum(copies.astype(F32), axis=0).astype(BF)
-    others = [move(mine, low * step, 0) for step in range(1, high)]
-    return sum((other.astype(F32) for other in others), mine.astype(F32)).astype(BF)
-
-
-def sum_over_all(packed):
-    rows, width = packed.shape
-    lons = lax.axis_size("lon")
-    part = rows // lons
-    chunks = lax.all_to_all(packed.reshape(lons, part, width), "lon", 0, 0, tiled=True)
-    mine = sum_over_lat(jnp.sum(chunks.astype(F32), axis=0).astype(BF))
-    copies = jnp.broadcast_to(mine[None], (lons, part, width))
-    return lax.all_to_all(copies, "lon", 0, 0, tiled=True).reshape(rows, width)
+    return lax.ppermute(array, LAT + LON, route)
+
+
+def swap(array):
+    count = lax.axis_size("core")
+    return lax.ppermute(array, "core", [(i, (i + 1) % count) for i in range(count)])
+
+
+def add_up(blocks):
+    return jnp.sum(blocks.astype(F32), axis=0).astype(BF)
+
+
+def copies(block, axes):
+    return jnp.broadcast_to(block[None], (lax.axis_size(axes),) + block.shape)
+
+
+def sum_over_all(keep, send):
+    rows, width = keep.shape
+    mine = (keep.astype(F32) + swap(send).astype(F32)).astype(BF)
+    chips = lax.axis_size(PLANE)
+    mine = add_up(lax.all_to_all(mine.reshape(chips, rows // chips, width), PLANE, 0, 0, tiled=True))
+    mine = add_up(lax.all_to_all(copies(mine, "z"), "z", 0, 0, tiled=True))
+    mine = lax.all_to_all(copies(mine, PLANE), PLANE, 0, 0, tiled=True).reshape(rows, width)
+    return mine, swap(mine)
 
 
 def per_device(latents, mask_ids, w_qkv, w_out, w_kv, level_queries, w_o, w_head, field_cotangent):
     perm = jnp.asarray(pack_matrix(), BF)
     columns, rows, extra = label_tables()
-    flag = (lax.axis_index("lat") == lax.axis_size("lat") - 1).astype(jnp.int32).reshape(1, 1)
+    flag = (lax.axis_index(LAT) == lax.axis_size(LAT) - 1).astype(jnp.int32).reshape(1, 1)
     shapes = [struct((MAIN, D)), struct((MAIN, D)), struct((SIDE, D)), struct((SIDE, D))]
     main, north, west, corner = call(pack_kernel, shapes)(
         latents.reshape(TOKENS, D), mask_ids, perm, jnp.asarray(columns, BF), jnp.asarray(rows)
     )
     north, west, corner = move(north, -1, 0), move(west, 0, -1), move(corner, -1, -1)
     head = jnp.pad(w_head.T, ((0, LANES - OUTS), (0, 0)))
-    up, dctx, both, base = call(
+    up, dctx, dsum, both, base = call(
         pre_kernel,
         [
             struct((PLEV, PATCHES, LANES)),
             struct((PLEV, PATCHES, D)),
+            struct((PATCHES, D), F32),
             struct((D, LANES)),
             struct((16, LANES), F32),
         ],
@@ -379,41 +401,49 @@
         attention_kernel,
         shapes,
         [pltpu.VMEM((PACKED, 3 * D), F32), pltpu.VMEM((PACKED, D), F32)],
-        smem=True,
+        smem=7,
     )(flag, main, north, west, corner, jnp.asarray(extra), w_qkv, w_out)
     north, west, corner = move(north, 1, 0), move(west, 0, 1), move(corner, 1, 1)
-    owned, fields, sums = call(
+    core = lax.axis_index("core").astype(jnp.int32).reshape(1, 1)
+    share = struct((ROWS // 2, D))
+    owned, fields, keep, send = call(
         decode_kernel,
-        [struct((TOKENS, D)), struct((PATCHES, PLEV * OUTS)), struct((ROWS, D))],
+        [struct((TOKENS, D)), struct((PATCHES, PLEV * OUTS)), share, share],
         [
-            pltpu.VMEM((TOKENS, 2 * D), F32),
-            pltpu.VMEM((TOKENS, LANES), F32),
+            pltpu.VMEM((TOKENS, D), F32),
             pltpu.VMEM((TOKENS, LANES), F32),
             pltpu.VMEM((TOKENS, D), F32),
             pltpu.VMEM((PLEV * PATCHES, D), BF),
+            pltpu.VMEM((PLEV, (LEV - 1) * PATCHES, D), BF),
             pltpu.VMEM((PATCHES, PLEV * OUTS), F32),
+            pltpu.VMEM((ROWS, D), F32),
         ],
-    )(main, north, west, corner, perm, w_kv, level_queries, up, dctx, both, base)
-    sums = sum_over_all(sums)
+        smem=12,
+    )(core, main, north, west, corner, perm, w_kv, level_queries, up, dctx, dsum, both, base)
+    mine, other = sum_over_all(keep, send)
     kv, query, out, pixels = call(
         final_kernel,
         [struct((D, 2 * D), F32), struct((PLEV, D), F32), struct((D, D), F32), struct((OUTS, D), F32)],
-    )(sums, w_kv, level_queries, w_o, head)
+        smem=6,
+    )(core, mine, other, w_kv, level_queries, w_o, head)
     shape = latents.shape
     return (owned.reshape(shape), fields.reshape(shape[1], shape[2], PLEV * OUTS), kv, query, out, pixels.T)
 
 
 def solution(mesh):
+    lats, lons = mesh.shape["lat"], mesh.shape["lon"]
+    sizes = (lats // 2, 2, 2, lons // 4, 2)
+    fine = jax.sharding.Mesh(mesh.devices.reshape(sizes), LAT + LON)
     in_specs = (
-        P(None, "lat", "lon", None),
-        P("lat", "lon"),
-        P(),
-        P(),
-        P(),
-        P(),
-        P(),
-        P(),
-        P("lat", "lon", None),
+        P(None, LAT, LON, None),
+        P(LAT, LON),
+        P(),
+        P(),
+        P(),
+        P(),
+        P(),
+        P(),
+        P(LAT, LON, None),
     )
-    out_specs = (P(None, "lat", "lon", None), P("lat", "lon", None), P(), P(), P(), P())
-    return jax.shard_map(per_device, mesh=mesh, in_specs=in_specs, out_specs=out_specs, check_vma=False)
+    out_specs = (P(None, LAT, LON, None), P(LAT, LON, None), P(), P(), P(), P())
+    return jax.shard_map(per_device, mesh=fine, in_specs=in_specs, out_specs=out_specs, check_vma=False)

time: 116 us -> 107 us (0.922)
  blocking collectives: 45.6 us -> 36.2 us
  waiting for transfers between devices: 14.4 us -> 12.6 us
    all_to_all x3, blocking collectives: 45.6 us -> 36.2 us  [the longest x1 12.9 us: sum_over_all(): mine = add_up(lax.all_to_all(copies(mine, 'z'), 'z', 0, 0, tiled=True))]
    ppermute x9 -> x8, waiting for transfers between devices: 14.4 us -> 12.6 us  [the longest x6 9.73 us: move(): return lax.ppermute(array, LAT + LON, route)]
    ppermute x9 -> x8, starting transfers between devices: 21.1 us -> 21 us  [the longest x6 15.4 us: move(): return lax.ppermute(array, LAT + LON, route)]
  transfers between devices with their start and end apart: 9 -> 8, of which waited for: 4 -> 4; matrix products, arithmetic and copies ran while one was open for 1% -> 1% of each run, Pallas kernels for 4% -> 5%
where the time goes in v3:
time: 107 us
  blocking collectives  36.2 us (34%)
  Pallas kernels  32 us (30%)
  starting transfers between devices  21 us (20%)
  waiting for transfers between devices  12.6 us (12%)
  local copies, waits for them, and re-layouts  2.89 us (3%)
  other arithmetic  1.19 us (1%)
    ppermute x6, starting transfers between devices, move(): return lax.ppermute(array, LAT + LON, route)  15.4 us
    pallas_call x1, Pallas kernels, per_device(): call(decode_kernel, [struct((TOKENS, D)), struct((PATCHES, PLEV * OUTS)),...  13.5 us
    all_to_all x1, blocking collectives, sum_over_all(): mine = add_up(lax.all_to_all(copies(mine, 'z'), 'z', 0, 0, tiled=True))  12.9 us
    all_to_all x1, blocking collectives, sum_over_all(): lax.all_to_all(mine.reshape(chips, rows // chips, width), PLANE, 0, 0, ti...  11.9 us
    all_to_all x1, blocking collectives, sum_over_all(): lax.all_to_all(copies(mine, PLANE), PLANE, 0, 0, tiled=True)  11.4 us
    ppermute x6, waiting for transfers between devices, move(): return lax.ppermute(array, LAT + LON, route)  9.73 us
    pallas_call x1, Pallas kernels, per_device(): call(attention_kernel, shapes, [pltpu.VMEM((PACKED, 3 * D), F32), pltpu.V...  6.11 us
    ppermute x2, starting transfers between devices, swap(): lax.ppermute(array, 'core', [(i, (i + 1) % count) for i in range(count)])  5.63 us
  transfers between devices with their start and end apart: 8, of which 4 were waited for; matrix products, arithmetic and copies ran while one was open for 1% of the time, Pallas kernels for 5%

profile of v3, /device:TPU:1, one launch (start us, length us, event | category | flops | bytes accessed | tf_op | source)
XLA Modules:
  0.0 106.7 jit_solution(6146010271509782148)
XLA Ops:
  0.6 2.9 %shard_map.172 = (bf16[224,512]{1,0:T(8,128)(2,1)}, bf16[224,512]{1,0:T(8,128)(2,1)}, bf16[80,512]{1,0:T(8,128)(2,1)}, bf16[80,512]{1,0:T(8,128)(2,1)}) custom-call(bf16[576,512]{1,0:T(8,128)(2,1)} %bitcast.13, s32[6,24]{1,0:T(8,128)} %ids_ref.1, bf16[608,576]{1,0:T(8,128)(2,1)} %constant.32.clone.perm_ref, bf16[24,3072]{1,0:T(8,128)(2,1)} %constant.33.clone.columns_ref, ...), custom_call_target="tpu_custom_call" | custom-call | tf_op jit(solution)/shard_map/pallas_call | solution.py:385
  3.5 8.9 %collective-permute-start = (bf16[224,512]{1,0:T(8,128)(2,1)}, bf16[224,512]{1,0:T(8,128)(2,1)S(1)}, u32[]{:S(2)}, u32[]{:S(2)}) collective-permute-start(bf16[224,512]{1,0:T(8,128)(2,1)} %get-tuple-element.28), channel_id=1, source_target_pairs={{0,240},{1,241},{2,242},{3,243},{4,244},{5,245},{6,246},{7,247},{8... | collective-permute-start | bytes 688136 | tf_op jit(solution)/shard_map/ppermute | solution.py:354
  12.4 1.0 collective-permute-start.1
  13.3 3.8 %collective-permute-start.2 = (bf16[80,512]{1,0:T(8,128)(2,1)}, bf16[80,512]{1,0:T(8,128)(2,1)S(1)}, u32[]{:S(2)}, u32[]{:S(2)}) collective-permute-start(bf16[80,512]{1,0:T(8,128)(2,1)} %get-tuple-element.30), channel_id=1, source_target_pairs={{0,255},{1,240},{2,241},{3,242},{4,243},{5,244},{6,245},{7,246},{8... | collective-permute-start | bytes 245768 | tf_op jit(solution)/shard_map/ppermute | solution.py:354
  17.1 0.0 collective-permute-done.1.west_ref
  17.1 3.0 %collective-permute-done.2.corner_ref = bf16[80,512]{1,0:T(8,128)(2,1)S(1)} collective-permute-done((bf16[80,512]{1,0:T(8,128)(2,1)}, bf16[80,512]{1,0:T(8,128)(2,1)S(1)}, u32[]{:S(2)}, u32[]{:S(2)}) %collective-permute-start.2) | collective-permute-done | bytes 81952 | tf_op jit(solution)/shard_map/ppermute | solution.py:354
  20.1 0.0 collective-permute-done.north_ref
  20.1 0.6 copy-done.5
  20.7 0.1 copy-done.2
  20.8 6.1 %shard_map.173 = (bf16[224,512]{1,0:T(8,128)(2,1)}, bf16[224,512]{1,0:T(8,128)(2,1)}, bf16[80,512]{1,0:T(8,128)(2,1)}, bf16[80,512]{1,0:T(8,128)(2,1)}) custom-call(s32[1,1]{1,0:T(1,128)} %bitcast.1.flag_ref, bf16[224,512]{1,0:T(8,128)(2,1)} %get-tuple-element.27.main_ref, bf16[224,512]{1,0:T(8,128)(2,1)} %copy-done.2, bf16[80,512]{1,0:T(8,128)(2,1)} %copy-done.4, ...), custom_call_target="tpu_custom_call" | custom-call | tf_op jit(solution)/shard_map/pallas_call | solution.py:400
  26.9 0.1 collective-permute-start.3
  27.0 1.3 %collective-permute-start.4 = (bf16[80,512]{1,0:T(8,128)(2,1)}, bf16[80,512]{1,0:T(8,128)(2,1)S(1)}, u32[]{:S(2)}, u32[]{:S(2)}) collective-permute-start(bf16[80,512]{1,0:T(8,128)(2,1)} %get-tuple-element.33), channel_id=1, source_target_pairs={{0,1},{1,2},{2,3},{3,4},{4,5},{5,6},{6,7},{7,8},{8,9},{9,10},{10,1... | collective-permute-start | bytes 245768 | tf_op jit(solution)/shard_map/ppermute | solution.py:354
  28.3 0.4 collective-permute-start.5
  28.7 0.7 pad.4.whead_ref
  29.4 5.1 %shard_map.174 = (bf16[13,144,128]{2,1,0:T(8,128)(2,1)}, bf16[13,144,512]{2,1,0:T(8,128)(2,1)}, f32[144,512]{1,0:T(8,128)}, bf16[512,128]{1,0:T(8,128)(2,1)}, f32[16,128]{1,0:T(8,128)}) custom-call(bf16[144,1040]{1,0:T(8,128)(2,1)} %bitcast.14, bf16[13,512]{1,0:T(8,128)(2,1)} %queries_ref.5, bf16[512,512]{1,0:T(8,128)(2,1)} %wo_ref.3, ...), custom_call_target="tpu_custom_call" | custom-call | tf_op jit(solution)/shard_map/pallas_call | solution.py:390
  34.5 0.0 collective-permute-done.4.west_ref
  34.5 6.8 %collective-permute-done.5.corner_ref = bf16[80,512]{1,0:T(8,128)(2,1)S(1)} collective-permute-done((bf16[80,512]{1,0:T(8,128)(2,1)}, bf16[80,512]{1,0:T(8,128)(2,1)S(1)}, u32[]{:S(2)}, u32[]{:S(2)}) %collective-permute-start.5) | collective-permute-done | bytes 81952 | tf_op jit(solution)/shard_map/ppermute | solution.py:354
  41.2 0.0 collective-permute-done.3.north_ref
  41.3 0.6 copy-done.8
  41.9 0.1 copy-done.3
  42.0 13.5 %shard_map.175 = (bf16[576,512]{1,0:T(8,128)(2,1)}, bf16[144,1040]{1,0:T(8,128)(2,1)}, bf16[384,512]{1,0:T(8,128)(2,1)}, bf16[384,512]{1,0:T(8,128)(2,1)}) custom-call(s32[1,1]{1,0:T(1,128)} %bitcast.flag_ref, bf16[224,512]{1,0:T(8,128)(2,1)} %get-tuple-element.31.main_ref, bf16[224,512]{1,0:T(8,128)(2,1)} %copy-done.3, bf16[80,512]{1,0:T(8,128)(2,1)} %copy-done.7, ...), custom_call_target="tpu_custom_call" | custom-call | tf_op jit(solution)/shard_map/pallas_call | solution.py:409
  55.4 1.3 %collective-permute-start.6 = (bf16[384,512]{1,0:T(8,128)(2,1)}, bf16[384,512]{1,0:T(8,128)(2,1)S(1)}, u32[]{:S(2)}, u32[]{:S(2)}) collective-permute-start(bf16[384,512]{1,0:T(8,128)(2,1)} %get-tuple-element.43), channel_id=1, source_target_pairs={{0,1},{1,0},{2,3},{3,2},{4,5},{5,4},{6,7},{7,6},{8,9},{9,8},{10,11... | collective-permute-start | bytes 1179656 | tf_op jit(solution)/shard_map/ppermute | solution.py:359
  56.8 1.6 %collective-permute-done.6 = bf16[384,512]{1,0:T(8,128)(2,1)S(1)} collective-permute-done((bf16[384,512]{1,0:T(8,128)(2,1)}, bf16[384,512]{1,0:T(8,128)(2,1)S(1)}, u32[]{:S(2)}, u32[]{:S(2)}) %collective-permute-start.6) | collective-permute-done | bytes 393248 | tf_op jit(solution)/shard_map/ppermute | solution.py:359
  58.3 1.1 %add_convert_fusion = bf16[384,512]{1,0:T(8,128)(2,1)S(1)} fusion(bf16[384,512]{1,0:T(8,128)(2,1)S(1)} %collective-permute-done.6, bf16[384,512]{1,0:T(8,128)(2,1)} %get-tuple-element.42), kind=kLoop, calls=%fused_computation | loop fusion | flops 786432 | bytes 1179648 | tf_op jit(solution)/shard_map/convert_element_type | solution.py:372
  59.4 11.9 %all_to_all.15 = bf16[16,24,512]{2,1,0:T(8,128)(2,1)S(1)} all-to-all(bf16[16,24,512]{2,1,0:T(8,128)(2,1)S(1)} %bitcast.10), channel_id=1, replica_groups=mesh['z'=8,'x_hi'=2,'x_lo'=2,'y'=4,'core'=2] {'x_hi','x_lo','y'}, dimensions={0} | all-to-all | bytes 786432 | tf_op jit(solution)/shard_map/all_to_all | solution.py:374
  71.4 0.1 reduce_sum.24
  71.4 12.9 %all_to_all.16 = bf16[8,24,512]{2,1,0:T(8,128)(2,1)S(1)} all-to-all(bf16[8,24,512]{2,1,0:T(8,128)(2,1)S(1)} %broadcast_in_dim.4), channel_id=1, replica_groups=mesh['z'=8,'x_hi'=2,'x_lo'=2,'y'=4,'core'=2] {'z'}, dimensions={0} | all-to-all | bytes 393216 | tf_op jit(solution)/shard_map/all_to_all | solution.py:375
  84.4 11.4 %all_to_all.17 = bf16[16,24,512]{2,1,0:T(8,128)(2,1)S(1)} all-to-all(bf16[16,24,512]{2,1,0:T(8,128)(2,1)S(1)} %broadcast_in_dim.5), channel_id=1, replica_groups=mesh['z'=8,'x_hi'=2,'x_lo'=2,'y'=4,'core'=2] {'x_hi','x_lo','y'}, dimensions={0} | all-to-all | bytes 786432 | tf_op jit(solution)/shard_map/all_to_all | solution.py:376
  95.8 4.3 %collective-permute-start.7 = (bf16[384,512]{1,0:T(8,128)(2,1)S(1)}, bf16[384,512]{1,0:T(8,128)(2,1)S(1)}, u32[]{:S(2)}, u32[]{:S(2)}) collective-permute-start(bf16[384,512]{1,0:T(8,128)(2,1)S(1)} %bitcast.11), channel_id=1, source_target_pairs={{0,1},{1,0},{2,3},{3,2},{4,5},{5,4},{6,7},{7,6},{8,9},{9,8},{10,11... | collective-permute-start | bytes 1179656 | tf_op jit(solution)/shard_map/ppermute | solution.py:359
  100.1 1.3 %collective-permute-done.7.other_ref = bf16[384,512]{1,0:T(8,128)(2,1)S(1)} collective-permute-done((bf16[384,512]{1,0:T(8,128)(2,1)S(1)}, bf16[384,512]{1,0:T(8,128)(2,1)S(1)}, u32[]{:S(2)}, u32[]{:S(2)}) %collective-permute-start.7) | collective-permute-done | bytes 393248 | tf_op jit(solution)/shard_map/ppermute | solution.py:359
  101.5 0.7 copy-done.1
  102.2 4.4 %shard_map.176 = (f32[512,1024]{1,0:T(8,128)}, f32[13,512]{1,0:T(8,128)}, f32[512,512]{1,0:T(8,128)}, f32[80,512]{1,0:T(8,128)}) custom-call(s32[1,1]{1,0:T(1,128)} %bitcast.flag_ref, bf16[384,512]{1,0:T(8,128)(2,1)} %bitcast.12, bf16[384,512]{1,0:T(8,128)(2,1)} %copy-done.1, bf16[512,1024]{1,0:T(8,128)(2,1)} %wkv_ref.3, bf16[13,512]{1,0:T(8,128)(2,1)} %queries_ref.5, ...), custom_call_target="tpu_custom_call" | custom-call | tf_op jit(solution)/shard_map/pallas_call | solution.py:424
  (16 shorter events, 0.1 us)
Async XLA Ops:
  0.6 28.1 %copy-start.6 = (bf16[512,80]{0,1:T(8,128)(2,1)S(1)}, bf16[512,80]{0,1:T(8,128)(2,1)}, u32[]{:S(2)}) copy-start(bf16[512,80]{0,1:T(8,128)(2,1)} %param.20) | copy-start | bytes 245764
  3.5 16.6 %collective-permute-start = (bf16[224,512]{1,0:T(8,128)(2,1)}, bf16[224,512]{1,0:T(8,128)(2,1)S(1)}, u32[]{:S(2)}, u32[]{:S(2)}) collective-permute-start(bf16[224,512]{1,0:T(8,128)(2,1)} %get-tuple-element.28), channel_id=1, source_target_pairs={{0,240},{1,241},{2,242},{3,243},{4,244},{5,245},{6,246},{7,247},{8... | collective-permute-start | bytes 688136 | tf_op jit(solution)/shard_map/ppermute | solution.py:354
  12.4 4.8 %collective-permute-start.1 = (bf16[80,512]{1,0:T(8,128)(2,1)}, bf16[80,512]{1,0:T(8,128)(2,1)S(1)}, u32[]{:S(2)}, u32[]{:S(2)}) collective-permute-start(bf16[80,512]{1,0:T(8,128)(2,1)} %get-tuple-element.29), channel_id=1, source_target_pairs={{0,15},{1,0},{2,1},{3,2},{4,3},{5,4},{6,5},{7,6},{8,7},{9,8},{10,9... | collective-permute-start | bytes 245768 | tf_op jit(solution)/shard_map/ppermute | solution.py:354
  13.3 6.8 %collective-permute-start.2 = (bf16[80,512]{1,0:T(8,128)(2,1)}, bf16[80,512]{1,0:T(8,128)(2,1)S(1)}, u32[]{:S(2)}, u32[]{:S(2)}) collective-permute-start(bf16[80,512]{1,0:T(8,128)(2,1)} %get-tuple-element.30), channel_id=1, source_target_pairs={{0,255},{1,240},{2,241},{3,242},{4,243},{5,244},{6,245},{7,246},{8... | collective-permute-start | bytes 245768 | tf_op jit(solution)/shard_map/ppermute | solution.py:354
  17.1 3.0 %copy-start.4 = (bf16[80,512]{1,0:T(8,128)(2,1)}, bf16[80,512]{1,0:T(8,128)(2,1)S(1)}, u32[]{:S(2)}) copy-start(bf16[80,512]{1,0:T(8,128)(2,1)S(1)} %collective-permute-done.1.west_ref) | copy-start | bytes 245764
  20.1 0.6 copy-start.5
  20.1 0.7 copy-start.2
  26.9 14.3 %collective-permute-start.3 = (bf16[224,512]{1,0:T(8,128)(2,1)}, bf16[224,512]{1,0:T(8,128)(2,1)S(1)}, u32[]{:S(2)}, u32[]{:S(2)}) collective-permute-start(bf16[224,512]{1,0:T(8,128)(2,1)} %get-tuple-element.32), channel_id=1, source_target_pairs={{0,16},{1,17},{2,18},{3,19},{4,20},{5,21},{6,22},{7,23},{8,24},{9,... | collective-permute-start | bytes 688136 | tf_op jit(solution)/shard_map/ppermute | solution.py:354
  27.0 7.5 %collective-permute-start.4 = (bf16[80,512]{1,0:T(8,128)(2,1)}, bf16[80,512]{1,0:T(8,128)(2,1)S(1)}, u32[]{:S(2)}, u32[]{:S(2)}) collective-permute-start(bf16[80,512]{1,0:T(8,128)(2,1)} %get-tuple-element.33), channel_id=1, source_target_pairs={{0,1},{1,2},{2,3},{3,4},{4,5},{5,6},{6,7},{7,8},{8,9},{9,10},{10,1... | collective-permute-start | bytes 245768 | tf_op jit(solution)/shard_map/ppermute | solution.py:354
  28.3 12.9 %collective-permute-start.5 = (bf16[80,512]{1,0:T(8,128)(2,1)}, bf16[80,512]{1,0:T(8,128)(2,1)S(1)}, u32[]{:S(2)}, u32[]{:S(2)}) collective-permute-start(bf16[80,512]{1,0:T(8,128)(2,1)} %get-tuple-element.34), channel_id=1, source_target_pairs={{0,17},{1,18},{2,19},{3,20},{4,21},{5,22},{6,23},{7,24},{8,25},{9,... | collective-permute-start | bytes 245768 | tf_op jit(solution)/shard_map/ppermute | solution.py:354
  34.5 6.8 %copy-start.7 = (bf16[80,512]{1,0:T(8,128)(2,1)}, bf16[80,512]{1,0:T(8,128)(2,1)S(1)}, u32[]{:S(2)}) copy-start(bf16[80,512]{1,0:T(8,128)(2,1)S(1)} %collective-permute-done.4.west_ref) | copy-start | bytes 245764
  41.2 0.6 copy-start.8
  41.3 0.7 copy-start.3
  55.4 2.9 %collective-permute-start.6 = (bf16[384,512]{1,0:T(8,128)(2,1)}, bf16[384,512]{1,0:T(8,128)(2,1)S(1)}, u32[]{:S(2)}, u32[]{:S(2)}) collective-permute-start(bf16[384,512]{1,0:T(8,128)(2,1)} %get-tuple-element.43), channel_id=1, source_target_pairs={{0,1},{1,0},{2,3},{3,2},{4,5},{5,4},{6,7},{7,6},{8,9},{9,8},{10,11... | collective-permute-start | bytes 1179656 | tf_op jit(solution)/shard_map/ppermute | solution.py:359
  95.8 5.6 %copy-start = (bf16[16,24,512]{2,1,0:T(8,128)(2,1)}, bf16[16,24,512]{2,1,0:T(8,128)(2,1)S(1)}, u32[]{:S(2)}) copy-start(bf16[16,24,512]{2,1,0:T(8,128)(2,1)S(1)} %all_to_all.17) | copy-start | bytes 1179652
  95.8 5.6 %collective-permute-start.7 = (bf16[384,512]{1,0:T(8,128)(2,1)S(1)}, bf16[384,512]{1,0:T(8,128)(2,1)S(1)}, u32[]{:S(2)}, u32[]{:S(2)}) collective-permute-start(bf16[384,512]{1,0:T(8,128)(2,1)S(1)} %bitcast.11), channel_id=1, source_target_pairs={{0,1},{1,0},{2,3},{3,2},{4,5},{5,4},{6,7},{7,6},{8,9},{9,8},{10,11... | collective-permute-start | bytes 1179656 | tf_op jit(solution)/shard_map/ppermute | solution.py:359
  101.5 0.8 copy-start.1

commit v4 on v3

--- a/solution.py
+++ b/solution.py
@@ -22,7 +22,7 @@
 SIDE = 80
 PACKED = 2 * MAIN + 2 * SIDE
 ROWS = 768
-BLOCK = 48
+BLOCK = 16
 LANES = 128
 
 SPAN = 256
@@ -125,7 +125,7 @@
 
 
 def attention_kernel(
-    flag_ref, main_ref, north_ref, west_ref, corner_ref, extra_ref, wqkv_ref, wout_ref,
+    flag_ref, extra_ref, main_ref, north_ref, west_ref, corner_ref, wqkv_ref, wout_ref,
     main_out, north_out, west_out, corner_out, proj, context,
 ):
     pieces = (main_ref, north_ref, west_ref, corner_ref)
@@ -229,7 +229,7 @@
 ):
     pieces = (main_ref, north_ref, west_ref, corner_ref)
     packed = jnp.concatenate([ref[...] for ref in pieces], axis=0)
-    wide = dot(perm_ref[...], packed, ((0,), (0,)))
+    wide = mm(perm_ref[...], packed)
     owned_ref[...] = wide.astype(BF)
     normed = layer_norm(wide)
     key = mm(normed, wkv_ref[:, :D]).astype(BF)
@@ -294,6 +294,10 @@
     send_ref[...] = jnp.where(second, top, bottom).astype(BF)
 
 
+def add_kernel(left_ref, right_ref, out_ref):
+    out_ref[...] = (left_ref[...].astype(F32) + right_ref[...].astype(F32)).astype(BF)
+
+
 def final_kernel(flag_ref, mine_ref, other_ref, wkv_ref, queries_ref, wo_ref, whead_ref, kv_ref, query_ref, o_ref, head_ref):
     second = flag_ref[0, 0] > 0
     mine, other = mine_ref[...].astype(F32), other_ref[...].astype(F32)
@@ -326,22 +330,33 @@
     head_ref[...] = pixels * factor
 
 
-def call(kernel, outs, scratch=(), smem=0):
-    more = {}
-    if smem:
-        whole = pl.BlockSpec(memory_space=pltpu.VMEM)
-        more["in_specs"] = [pl.BlockSpec(memory_space=pltpu.SMEM)] + [whole] * smem
-    return pl.pallas_call(
+def call(kernel, outs, spaces, scratch=(), limit=40):
+    where = {"V": pltpu.VMEM, "H": pltpu.HBM}
+    whole, scalar = pl.BlockSpec(memory_space=pltpu.VMEM), pl.BlockSpec(memory_space=pltpu.SMEM)
+    run = pl.pallas_call(
         kernel,
-        **more,
+        in_specs=[scalar if space == "S" else whole for space in spaces],
         out_shape=outs,
         scratch_shapes=list(scratch),
-        compiler_params=pltpu.CompilerParams(vmem_limit_bytes=56 * 2**20),
+        compiler_params=pltpu.CompilerParams(vmem_limit_bytes=limit * 2**20),
     )
+
+    def close(*operands):
+        held = [
+            pltpu.with_memory_space_constraint(x, where[space]) if space in where else x
+            for space, x in zip(spaces, operands, strict=True)
+        ]
+        return run(*held)
+
+    return close
 
 
 def struct(shape, dtype=BF):
     return jax.ShapeDtypeStruct(shape, dtype)
+
+
+def far_struct(shape, dtype=BF):
+    return pltpu.HBM(shape, dtype)
 
 
 def move(array, lat_step, lon_step):
@@ -369,7 +384,7 @@
 
 def sum_over_all(keep, send):
     rows, width = keep.shape
-    mine = (keep.astype(F32) + swap(send).astype(F32)).astype(BF)
+    mine = call(add_kernel, struct((rows, width)), "VV", limit=8)(keep, swap(send))
     chips = lax.axis_size(PLANE)
     mine = add_up(lax.all_to_all(mine.reshape(chips, rows // chips, width), PLANE, 0, 0, tiled=True))
     mine = add_up(lax.all_to_all(copies(mine, "z"), "z", 0, 0, tiled=True))
@@ -378,12 +393,12 @@
 
 
 def per_device(latents, mask_ids, w_qkv, w_out, w_kv, level_queries, w_o, w_head, field_cotangent):
-    perm = jnp.asarray(pack_matrix(), BF)
+    perm = pack_matrix()
     columns, rows, extra = label_tables()
     flag = (lax.axis_index(LAT) == lax.axis_size(LAT) - 1).astype(jnp.int32).reshape(1, 1)
-    shapes = [struct((MAIN, D)), struct((MAIN, D)), struct((SIDE, D)), struct((SIDE, D))]
-    main, north, west, corner = call(pack_kernel, shapes)(
-        latents.reshape(TOKENS, D), mask_ids, perm, jnp.asarray(columns, BF), jnp.asarray(rows)
+    shapes = [far_struct((MAIN, D)), struct((MAIN, D)), struct((SIDE, D)), struct((SIDE, D))]
+    main, north, west, corner = call(pack_kernel, shapes, "HHHHH", limit=56)(
+        latents.reshape(TOKENS, D), mask_ids, jnp.asarray(perm, BF), jnp.asarray(columns, BF), jnp.asarray(rows)
     )
     north, west, corner = move(north, -1, 0), move(west, 0, -1), move(corner, -1, -1)
     head = jnp.pad(w_head.T, ((0, LANES - OUTS), (0, 0)))
@@ -396,19 +411,22 @@
             struct((D, LANES)),
             struct((16, LANES), F32),
         ],
+        "VVVV",
     )(field_cotangent.reshape(PATCHES, PLEV * OUTS), level_queries, w_o, head)
     main, north, west, corner = call(
         attention_kernel,
         shapes,
+        "SHHHHHVV",
         [pltpu.VMEM((PACKED, 3 * D), F32), pltpu.VMEM((PACKED, D), F32)],
-        smem=7,
-    )(flag, main, north, west, corner, jnp.asarray(extra), w_qkv, w_out)
+        limit=48,
+    )(flag, jnp.asarray(extra), main, north, west, corner, w_qkv, w_out)
     north, west, corner = move(north, 1, 0), move(west, 0, 1), move(corner, 1, 1)
     core = lax.axis_index("core").astype(jnp.int32).reshape(1, 1)
     share = struct((ROWS // 2, D))
     owned, fields, keep, send = call(
         decode_kernel,
         [struct((TOKENS, D)), struct((PATCHES, PLEV * OUTS)), share, share],
+        "SHVVVHVVVVVVV",
         [
             pltpu.VMEM((TOKENS, D), F32),
             pltpu.VMEM((TOKENS, LANES), F32),
@@ -418,13 +436,12 @@
             pltpu.VMEM((PATCHES, PLEV * OUTS), F32),
             pltpu.VMEM((ROWS, D), F32),
         ],
-        smem=12,
-    )(core, main, north, west, corner, perm, w_kv, level_queries, up, dctx, dsum, both, base)
+    )(core, main, north, west, corner, jnp.asarray(perm.T, BF), w_kv, level_queries, up, dctx, dsum, both, base)
     mine, other = sum_over_all(keep, send)
     kv, query, out, pixels = call(
         final_kernel,
         [struct((D, 2 * D), F32), struct((PLEV, D), F32), struct((D, D), F32), struct((OUTS, D), F32)],
-        smem=6,
+        "SVVVVVV",
     )(core, mine, other, w_kv, level_queries, w_o, head)
     shape = latents.shape
     return (owned.reshape(shape), fields.reshape(shape[1], shape[2], PLEV * OUTS), kv, query, out, pixels.T)

time: 107 us -> 102 us (0.953)
  Pallas kernels: 32 us -> 25.6 us
  waiting for transfers between devices: 12.6 us -> 14.7 us
  other arithmetic: 1.19 us -> 0.09 us
    pallas_call x5 -> x6, Pallas kernels: 32 us -> 25.6 us  [close(): return run(*held)]
    ppermute x6, waiting for transfers between devices: 9.73 us -> 12 us  [move(): return lax.ppermute(array, LAT + LON, route)]
    convert_element_type x1 -> x0, other arithmetic: 1.09 us -> none  [sum_over_all(): mine = (keep.astype(F32) + swap(send).astype(F32)).astype(BF)]
  transfers between devices with their start and end apart: 8 -> 8, of which waited for: 4 -> 4; matrix products, arithmetic and copies ran while one was open for 1% -> 1% of each run, Pallas kernels for 5% -> 3%
where the time goes in v4:
time: 102 us; the launch traced here: 101 us
  blocking collectives  36.3 us (36%)
  Pallas kernels  25.6 us (25%)
  starting transfers between devices  21.1 us (21%)
  waiting for transfers between devices  14.7 us (14%)
  local copies, waits for them, and re-layouts  2.71 us (3%)
    pallas_call x6, Pallas kernels, close(): return run(*held)  25.6 us
    ppermute x6, starting transfers between devices, move(): return lax.ppermute(array, LAT + LON, route)  15.4 us
    all_to_all x1, blocking collectives, sum_over_all(): mine = add_up(lax.all_to_all(copies(mine, 'z'), 'z', 0, 0, tiled=True))  12.9 us
    ppermute x6, waiting for transfers between devices, move(): return lax.ppermute(array, LAT + LON, route)  12 us
    all_to_all x1, blocking collectives, sum_over_all(): lax.all_to_all(mine.reshape(chips, rows // chips, width), PLANE, 0, 0, ti...  11.9 us
    all_to_all x1, blocking collectives, sum_over_all(): lax.all_to_all(copies(mine, PLANE), PLANE, 0, 0, tiled=True)  11.4 us
    ppermute x2, starting transfers between devices, swap(): lax.ppermute(array, 'core', [(i, (i + 1) % count) for i in range(count)])  5.7 us
    ppermute x2, waiting for transfers between devices, swap(): lax.ppermute(array, 'core', [(i, (i + 1) % count) for i in range(count)])  2.7 us
  transfers between devices with their start and end apart: 8, of which 4 were waited for; matrix products, arithmetic and copies ran while one was open for 1% of the time, Pallas kernels for 3%

profile of v4, /device:TPU:1, one launch (start us, length us, event | category | flops | bytes accessed | tf_op | source)
XLA Modules:
  0.0 101.2 jit_solution(12599596476341464813)
XLA Ops:
  0.6 0.0 copy-start.2
  0.7 3.0 %shard_map.181 = (bf16[224,512]{1,0:T(8,128)(2,1)}, bf16[224,512]{1,0:T(8,128)(2,1)}, bf16[80,512]{1,0:T(8,128)(2,1)}, bf16[80,512]{1,0:T(8,128)(2,1)}) custom-call(bf16[576,512]{1,0:T(8,128)(2,1)} %bitcast.14, s32[6,24]{1,0:T(8,128)} %ids_ref.1, bf16[608,576]{1,0:T(8,128)(2,1)} %constant.34.clone.perm_ref, bf16[24,3072]{1,0:T(8,128)(2,1)} %constant.35.clone.columns_ref, ...), custom_call_target="tpu_custom_call" | custom-call | tf_op jit(solution)/shard_map/pallas_call | solution.py:349
  3.6 8.9 %collective-permute-start = (bf16[224,512]{1,0:T(8,128)(2,1)}, bf16[224,512]{1,0:T(8,128)(2,1)S(1)}, u32[]{:S(2)}, u32[]{:S(2)}) collective-permute-start(bf16[224,512]{1,0:T(8,128)(2,1)} %get-tuple-element.28), channel_id=1, source_target_pairs={{0,240},{1,241},{2,242},{3,243},{4,244},{5,245},{6,246},{7,247},{8... | collective-permute-start | bytes 688136 | tf_op jit(solution)/shard_map/ppermute | solution.py:369
  12.5 1.0 collective-permute-start.1
  13.4 3.8 %collective-permute-start.2 = (bf16[80,512]{1,0:T(8,128)(2,1)}, bf16[80,512]{1,0:T(8,128)(2,1)S(1)}, u32[]{:S(2)}, u32[]{:S(2)}) collective-permute-start(bf16[80,512]{1,0:T(8,128)(2,1)} %get-tuple-element.30), channel_id=1, source_target_pairs={{0,255},{1,240},{2,241},{3,242},{4,243},{5,244},{6,245},{7,246},{8... | collective-permute-start | bytes 245768 | tf_op jit(solution)/shard_map/ppermute | solution.py:369
  17.3 0.0 collective-permute-done.1.west_ref
  17.3 3.0 %collective-permute-done.2.corner_ref = bf16[80,512]{1,0:T(8,128)(2,1)S(1)} collective-permute-done((bf16[80,512]{1,0:T(8,128)(2,1)}, bf16[80,512]{1,0:T(8,128)(2,1)S(1)}, u32[]{:S(2)}, u32[]{:S(2)}) %collective-permute-start.2) | collective-permute-done | bytes 81952 | tf_op jit(solution)/shard_map/ppermute | solution.py:369
  20.2 0.0 collective-permute-done.north_ref
  20.2 0.0 copy-done.7
  20.2 0.6 copy-done.8
  20.8 0.1 copy-done.6
  20.9 1.0 %copy-done.3 = bf16[512,512]{1,0:T(8,128)(2,1)S(1)} copy-done((bf16[512,512]{1,0:T(8,128)(2,1)S(1)}, bf16[512,512]{1,0:T(8,128)(2,1)}, u32[]{:S(2)}) %copy-start.3) | copy-done | bytes 524312
  22.0 5.6 %shard_map.182 = (bf16[224,512]{1,0:T(8,128)(2,1)}, bf16[224,512]{1,0:T(8,128)(2,1)}, bf16[80,512]{1,0:T(8,128)(2,1)}, bf16[80,512]{1,0:T(8,128)(2,1)}) custom-call(s32[1,1]{1,0:T(1,128)} %bitcast.1.flag_ref, f32[8,256]{1,0:T(8,128)} %constant.37.clone.extra_ref, bf16[224,512]{1,0:T(8,128)(2,1)} %get-tuple-element.27.main_ref, bf16[224,512]{1,0:T(8,128)(2,1)} %copy-done.6, ...), custom_call_target="tpu_custom_call" | custom-call | tf_op jit(solution)/shard_map/pallas_call | solution.py:349
  27.6 0.1 collective-permute-start.3
  27.7 1.3 %collective-permute-start.4 = (bf16[80,512]{1,0:T(8,128)(2,1)}, bf16[80,512]{1,0:T(8,128)(2,1)S(1)}, u32[]{:S(2)}, u32[]{:S(2)}) collective-permute-start(bf16[80,512]{1,0:T(8,128)(2,1)} %get-tuple-element.33), channel_id=1, source_target_pairs={{0,1},{1,2},{2,3},{3,4},{4,5},{5,6},{6,7},{7,8},{8,9},{9,10},{10,1... | collective-permute-start | bytes 245768 | tf_op jit(solution)/shard_map/ppermute | solution.py:369
  28.9 0.4 collective-permute-start.5
  29.4 0.9 pad.4.whead_ref
  30.3 2.6 %shard_map.183 = (bf16[13,144,128]{2,1,0:T(8,128)(2,1)S(1)}, bf16[13,144,512]{2,1,0:T(8,128)(2,1)S(1)}, f32[144,512]{1,0:T(8,128)S(1)}, bf16[512,128]{1,0:T(8,128)(2,1)S(1)}, f32[16,128]{1,0:T(8,128)S(1)}) custom-call(bf16[144,1040]{1,0:T(8,128)(2,1)S(1)} %bitcast.13, bf16[13,512]{1,0:T(8,128)(2,1)S(1)} %copy-done.5, bf16[512,512]{1,0:T(8,128)(2,1)S(1)} %copy-done.1, ...), custom_call_target="tpu_custom_call" | custom-call | tf_op jit(solution)/shard_map/pallas_call | solution.py:349
  32.9 0.0 collective-permute-done.4.west_ref
  32.9 9.0 %collective-permute-done.5.corner_ref = bf16[80,512]{1,0:T(8,128)(2,1)S(1)} collective-permute-done((bf16[80,512]{1,0:T(8,128)(2,1)}, bf16[80,512]{1,0:T(8,128)(2,1)S(1)}, u32[]{:S(2)}, u32[]{:S(2)}) %collective-permute-start.5) | collective-permute-done | bytes 81952 | tf_op jit(solution)/shard_map/ppermute | solution.py:369
  41.9 0.0 collective-permute-done.3.north_ref
  41.9 11.6 %shard_map.184 = (bf16[576,512]{1,0:T(8,128)(2,1)}, bf16[144,1040]{1,0:T(8,128)(2,1)}, bf16[384,512]{1,0:T(8,128)(2,1)S(1)}, bf16[384,512]{1,0:T(8,128)(2,1)S(1)}) custom-call(s32[1,1]{1,0:T(1,128)} %bitcast.flag_ref, bf16[224,512]{1,0:T(8,128)(2,1)} %get-tuple-element.31.main_ref, bf16[224,512]{1,0:T(8,128)(2,1)S(1)} %collective-permute-done.3.north_ref, ...), custom_call_target="tpu_custom_call" | custom-call | tf_op jit(solution)/shard_map/pallas_call | solution.py:349
  53.5 1.4 %collective-permute-start.6 = (bf16[384,512]{1,0:T(8,128)(2,1)S(1)}, bf16[384,512]{1,0:T(8,128)(2,1)S(1)}, u32[]{:S(2)}, u32[]{:S(2)}) collective-permute-start(bf16[384,512]{1,0:T(8,128)(2,1)S(1)} %get-tuple-element.43), channel_id=1, source_target_pairs={{0,1},{1,0},{2,3},{3,2},{4,5},{5,4},{6,7},{7,6},{8,9},{9,8},{10,11... | collective-permute-start | bytes 1179656 | tf_op jit(solution)/shard_map/ppermute | solution.py:374
  54.9 1.3 %collective-permute-done.6.right_ref = bf16[384,512]{1,0:T(8,128)(2,1)S(1)} collective-permute-done((bf16[384,512]{1,0:T(8,128)(2,1)S(1)}, bf16[384,512]{1,0:T(8,128)(2,1)S(1)}, u32[]{:S(2)}, u32[]{:S(2)}) %collective-permute-start.6) | collective-permute-done | bytes 393248 | tf_op jit(solution)/shard_map/ppermute | solution.py:374
  56.3 0.1 shard_map.185
  56.4 11.9 %all_to_all.15 = bf16[16,24,512]{2,1,0:T(8,128)(2,1)S(1)} all-to-all(bf16[16,24,512]{2,1,0:T(8,128)(2,1)S(1)} %bitcast.10), channel_id=1, replica_groups=mesh['z'=8,'x_hi'=2,'x_lo'=2,'y'=4,'core'=2] {'x_hi','x_lo','y'}, dimensions={0} | all-to-all | bytes 786432 | tf_op jit(solution)/shard_map/all_to_all | solution.py:389
  68.3 0.1 reduce_sum.24
  68.4 12.9 %all_to_all.16 = bf16[8,24,512]{2,1,0:T(8,128)(2,1)S(1)} all-to-all(bf16[8,24,512]{2,1,0:T(8,128)(2,1)S(1)} %broadcast_in_dim.4), channel_id=1, replica_groups=mesh['z'=8,'x_hi'=2,'x_lo'=2,'y'=4,'core'=2] {'z'}, dimensions={0} | all-to-all | bytes 393216 | tf_op jit(solution)/shard_map/all_to_all | solution.py:390
  81.4 11.4 %all_to_all.17 = bf16[16,24,512]{2,1,0:T(8,128)(2,1)S(1)} all-to-all(bf16[16,24,512]{2,1,0:T(8,128)(2,1)S(1)} %broadcast_in_dim.5), channel_id=1, replica_groups=mesh['z'=8,'x_hi'=2,'x_lo'=2,'y'=4,'core'=2] {'x_hi','x_lo','y'}, dimensions={0} | all-to-all | bytes 786432 | tf_op jit(solution)/shard_map/all_to_all | solution.py:391
  92.8 4.3 %collective-permute-start.7 = (bf16[384,512]{1,0:T(8,128)(2,1)S(1)}, bf16[384,512]{1,0:T(8,128)(2,1)S(1)}, u32[]{:S(2)}, u32[]{:S(2)}) collective-permute-start(bf16[384,512]{1,0:T(8,128)(2,1)S(1)} %bitcast.11), channel_id=1, source_target_pairs={{0,1},{1,0},{2,3},{3,2},{4,5},{5,4},{6,7},{7,6},{8,9},{9,8},{10,11... | collective-permute-start | bytes 1179656 | tf_op jit(solution)/shard_map/ppermute | solution.py:374
  97.1 1.3 %collective-permute-done.7.other_ref = bf16[384,512]{1,0:T(8,128)(2,1)S(1)} collective-permute-done((bf16[384,512]{1,0:T(8,128)(2,1)S(1)}, bf16[384,512]{1,0:T(8,128)(2,1)S(1)}, u32[]{:S(2)}, u32[]{:S(2)}) %collective-permute-start.7) | collective-permute-done | bytes 393248 | tf_op jit(solution)/shard_map/ppermute | solution.py:374
  98.4 2.8 %shard_map.186 = (f32[512,1024]{1,0:T(8,128)}, f32[13,512]{1,0:T(8,128)}, f32[512,512]{1,0:T(8,128)}, f32[80,512]{1,0:T(8,128)}) custom-call(s32[1,1]{1,0:T(1,128)} %bitcast.flag_ref, bf16[384,512]{1,0:T(8,128)(2,1)S(1)} %bitcast.12, bf16[384,512]{1,0:T(8,128)(2,1)S(1)} %collective-permute-done.7.other_ref, bf16[512,1024]{1,0:T(8,128)(2,1)S(1)} %copy-done, ...), custom_call_target="tpu_custom_call" | custom-call | tf_op jit(solution)/shard_map/pallas_call | solution.py:349
  (16 shorter events, 0.1 us)
Async XLA Ops:
  0.6 20.3 %copy-start.2 = (bf16[512,1536]{1,0:T(8,128)(2,1)S(1)}, bf16[512,1536]{1,0:T(8,128)(2,1)}, u32[]{:S(2)}) copy-start(bf16[512,1536]{1,0:T(8,128)(2,1)} %wqkv_ref.1) | copy-start | bytes 4718596
  0.6 29.6 %copy-start.1 = (bf16[512,512]{1,0:T(8,128)(2,1)S(1)}, bf16[512,512]{1,0:T(8,128)(2,1)}, u32[]{:S(2)}) copy-start(bf16[512,512]{1,0:T(8,128)(2,1)} %wo_ref.3) | copy-start | bytes 1572868
  3.6 16.6 %collective-permute-start = (bf16[224,512]{1,0:T(8,128)(2,1)}, bf16[224,512]{1,0:T(8,128)(2,1)S(1)}, u32[]{:S(2)}, u32[]{:S(2)}) collective-permute-start(bf16[224,512]{1,0:T(8,128)(2,1)} %get-tuple-element.28), channel_id=1, source_target_pairs={{0,240},{1,241},{2,242},{3,243},{4,244},{5,245},{6,246},{7,247},{8... | collective-permute-start | bytes 688136 | tf_op jit(solution)/shard_map/ppermute | solution.py:369
  12.5 4.8 %collective-permute-start.1 = (bf16[80,512]{1,0:T(8,128)(2,1)}, bf16[80,512]{1,0:T(8,128)(2,1)S(1)}, u32[]{:S(2)}, u32[]{:S(2)}) collective-permute-start(bf16[80,512]{1,0:T(8,128)(2,1)} %get-tuple-element.29), channel_id=1, source_target_pairs={{0,15},{1,0},{2,1},{3,2},{4,3},{5,4},{6,5},{7,6},{8,7},{9,8},{10,9... | collective-permute-start | bytes 245768 | tf_op jit(solution)/shard_map/ppermute | solution.py:369
  13.4 6.8 %collective-permute-start.2 = (bf16[80,512]{1,0:T(8,128)(2,1)}, bf16[80,512]{1,0:T(8,128)(2,1)S(1)}, u32[]{:S(2)}, u32[]{:S(2)}) collective-permute-start(bf16[80,512]{1,0:T(8,128)(2,1)} %get-tuple-element.30), channel_id=1, source_target_pairs={{0,255},{1,240},{2,241},{3,242},{4,243},{5,244},{6,245},{7,246},{8... | collective-permute-start | bytes 245768 | tf_op jit(solution)/shard_map/ppermute | solution.py:369
  17.3 3.0 %copy-start.7 = (bf16[80,512]{1,0:T(8,128)(2,1)}, bf16[80,512]{1,0:T(8,128)(2,1)S(1)}, u32[]{:S(2)}) copy-start(bf16[80,512]{1,0:T(8,128)(2,1)S(1)} %collective-permute-done.1.west_ref) | copy-start | bytes 245764
  20.2 0.6 copy-start.8
  20.2 0.7 copy-start.6
  20.9 1.0 %copy-start.3 = (bf16[512,512]{1,0:T(8,128)(2,1)S(1)}, bf16[512,512]{1,0:T(8,128)(2,1)}, u32[]{:S(2)}) copy-start(bf16[512,512]{1,0:T(8,128)(2,1)} %wout_ref.1) | copy-start | bytes 1572868
  22.0 8.3 %copy-start.4 = (bf16[6,24,1040]{2,1,0:T(8,128)(2,1)S(1)}, bf16[6,24,1040]{2,1,0:T(8,128)(2,1)}, u32[]{:S(2)}) copy-start(bf16[6,24,1040]{2,1,0:T(8,128)(2,1)} %param.22) | copy-start | bytes 898564
  22.0 8.3 %copy-start.5 = (bf16[13,512]{1,0:T(8,128)(2,1)S(1)}, bf16[13,512]{1,0:T(8,128)(2,1)}, u32[]{:S(2)}) copy-start(bf16[13,512]{1,0:T(8,128)(2,1)} %queries_ref.5) | copy-start | bytes 39940
  22.0 19.9 %copy-start = (bf16[512,1024]{1,0:T(8,128)(2,1)S(1)}, bf16[512,1024]{1,0:T(8,128)(2,1)}, u32[]{:S(2)}) copy-start(bf16[512,1024]{1,0:T(8,128)(2,1)} %wkv_ref.3) | copy-start | bytes 3145732
  27.6 14.3 %collective-permute-start.3 = (bf16[224,512]{1,0:T(8,128)(2,1)}, bf16[224,512]{1,0:T(8,128)(2,1)S(1)}, u32[]{:S(2)}, u32[]{:S(2)}) collective-permute-start(bf16[224,512]{1,0:T(8,128)(2,1)} %get-tuple-element.32), channel_id=1, source_target_pairs={{0,16},{1,17},{2,18},{3,19},{4,20},{5,21},{6,22},{7,23},{8,24},{9,... | collective-permute-start | bytes 688136 | tf_op jit(solution)/shard_map/ppermute | solution.py:369
  27.7 5.2 %collective-permute-start.4 = (bf16[80,512]{1,0:T(8,128)(2,1)}, bf16[80,512]{1,0:T(8,128)(2,1)S(1)}, u32[]{:S(2)}, u32[]{:S(2)}) collective-permute-start(bf16[80,512]{1,0:T(8,128)(2,1)} %get-tuple-element.33), channel_id=1, source_target_pairs={{0,1},{1,2},{2,3},{3,4},{4,5},{5,6},{6,7},{7,8},{8,9},{9,10},{10,1... | collective-permute-start | bytes 245768 | tf_op jit(solution)/shard_map/ppermute | solution.py:369
  28.9 13.0 %collective-permute-start.5 = (bf16[80,512]{1,0:T(8,128)(2,1)}, bf16[80,512]{1,0:T(8,128)(2,1)S(1)}, u32[]{:S(2)}, u32[]{:S(2)}) collective-permute-start(bf16[80,512]{1,0:T(8,128)(2,1)} %get-tuple-element.34), channel_id=1, source_target_pairs={{0,17},{1,18},{2,19},{3,20},{4,21},{5,22},{6,23},{7,24},{8,25},{9,... | collective-permute-start | bytes 245768 | tf_op jit(solution)/shard_map/ppermute | solution.py:369
  53.5 2.8 %collective-permute-start.6 = (bf16[384,512]{1,0:T(8,128)(2,1)S(1)}, bf16[384,512]{1,0:T(8,128)(2,1)S(1)}, u32[]{:S(2)}, u32[]{:S(2)}) collective-permute-start(bf16[384,512]{1,0:T(8,128)(2,1)S(1)} %get-tuple-element.43), channel_id=1, source_target_pairs={{0,1},{1,0},{2,3},{3,2},{4,5},{5,4},{6,7},{7,6},{8,9},{9,8},{10,11... | collective-permute-start | bytes 1179656 | tf_op jit(solution)/shard_map/ppermute | solution.py:374
  92.8 5.6 %collective-permute-start.7 = (bf16[384,512]{1,0:T(8,128)(2,1)S(1)}, bf16[384,512]{1,0:T(8,128)(2,1)S(1)}, u32[]{:S(2)}, u32[]{:S(2)}) collective-permute-start(bf16[384,512]{1,0:T(8,128)(2,1)S(1)} %bitcast.11), channel_id=1, source_target_pairs={{0,1},{1,0},{2,3},{3,2},{4,5},{5,4},{6,7},{7,6},{8,9},{9,8},{10,11... | collective-permute-start | bytes 1179656 | tf_op jit(solution)/shard_map/ppermute | solution.py:374

commit v5 on v4

--- a/solution.py
+++ b/solution.py
@@ -1,3 +1,4 @@
+import functools
 import math
 
 import jax
@@ -102,15 +103,16 @@
     return (center * lax.rsqrt(spread + norm_eps)).astype(BF)
 
 
-def pack_kernel(x_ref, ids_ref, perm_ref, columns_ref, rows_ref, main_ref, north_ref, west_ref, corner_ref):
+def pack_kernel(pieces, x_ref, ids_ref, perm_ref, columns_ref, rows_ref, *piece_refs):
     ids = ids_ref[...].astype(F32).astype(BF)
     lines = jnp.sum(mm(ids, columns_ref[...]) * rows_ref[:WH], axis=0, keepdims=True)
     x = x_ref[...]
     segment = 0
-    for ref, windows in zip((main_ref, north_ref, west_ref, corner_ref), PIECES):
+    first = 0
+    for ref, windows in zip(piece_refs, pieces, strict=True):
         height = ref.shape[0]
-        first = min(at for at, _, _ in windows.values())
         packed = mm(perm_ref[first : first + height], x)
+        first += height
         bottom = [jnp.zeros((12, SPAN), F32)]
         for window in range(4):
             if window in windows:
@@ -176,13 +178,6 @@
     corner_out[...] = mixed[c:]
 
 
-def expand_matrices():
-    c = lax.broadcasted_iota(jnp.int32, (LANES, D), 0)
-    j = lax.broadcasted_iota(jnp.int32, (LANES, D), 1)
-    gap = c - j // (D // HEADS)
-    return [jnp.where(gap == level * HEADS, 1.0, 0.0).astype(BF) for level in range(PLEV)]
-
-
 def shift_matrix(offset, width):
     i = lax.broadcasted_iota(jnp.int32, (width, LANES), 0)
     j = lax.broadcasted_iota(jnp.int32, (width, LANES), 1)
@@ -203,9 +198,24 @@
     return jnp.where(c % HEADS == j // (D // HEADS), tall, 0.0)
 
 
-def pre_kernel(cot_ref, queries_ref, wo_ref, whead_ref, up_ref, dctx_ref, dsum_ref, map_ref, base_ref):
+def feature_order():
+    j = lax.broadcasted_iota(jnp.int32, (D, D), 0)
+    lane = lax.broadcasted_iota(jnp.int32, (D, D), 1)
+    size = D // HEADS
+    wanted = j % size // 16 * LANES + j // size * 16 + j % 16
+    return jnp.where(wanted == lane, 1.0, 0.0).astype(BF)
+
+
+def pre_kernel(
+    cot_ref, queries_ref, wo_ref, whead_ref, wkv_ref,
+    up_ref, dctx_ref, dsum_ref, map_ref, base_ref, wv_ref, order_ref,
+):
+    order = feature_order()
+    order_ref[...] = order
+    wv_ref[...] = mm(wkv_ref[:, D:], order).astype(BF)
     head = whead_ref[...]
     both = dot(wo_ref[...], head, ((1,), (1,))).astype(BF)
+    both = dot(order, both, ((0,), (0,))).astype(BF)
     map_ref[...] = both
     base_ref[...] = jnp.concatenate(
         [dot(queries_ref[...], head, ((1,), (1,))), jnp.zeros((16 - PLEV, LANES), F32)], axis=0
@@ -223,7 +233,7 @@
 
 def decode_kernel(
     flag_ref, main_ref, north_ref, west_ref, corner_ref, perm_ref, wkv_ref, queries_ref, up_ref, dctx_ref, dsum_ref,
-    map_ref, base_ref,
+    map_ref, base_ref, wv_ref,
     owned_ref, fields_ref, keep_ref, send_ref,
     value, weights, dvalues, context, products, fields, sums,
 ):
@@ -233,7 +243,7 @@
     owned_ref[...] = wide.astype(BF)
     normed = layer_norm(wide)
     key = mm(normed, wkv_ref[:, :D]).astype(BF)
-    value[...] = mm(normed, wkv_ref[:, D:]).astype(BF).astype(F32)
+    value[...] = mm(normed, wv_ref[...]).astype(BF).astype(F32)
     queries = spread_queries(queries_ref[...].astype(F32)).astype(BF)
     scores = dot(key, queries, ((1,), (1,))) * 0.125
     slabs = [scores[l * PATCHES : (l + 1) * PATCHES] for l in range(LEV)]
@@ -243,33 +253,36 @@
     slabs = [s * scale for s in slabs]
     for l in range(LEV):
         weights[l * PATCHES : (l + 1) * PATCHES] = slabs[l]
-    half = lax.broadcasted_iota(jnp.int32, (BLOCK, LANES), 1) // (D // HEADS)
-    for tile in range(D // LANES):
-        lanes = slice(tile * LANES, (tile + 1) * LANES)
-        for start in range(0, PATCHES, BLOCK):
-            at = [slice(l * PATCHES + start, l * PATCHES + start + BLOCK) for l in range(LEV)]
-            last = value[at[LEV - 1], lanes]
-            gaps = [value[at[l], lanes] - last for l in range(LEV - 1)]
-            heads = [weights[at[l]] for l in range(LEV - 1)]
-            found = [jnp.zeros((BLOCK, LANES), F32) for _ in range(LEV - 1)]
-            for level in range(PLEV):
-                index = half + (level * HEADS + 2 * tile)
-                upstream = dctx_ref[level, start : start + BLOCK, lanes].astype(F32)
-                total = last
-                for l in range(LEV - 1):
-                    spread = jnp.take_along_axis(heads[l], index, axis=1)
-                    total = total + spread * gaps[l]
-                    found[l] = found[l] + spread * upstream
-                    products[level, at[l], lanes] = (upstream * gaps[l]).astype(BF)
-                context[level * PATCHES + start : level * PATCHES + start + BLOCK, lanes] = total.astype(BF)
+    head_of = lax.broadcasted_iota(jnp.int32, (BLOCK, LANES), 1) // 16
+    for start in range(0, PATCHES, BLOCK):
+        at = [slice(l * PATCHES + start, l * PATCHES + start + BLOCK) for l in range(LEV)]
+        last = value[at[LEV - 1]]
+        gaps = [value[at[l]] - last for l in range(LEV - 1)]
+        heads = [weights[at[l]] for l in range(LEV - 1)]
+        found = [jnp.zeros((BLOCK, D), F32) for _ in range(LEV - 1)]
+        for level in range(PLEV):
+            index = head_of + level * HEADS
+            upstream = dctx_ref[level, start : start + BLOCK].astype(F32)
+            total = last
             for l in range(LEV - 1):
-                dvalues[at[l], lanes] = found[l]
-            dvalues[at[LEV - 1], lanes] = dsum_ref[start : start + BLOCK, lanes] - (found[0] + found[1] + found[2])
+                spread = jnp.take_along_axis(heads[l], index, axis=1)
+                spread = jnp.concatenate([spread] * (D // LANES), axis=1)
+                total = total + spread * gaps[l]
+                found[l] = found[l] + spread * upstream
+                product = upstream * gaps[l]
+                folded = (product[:, :LANES] + product[:, LANES : 2 * LANES]) + (
+                    product[:, 2 * LANES : 3 * LANES] + product[:, 3 * LANES :]
+                )
+                products[at[l], level * LANES : (level + 1) * LANES] = folded.astype(BF)
+            context[level * PATCHES + start : level * PATCHES + start + BLOCK] = total.astype(BF)
+        for l in range(LEV - 1):
+            dvalues[at[l]] = found[l]
+        dvalues[at[LEV - 1]] = dsum_ref[start : start + BLOCK] - (found[0] + found[1] + found[2])
     fields[...] = jnp.zeros_like(fields)
-    slopes = jnp.zeros(((LEV - 1) * PATCHES, LANES), F32)
-    expand = expand_matrices()
+    row = lax.broadcasted_iota(jnp.int32, (PLEV * LANES, LANES), 0)
+    c = lax.broadcasted_iota(jnp.int32, (PLEV * LANES, LANES), 1)
+    slopes = mm(products[...], jnp.where(row // 16 == c, 1.0, 0.0).astype(BF))
     for level in range(PLEV):
-        slopes = slopes + dot(products[level], expand[level], ((1,), (1,)))
         first, offset, width = spot(level)
         decoded = mm(context[level * PATCHES : (level + 1) * PATCHES], map_ref[...]) + base_ref[level : level + 1]
         fields[:, first : first + width] += dot(decoded.astype(BF), shift_matrix(offset, width), ((1,), (1,)))
@@ -298,7 +311,7 @@
     out_ref[...] = (left_ref[...].astype(F32) + right_ref[...].astype(F32)).astype(BF)
 
 
-def final_kernel(flag_ref, mine_ref, other_ref, wkv_ref, queries_ref, wo_ref, whead_ref, kv_ref, query_ref, o_ref, head_ref):
+def final_kernel(flag_ref, mine_ref, other_ref, order_ref, wkv_ref, queries_ref, wo_ref, whead_ref, kv_ref, query_ref, o_ref, head_ref):
     second = flag_ref[0, 0] > 0
     mine, other = mine_ref[...].astype(F32), other_ref[...].astype(F32)
     sums = jnp.concatenate([jnp.where(second, other, mine), jnp.where(second, mine, other)], axis=0).astype(BF)
@@ -308,14 +321,14 @@
     outer = sums[D + LANES :]
     level_sums = outer[OUTS : OUTS + 16, :LANES]
     spread = spread_queries(queries.astype(F32)).astype(BF)
-    values = sums[:D].astype(F32)
+    values = dot(sums[:D], order_ref[...], ((1,), (1,)))
     keys = dot(keyed, spread, ((0,), (0,)))
     c = lax.broadcasted_iota(jnp.int32, (LANES, D), 0)
     j = lax.broadcasted_iota(jnp.int32, (LANES, D), 1)
     grouped = jnp.where(c % HEADS == j // (D // HEADS), mm(keyed, wkv_ref[:, :D]), 0.0)
     grouped = jnp.sum(grouped.reshape(LANES // HEADS, HEADS, D), axis=1)
     level = grouped[:PLEV] + mm(level_sums, head)[:PLEV]
-    clean = outer[:OUTS]
+    clean = dot(outer[:OUTS], order_ref[...], ((1,), (1,))).astype(BF)
     out = dot(clean, head[:OUTS], ((0,), (0,)))
     pixels = mm(clean, wo_ref[...])
     pixels = pixels + dot(level_sums[:PLEV, :OUTS], queries, ((0,), (0,)))
@@ -387,7 +400,7 @@
     mine = call(add_kernel, struct((rows, width)), "VV", limit=8)(keep, swap(send))
     chips = lax.axis_size(PLANE)
     mine = add_up(lax.all_to_all(mine.reshape(chips, rows // chips, width), PLANE, 0, 0, tiled=True))
-    mine = add_up(lax.all_to_all(copies(mine, "z"), "z", 0, 0, tiled=True))
+    mine = lax.psum(mine, "z")
     mine = lax.all_to_all(copies(mine, PLANE), PLANE, 0, 0, tiled=True).reshape(rows, width)
     return mine, swap(mine)
 
@@ -397,12 +410,17 @@
     columns, rows, extra = label_tables()
     flag = (lax.axis_index(LAT) == lax.axis_size(LAT) - 1).astype(jnp.int32).reshape(1, 1)
     shapes = [far_struct((MAIN, D)), struct((MAIN, D)), struct((SIDE, D)), struct((SIDE, D))]
-    main, north, west, corner = call(pack_kernel, shapes, "HHHHH", limit=56)(
-        latents.reshape(TOKENS, D), mask_ids, jnp.asarray(perm, BF), jnp.asarray(columns, BF), jnp.asarray(rows)
+    split = 4 * SPAN
+    flat = latents.reshape(TOKENS, D)
+    north, west, corner = call(functools.partial(pack_kernel, PIECES[1:]), shapes[1:], "HHHHH", limit=56)(
+        flat, mask_ids, jnp.asarray(perm[MAIN:], BF), jnp.asarray(columns[:, split:], BF), jnp.asarray(rows[:, split:])
+    )
+    (main,) = call(functools.partial(pack_kernel, PIECES[:1]), shapes[:1], "HHHHH", limit=56)(
+        flat, mask_ids, jnp.asarray(perm[:MAIN], BF), jnp.asarray(columns[:, :split], BF), jnp.asarray(rows[:, :split])
     )
     north, west, corner = move(north, -1, 0), move(west, 0, -1), move(corner, -1, -1)
     head = jnp.pad(w_head.T, ((0, LANES - OUTS), (0, 0)))
-    up, dctx, dsum, both, base = call(
+    up, dctx, dsum, both, base, wv, feature = call(
         pre_kernel,
         [
             struct((PLEV, PATCHES, LANES)),
@@ -410,13 +428,15 @@
             struct((PATCHES, D), F32),
             struct((D, LANES)),
             struct((16, LANES), F32),
+            struct((D, D)),
+            far_struct((D, D)),
         ],
-        "VVVV",
-    )(field_cotangent.reshape(PATCHES, PLEV * OUTS), level_queries, w_o, head)
+        "VVVVV",
+    )(field_cotangent.reshape(PATCHES, PLEV * OUTS), level_queries, w_o, head, w_kv)
     main, north, west, corner = call(
         attention_kernel,
         shapes,
-        "SHHHHHVV",
+        "SHHHHHVH",
         [pltpu.VMEM((PACKED, 3 * D), F32), pltpu.VMEM((PACKED, D), F32)],
         limit=48,
     )(flag, jnp.asarray(extra), main, north, west, corner, w_qkv, w_out)
@@ -426,23 +446,23 @@
     owned, fields, keep, send = call(
         decode_kernel,
         [struct((TOKENS, D)), struct((PATCHES, PLEV * OUTS)), share, share],
-        "SHVVVHVVVVVVV",
+        "SHVVVHVVVVVVVV",
         [
             pltpu.VMEM((TOKENS, D), F32),
             pltpu.VMEM((TOKENS, LANES), F32),
             pltpu.VMEM((TOKENS, D), F32),
             pltpu.VMEM((PLEV * PATCHES, D), BF),
-            pltpu.VMEM((PLEV, (LEV - 1) * PATCHES, D), BF),
+            pltpu.VMEM(((LEV - 1) * PATCHES, PLEV * LANES), BF),
             pltpu.VMEM((PATCHES, PLEV * OUTS), F32),
             pltpu.VMEM((ROWS, D), F32),
         ],
-    )(core, main, north, west, corner, jnp.asarray(perm.T, BF), w_kv, level_queries, up, dctx, dsum, both, base)
+    )(core, main, north, west, corner, jnp.asarray(perm.T, BF), w_kv, level_queries, up, dctx, dsum, both, base, wv)
     mine, other = sum_over_all(keep, send)
     kv, query, out, pixels = call(
         final_kernel,
         [struct((D, 2 * D), F32), struct((PLEV, D), F32), struct((D, D), F32), struct((OUTS, D), F32)],
-        "SVVVVVV",
-    )(core, mine, other, w_kv, level_queries, w_o, head)
+        "SVVHVVVV",
+    )(core, mine, other, feature, w_kv, level_queries, w_o, head)
     shape = latents.shape
     return (owned.reshape(shape), fields.reshape(shape[1], shape[2], PLEV * OUTS), kv, query, out, pixels.T)
 

time: 102 us -> 113 us (1.11)
  blocking collectives: 36.3 us -> 45.9 us
  starting transfers between devices: 21.1 us -> 26.9 us
  waiting for transfers between devices: 14.7 us -> 11.2 us
  local copies, waits for them, and re-layouts: 2.71 us -> 0.94 us
    psum x0 -> x1, blocking collectives: none -> 22.8 us  [sum_over_all(): mine = lax.psum(mine, 'z')]
    all_to_all x1 -> x0, blocking collectives: 12.9 us -> none  [sum_over_all(): mine = add_up(lax.all_to_all(copies(mine, 'z'), 'z', 0, 0, tiled=True))]
    ppermute x2, starting transfers between devices: 5.7 us -> 11.5 us  [swap(): lax.ppermute(array, 'core', [(i, (i + 1) % count) for i in range(count)])]
    ppermute x6, waiting for transfers between devices: 12 us -> 8.48 us  [move(): return lax.ppermute(array, LAT + LON, route)]
    unnamed x18 -> x10, local copies, waits for them, and re-layouts: 1.77 us -> 0.02 us
    pallas_call x6 -> x7, Pallas kernels: 25.6 us -> 26.7 us  [close(): return run(*held)]
  transfers between devices with their start and end apart: 8 -> 8, of which waited for: 4 -> 4; matrix products, arithmetic and copies ran while one was open for 1% -> 1% of each run, Pallas kernels for 3% -> 6%
where the time goes in v5:
time: 113 us; the launch traced here: 112 us
  blocking collectives  45.9 us (41%)
  starting transfers between devices  26.9 us (24%)
  Pallas kernels  26.7 us (24%)
  waiting for transfers between devices  11.2 us (10%)
    pallas_call x7, Pallas kernels, close(): return run(*held)  26.7 us
    psum x1, blocking collectives, sum_over_all(): mine = lax.psum(mine, 'z')  22.8 us
    ppermute x6, starting transfers between devices, move(): return lax.ppermute(array, LAT + LON, route)  15.4 us
    all_to_all x1, blocking collectives, sum_over_all(): lax.all_to_all(mine.reshape(chips, rows // chips, width), PLANE, 0, 0, ti...  11.9 us
    ppermute x2, starting transfers between devices, swap(): lax.ppermute(array, 'core', [(i, (i + 1) % count) for i in range(count)])  11.5 us
    all_to_all x1, blocking collectives, sum_over_all(): lax.all_to_all(copies(mine, PLANE), PLANE, 0, 0, tiled=True)  11.2 us
    ppermute x6, waiting for transfers between devices, move(): return lax.ppermute(array, LAT + LON, route)  8.48 us
    ppermute x2, waiting for transfers between devices, swap(): lax.ppermute(array, 'core', [(i, (i + 1) % count) for i in range(count)])  2.7 us
  transfers between devices with their start and end apart: 8, of which 4 were waited for; matrix products, arithmetic and copies ran while one was open for 1% of the time, Pallas kernels for 6%

profile of v5, /device:TPU:1, one launch (start us, length us, event | category | flops | bytes accessed | tf_op | source)
XLA Modules:
  0.0 112.4 jit_solution(10964122555834308260)
XLA Ops:
  0.6 0.0 copy-start.2
  0.6 2.6 %shard_map.209 = (bf16[224,512]{1,0:T(8,128)(2,1)}, bf16[80,512]{1,0:T(8,128)(2,1)}, bf16[80,512]{1,0:T(8,128)(2,1)}) custom-call(bf16[576,512]{1,0:T(8,128)(2,1)} %bitcast.14, s32[6,24]{1,0:T(8,128)} %ids_ref.3, bf16[384,576]{1,0:T(8,128)(2,1)} %constant.39.clone.perm_ref, bf16[24,2048]{1,0:T(8,128)(2,1)} %constant.40.clone.columns_ref, ...), custom_call_target="tpu_custom_call" | custom-call | tf_op jit(solution)/shard_map/pallas_call | solution.py:362
  3.2 8.9 %collective-permute-start = (bf16[224,512]{1,0:T(8,128)(2,1)}, bf16[224,512]{1,0:T(8,128)(2,1)}, u32[]{:S(2)}, u32[]{:S(2)}) collective-permute-start(bf16[224,512]{1,0:T(8,128)(2,1)} %get-tuple-element.28), channel_id=1, source_target_pairs={{0,240},{1,241},{2,242},{3,243},{4,244},{5,245},{6,246},{7,247},{8... | collective-permute-start | bytes 688136 | tf_op jit(solution)/shard_map/ppermute | solution.py:382
  12.1 1.0 collective-permute-start.1
  13.1 3.8 %collective-permute-start.2 = (bf16[80,512]{1,0:T(8,128)(2,1)}, bf16[80,512]{1,0:T(8,128)(2,1)}, u32[]{:S(2)}, u32[]{:S(2)}) collective-permute-start(bf16[80,512]{1,0:T(8,128)(2,1)} %get-tuple-element.30), channel_id=1, source_target_pairs={{0,255},{1,240},{2,241},{3,242},{4,243},{5,244},{6,245},{7,246},{8... | collective-permute-start | bytes 245768 | tf_op jit(solution)/shard_map/ppermute | solution.py:382
  16.9 2.4 %shard_map.208.main_ref = bf16[224,512]{1,0:T(8,128)(2,1)} custom-call(bf16[576,512]{1,0:T(8,128)(2,1)} %bitcast.15, s32[6,24]{1,0:T(8,128)} %ids_ref.3, bf16[224,576]{1,0:T(8,128)(2,1)} %constant.42.clone.perm_ref, bf16[24,1024]{1,0:T(8,128)(2,1)} %constant.43.clone.columns_ref, f32[8,1024]{1,0:T(8,128)} %constant.44.clone.rows_ref), custom_call_target="tpu_custom_call" | custom-call | tf_op jit(solution)/shard_map/pallas_call | solution.py:362
  19.3 0.0 collective-permute-done.1.west_ref
  19.3 0.7 collective-permute-done.2.corner_ref
  20.0 0.0 collective-permute-done.north_ref
  20.0 0.0 copy-done.2
  20.0 5.7 %shard_map.210 = (bf16[224,512]{1,0:T(8,128)(2,1)}, bf16[224,512]{1,0:T(8,128)(2,1)}, bf16[80,512]{1,0:T(8,128)(2,1)}, bf16[80,512]{1,0:T(8,128)(2,1)}) custom-call(s32[1,1]{1,0:T(1,128)} %bitcast.1.flag_ref, f32[8,256]{1,0:T(8,128)} %constant.45.clone.extra_ref, bf16[224,512]{1,0:T(8,128)(2,1)} %shard_map.208.main_ref, ...), custom_call_target="tpu_custom_call" | custom-call | tf_op jit(solution)/shard_map/pallas_call | solution.py:362
  25.7 0.6 collective-permute-start.3
  26.2 0.7 collective-permute-start.4
  26.9 0.5 collective-permute-start.5
  27.4 0.9 pad.4.whead_ref
  28.3 0.0 copy-done
  28.3 0.0 copy-done.1
  28.4 3.8 %shard_map.211 = (bf16[13,144,128]{2,1,0:T(8,128)(2,1)S(1)}, bf16[13,144,512]{2,1,0:T(8,128)(2,1)S(1)}, f32[144,512]{1,0:T(8,128)S(1)}, bf16[512,128]{1,0:T(8,12...) custom-call(bf16[144,1040]{1,0:T(8,128)(2,1)S(1)} %bitcast.13, ...), custom_call_target="tpu_custom_call" | custom-call | tf_op jit(solution)/shard_map/pallas_call | solution.py:362
  32.2 0.0 collective-permute-done.4.west_ref
  32.2 7.8 %collective-permute-done.5.corner_ref = bf16[80,512]{1,0:T(8,128)(2,1)S(1)} collective-permute-done((bf16[80,512]{1,0:T(8,128)(2,1)}, bf16[80,512]{1,0:T(8,128)(2,1)S(1)}, u32[]{:S(2)}, u32[]{:S(2)}) %collective-permute-start.5) | collective-permute-done | bytes 81952 | tf_op jit(solution)/shard_map/ppermute | solution.py:382
  40.0 0.0 collective-permute-done.3.north_ref
  40.0 7.7 %shard_map.212 = (bf16[576,512]{1,0:T(8,128)(2,1)}, bf16[144,1040]{1,0:T(8,128)(2,1)}, bf16[384,512]{1,0:T(8,128)(2,1)S(1)}, bf16[384,512]{1,0:T(8,128)(2,1)S(1)}) custom-call(s32[1,1]{1,0:T(1,128)} %bitcast.flag_ref, bf16[224,512]{1,0:T(8,128)(2,1)} %get-tuple-element.31.main_ref, bf16[224,512]{1,0:T(8,128)(2,1)S(1)} %collective-permute-done.3.north_ref, ...), custom_call_target="tpu_custom_call" | custom-call | tf_op jit(solution)/shard_map/pallas_call | solution.py:362
  47.7 1.5 %collective-permute-start.6 = (bf16[384,512]{1,0:T(8,128)(2,1)S(1)}, bf16[384,512]{1,0:T(8,128)(2,1)S(1)}, u32[]{:S(2)}, u32[]{:S(2)}) collective-permute-start(bf16[384,512]{1,0:T(8,128)(2,1)S(1)} %get-tuple-element.44), channel_id=1, source_target_pairs={{0,1},{1,0},{2,3},{3,2},{4,5},{5,4},{6,7},{7,6},{8,9},{9,8},{10,11... | collective-permute-start | bytes 1179656 | tf_op jit(solution)/shard_map/ppermute | solution.py:387
  49.2 1.3 %collective-permute-done.6.right_ref = bf16[384,512]{1,0:T(8,128)(2,1)S(1)} collective-permute-done((bf16[384,512]{1,0:T(8,128)(2,1)S(1)}, bf16[384,512]{1,0:T(8,128)(2,1)S(1)}, u32[]{:S(2)}, u32[]{:S(2)}) %collective-permute-start.6) | collective-permute-done | bytes 393248 | tf_op jit(solution)/shard_map/ppermute | solution.py:387
  50.6 0.1 shard_map.213
  50.7 11.9 %all_to_all.10 = bf16[16,24,512]{2,1,0:T(8,128)(2,1)S(1)} all-to-all(bf16[16,24,512]{2,1,0:T(8,128)(2,1)S(1)} %bitcast.12), channel_id=1, replica_groups=mesh['z'=8,'x_hi'=2,'x_lo'=2,'y'=4,'core'=2] {'x_hi','x_lo','y'}, dimensions={0} | all-to-all | bytes 786432 | tf_op jit(solution)/shard_map/all_to_all | solution.py:402
  62.6 0.1 reduce_sum.12
  62.7 22.8 %psum.7 = bf16[24,512]{1,0:T(8,128)(2,1)S(1)} all-reduce(bf16[24,512]{1,0:T(8,128)(2,1)S(1)} %reduce_sum.12), channel_id=1, replica_groups=mesh['z'=8,'x_hi'=2,'x_lo'=2,'y'=4,'core'=2] {'z'}, use_global_device_ids=true, to_apply=%region_1.2 | all-reduce | flops 12288 | bytes 49152 | tf_op jit(solution)/shard_map/psum | solution.py:403
  85.5 11.2 %all_to_all.11 = bf16[16,24,512]{2,1,0:T(8,128)(2,1)S(1)} all-to-all(bf16[16,24,512]{2,1,0:T(8,128)(2,1)S(1)} %broadcast_in_dim.2), channel_id=1, replica_groups=mesh['z'=8,'x_hi'=2,'x_lo'=2,'y'=4,'core'=2] {'x_hi','x_lo','y'}, dimensions={0} | all-to-all | bytes 786432 | tf_op jit(solution)/shard_map/all_to_all | solution.py:404
  96.7 10.0 %collective-permute-start.7 = (bf16[384,512]{1,0:T(8,128)(2,1)S(1)}, bf16[384,512]{1,0:T(8,128)(2,1)S(1)}, u32[]{:S(2)}, u32[]{:S(2)}) collective-permute-start(bf16[384,512]{1,0:T(8,128)(2,1)S(1)} %bitcast.10), channel_id=1, source_target_pairs={{0,1},{1,0},{2,3},{3,2},{4,5},{5,4},{6,7},{7,6},{8,9},{9,8},{10,11... | collective-permute-start | bytes 1179656 | tf_op jit(solution)/shard_map/ppermute | solution.py:387
  106.6 1.3 %collective-permute-done.7.other_ref = bf16[384,512]{1,0:T(8,128)(2,1)S(1)} collective-permute-done((bf16[384,512]{1,0:T(8,128)(2,1)S(1)}, bf16[384,512]{1,0:T(8,128)(2,1)S(1)}, u32[]{:S(2)}, u32[]{:S(2)}) %collective-permute-start.7) | collective-permute-done | bytes 393248 | tf_op jit(solution)/shard_map/ppermute | solution.py:387
  108.0 4.4 %shard_map.214 = (f32[512,1024]{1,0:T(8,128)}, f32[13,512]{1,0:T(8,128)}, f32[512,512]{1,0:T(8,128)}, f32[80,512]{1,0:T(8,128)}) custom-call(s32[1,1]{1,0:T(1,128)} %bitcast.flag_ref, bf16[384,512]{1,0:T(8,128)(2,1)S(1)} %bitcast.11, bf16[384,512]{1,0:T(8,128)(2,1)S(1)} %collective-permute-done.7.other_ref, bf16[512,512]{1,0:T(8,128)(2,1)} %get-tuple-element.45.order_ref, ...), custom_call_target="tpu_custom_call" | custom-call | tf_op jit(solution)/shard_map/pallas_call | solution.py:362
  (7 shorter events, 0.0 us)
Async XLA Ops:
  0.6 19.3 %copy-start.2 = (bf16[512,1536]{1,0:T(8,128)(2,1)S(1)}, bf16[512,1536]{1,0:T(8,128)(2,1)}, u32[]{:S(2)}) copy-start(bf16[512,1536]{1,0:T(8,128)(2,1)} %wqkv_ref.1) | copy-start | bytes 4718596
  3.2 16.7 %collective-permute-start = (bf16[224,512]{1,0:T(8,128)(2,1)}, bf16[224,512]{1,0:T(8,128)(2,1)}, u32[]{:S(2)}, u32[]{:S(2)}) collective-permute-start(bf16[224,512]{1,0:T(8,128)(2,1)} %get-tuple-element.28), channel_id=1, source_target_pairs={{0,240},{1,241},{2,242},{3,243},{4,244},{5,245},{6,246},{7,247},{8... | collective-permute-start | bytes 688136 | tf_op jit(solution)/shard_map/ppermute | solution.py:382
  12.1 7.2 %collective-permute-start.1 = (bf16[80,512]{1,0:T(8,128)(2,1)}, bf16[80,512]{1,0:T(8,128)(2,1)}, u32[]{:S(2)}, u32[]{:S(2)}) collective-permute-start(bf16[80,512]{1,0:T(8,128)(2,1)} %get-tuple-element.29), channel_id=1, source_target_pairs={{0,15},{1,0},{2,1},{3,2},{4,3},{5,4},{6,5},{7,6},{8,7},{9,8},{10,9... | collective-permute-start | bytes 245768 | tf_op jit(solution)/shard_map/ppermute | solution.py:382
  13.1 6.9 %collective-permute-start.2 = (bf16[80,512]{1,0:T(8,128)(2,1)}, bf16[80,512]{1,0:T(8,128)(2,1)}, u32[]{:S(2)}, u32[]{:S(2)}) collective-permute-start(bf16[80,512]{1,0:T(8,128)(2,1)} %get-tuple-element.30), channel_id=1, source_target_pairs={{0,255},{1,240},{2,241},{3,242},{4,243},{5,244},{6,245},{7,246},{8... | collective-permute-start | bytes 245768 | tf_op jit(solution)/shard_map/ppermute | solution.py:382
  16.9 11.4 %copy-start = (bf16[512,1024]{1,0:T(8,128)(2,1)S(1)}, bf16[512,1024]{1,0:T(8,128)(2,1)}, u32[]{:S(2)}) copy-start(bf16[512,1024]{1,0:T(8,128)(2,1)} %wkv_ref.5) | copy-start | bytes 3145732
  16.9 11.4 %copy-start.1 = (bf16[512,512]{1,0:T(8,128)(2,1)S(1)}, bf16[512,512]{1,0:T(8,128)(2,1)}, u32[]{:S(2)}) copy-start(bf16[512,512]{1,0:T(8,128)(2,1)} %wo_ref.3) | copy-start | bytes 1572868
  16.9 11.5 %copy-start.3 = (bf16[6,24,1040]{2,1,0:T(8,128)(2,1)S(1)}, bf16[6,24,1040]{2,1,0:T(8,128)(2,1)}, u32[]{:S(2)}) copy-start(bf16[6,24,1040]{2,1,0:T(8,128)(2,1)} %param.25) | copy-start | bytes 898564
  16.9 11.5 %copy-start.4 = (bf16[13,512]{1,0:T(8,128)(2,1)S(1)}, bf16[13,512]{1,0:T(8,128)(2,1)}, u32[]{:S(2)}) copy-start(bf16[13,512]{1,0:T(8,128)(2,1)} %queries_ref.5) | copy-start | bytes 39940
  25.7 14.3 %collective-permute-start.3 = (bf16[224,512]{1,0:T(8,128)(2,1)}, bf16[224,512]{1,0:T(8,128)(2,1)S(1)}, u32[]{:S(2)}, u32[]{:S(2)}) collective-permute-start(bf16[224,512]{1,0:T(8,128)(2,1)} %get-tuple-element.32), channel_id=1, source_target_pairs={{0,16},{1,17},{2,18},{3,19},{4,20},{5,21},{6,22},{7,23},{8,24},{9,... | collective-permute-start | bytes 688136 | tf_op jit(solution)/shard_map/ppermute | solution.py:382
  26.2 5.9 %collective-permute-start.4 = (bf16[80,512]{1,0:T(8,128)(2,1)}, bf16[80,512]{1,0:T(8,128)(2,1)S(1)}, u32[]{:S(2)}, u32[]{:S(2)}) collective-permute-start(bf16[80,512]{1,0:T(8,128)(2,1)} %get-tuple-element.33), channel_id=1, source_target_pairs={{0,1},{1,2},{2,3},{3,4},{4,5},{5,6},{6,7},{7,8},{8,9},{9,10},{10,1... | collective-permute-start | bytes 245768 | tf_op jit(solution)/shard_map/ppermute | solution.py:382
  26.9 13.1 %collective-permute-start.5 = (bf16[80,512]{1,0:T(8,128)(2,1)}, bf16[80,512]{1,0:T(8,128)(2,1)S(1)}, u32[]{:S(2)}, u32[]{:S(2)}) collective-permute-start(bf16[80,512]{1,0:T(8,128)(2,1)} %get-tuple-element.34), channel_id=1, source_target_pairs={{0,17},{1,18},{2,19},{3,20},{4,21},{5,22},{6,23},{7,24},{8,25},{9,... | collective-permute-start | bytes 245768 | tf_op jit(solution)/shard_map/ppermute | solution.py:382
  47.7 2.9 %collective-permute-start.6 = (bf16[384,512]{1,0:T(8,128)(2,1)S(1)}, bf16[384,512]{1,0:T(8,128)(2,1)S(1)}, u32[]{:S(2)}, u32[]{:S(2)}) collective-permute-start(bf16[384,512]{1,0:T(8,128)(2,1)S(1)} %get-tuple-element.44), channel_id=1, source_target_pairs={{0,1},{1,0},{2,3},{3,2},{4,5},{5,4},{6,7},{7,6},{8,9},{9,8},{10,11... | collective-permute-start | bytes 1179656 | tf_op jit(solution)/shard_map/ppermute | solution.py:387
  96.7 11.3 %collective-permute-start.7 = (bf16[384,512]{1,0:T(8,128)(2,1)S(1)}, bf16[384,512]{1,0:T(8,128)(2,1)S(1)}, u32[]{:S(2)}, u32[]{:S(2)}) collective-permute-start(bf16[384,512]{1,0:T(8,128)(2,1)S(1)} %bitcast.10), channel_id=1, source_target_pairs={{0,1},{1,0},{2,3},{3,2},{4,5},{5,4},{6,7},{7,6},{8,9},{9,8},{10,11... | collective-permute-start | bytes 1179656 | tf_op jit(solution)/shard_map/ppermute | solution.py:387

commit v6 on v5

--- a/solution.py
+++ b/solution.py
@@ -198,20 +198,30 @@
     return jnp.where(c % HEADS == j // (D // HEADS), tall, 0.0)
 
 
+def lane_of(j):
+    size = D // HEADS
+    return j % size // 16 * LANES + j // size * 16 + j % 16
+
+
 def feature_order():
-    j = lax.broadcasted_iota(jnp.int32, (D, D), 0)
-    lane = lax.broadcasted_iota(jnp.int32, (D, D), 1)
-    size = D // HEADS
-    wanted = j % size // 16 * LANES + j // size * 16 + j % 16
-    return jnp.where(wanted == lane, 1.0, 0.0).astype(BF)
+    wanted = lane_of(lax.broadcasted_iota(jnp.int32, (D, LANES), 0))
+    lane = lax.broadcasted_iota(jnp.int32, (D, LANES), 1)
+    tiles = [jnp.where(wanted == lane + start, 1.0, 0.0) for start in range(0, D, LANES)]
+    return jnp.concatenate(tiles, axis=1).astype(BF)
+
+
+def natural_order():
+    wanted = lane_of(lax.broadcasted_iota(jnp.int32, (8, D), 1))
+    lane = lax.broadcasted_iota(jnp.int32, (8, D), 0)
+    tiles = [jnp.where(wanted == lane + start, 1.0, 0.0) for start in range(0, D, 8)]
+    return jnp.concatenate(tiles, axis=0).astype(BF)
 
 
 def pre_kernel(
     cot_ref, queries_ref, wo_ref, whead_ref, wkv_ref,
-    up_ref, dctx_ref, dsum_ref, map_ref, base_ref, wv_ref, order_ref,
+    up_ref, dctx_ref, dsum_ref, map_ref, base_ref, wv_ref,
 ):
     order = feature_order()
-    order_ref[...] = order
     wv_ref[...] = mm(wkv_ref[:, D:], order).astype(BF)
     head = whead_ref[...]
     both = dot(wo_ref[...], head, ((1,), (1,))).astype(BF)
@@ -235,12 +245,14 @@
     flag_ref, main_ref, north_ref, west_ref, corner_ref, perm_ref, wkv_ref, queries_ref, up_ref, dctx_ref, dsum_ref,
     map_ref, base_ref, wv_ref,
     owned_ref, fields_ref, keep_ref, send_ref,
-    value, weights, dvalues, context, products, fields, sums,
+    value, weights, dvalues, context, products, fields, sums, owned, decoded_out, sems,
 ):
     pieces = (main_ref, north_ref, west_ref, corner_ref)
     packed = jnp.concatenate([ref[...] for ref in pieces], axis=0)
     wide = mm(perm_ref[...], packed)
-    owned_ref[...] = wide.astype(BF)
+    owned[...] = wide.astype(BF)
+    owned_copy = pltpu.make_async_copy(owned, owned_ref, sems.at[0])
+    owned_copy.start()
     normed = layer_norm(wide)
     key = mm(normed, wkv_ref[:, :D]).astype(BF)
     value[...] = mm(normed, wv_ref[...]).astype(BF).astype(F32)
@@ -286,7 +298,9 @@
         first, offset, width = spot(level)
         decoded = mm(context[level * PATCHES : (level + 1) * PATCHES], map_ref[...]) + base_ref[level : level + 1]
         fields[:, first : first + width] += dot(decoded.astype(BF), shift_matrix(offset, width), ((1,), (1,)))
-    fields_ref[...] = fields[...].astype(BF)
+    decoded_out[...] = fields[...].astype(BF)
+    fields_copy = pltpu.make_async_copy(decoded_out, fields_ref, sems.at[1])
+    fields_copy.start()
     slopes = [slopes[l * PATCHES : (l + 1) * PATCHES] for l in range(LEV - 1)]
     mean = sum(p * d for p, d in zip(slabs, slopes))
     dscores = [p * (d - mean) * 0.125 for p, d in zip(slabs, slopes)]
@@ -305,13 +319,15 @@
     top, bottom = sums[: ROWS // 2], sums[ROWS // 2 :]
     keep_ref[...] = jnp.where(second, bottom, top).astype(BF)
     send_ref[...] = jnp.where(second, top, bottom).astype(BF)
+    owned_copy.wait()
+    fields_copy.wait()
 
 
 def add_kernel(left_ref, right_ref, out_ref):
     out_ref[...] = (left_ref[...].astype(F32) + right_ref[...].astype(F32)).astype(BF)
 
 
-def final_kernel(flag_ref, mine_ref, other_ref, order_ref, wkv_ref, queries_ref, wo_ref, whead_ref, kv_ref, query_ref, o_ref, head_ref):
+def final_kernel(flag_ref, mine_ref, other_ref, wkv_ref, queries_ref, wo_ref, whead_ref, kv_ref, query_ref, o_ref, head_ref):
     second = flag_ref[0, 0] > 0
     mine, other = mine_ref[...].astype(F32), other_ref[...].astype(F32)
     sums = jnp.concatenate([jnp.where(second, other, mine), jnp.where(second, mine, other)], axis=0).astype(BF)
@@ -321,14 +337,15 @@
     outer = sums[D + LANES :]
     level_sums = outer[OUTS : OUTS + 16, :LANES]
     spread = spread_queries(queries.astype(F32)).astype(BF)
-    values = dot(sums[:D], order_ref[...], ((1,), (1,)))
+    natural = natural_order()
+    values = mm(sums[:D], natural)
     keys = dot(keyed, spread, ((0,), (0,)))
     c = lax.broadcasted_iota(jnp.int32, (LANES, D), 0)
     j = lax.broadcasted_iota(jnp.int32, (LANES, D), 1)
     grouped = jnp.where(c % HEADS == j // (D // HEADS), mm(keyed, wkv_ref[:, :D]), 0.0)
     grouped = jnp.sum(grouped.reshape(LANES // HEADS, HEADS, D), axis=1)
     level = grouped[:PLEV] + mm(level_sums, head)[:PLEV]
-    clean = dot(outer[:OUTS], order_ref[...], ((1,), (1,))).astype(BF)
+    clean = mm(outer[:OUTS], natural).astype(BF)
     out = dot(clean, head[:OUTS], ((0,), (0,)))
     pixels = mm(clean, wo_ref[...])
     pixels = pixels + dot(level_sums[:PLEV, :OUTS], queries, ((0,), (0,)))
@@ -343,11 +360,13 @@
     head_ref[...] = pixels * factor
 
 
-def call(kernel, outs, spaces, scratch=(), limit=40):
+def call(kernel, outs, spaces, scratch=(), limit=40, out_specs=None):
     where = {"V": pltpu.VMEM, "H": pltpu.HBM}
     whole, scalar = pl.BlockSpec(memory_space=pltpu.VMEM), pl.BlockSpec(memory_space=pltpu.SMEM)
+    more = {} if out_specs is None else {"out_specs": out_specs}
     run = pl.pallas_call(
         kernel,
+        **more,
         in_specs=[scalar if space == "S" else whole for space in spaces],
         out_shape=outs,
         scratch_shapes=list(scratch),
@@ -400,7 +419,7 @@
     mine = call(add_kernel, struct((rows, width)), "VV", limit=8)(keep, swap(send))
     chips = lax.axis_size(PLANE)
     mine = add_up(lax.all_to_all(mine.reshape(chips, rows // chips, width), PLANE, 0, 0, tiled=True))
-    mine = lax.psum(mine, "z")
+    mine = add_up(lax.all_to_all(copies(mine, "z"), "z", 0, 0, tiled=True))
     mine = lax.all_to_all(copies(mine, PLANE), PLANE, 0, 0, tiled=True).reshape(rows, width)
     return mine, swap(mine)
 
@@ -420,7 +439,7 @@
     )
     north, west, corner = move(north, -1, 0), move(west, 0, -1), move(corner, -1, -1)
     head = jnp.pad(w_head.T, ((0, LANES - OUTS), (0, 0)))
-    up, dctx, dsum, both, base, wv, feature = call(
+    up, dctx, dsum, both, base, wv = call(
         pre_kernel,
         [
             struct((PLEV, PATCHES, LANES)),
@@ -429,7 +448,6 @@
             struct((D, LANES)),
             struct((16, LANES), F32),
             struct((D, D)),
-            far_struct((D, D)),
         ],
         "VVVVV",
     )(field_cotangent.reshape(PATCHES, PLEV * OUTS), level_queries, w_o, head, w_kv)
@@ -455,14 +473,18 @@
             pltpu.VMEM(((LEV - 1) * PATCHES, PLEV * LANES), BF),
             pltpu.VMEM((PATCHES, PLEV * OUTS), F32),
             pltpu.VMEM((ROWS, D), F32),
+            pltpu.VMEM((TOKENS, D), BF),
+            pltpu.VMEM((PATCHES, PLEV * OUTS), BF),
+            pltpu.SemaphoreType.DMA((2,)),
         ],
+        out_specs=[pl.BlockSpec(memory_space=pl.ANY)] * 2 + [pl.BlockSpec(memory_space=pltpu.VMEM)] * 2,
     )(core, main, north, west, corner, jnp.asarray(perm.T, BF), w_kv, level_queries, up, dctx, dsum, both, base, wv)
     mine, other = sum_over_all(keep, send)
     kv, query, out, pixels = call(
         final_kernel,
         [struct((D, 2 * D), F32), struct((PLEV, D), F32), struct((D, D), F32), struct((OUTS, D), F32)],
-        "SVVHVVVV",
-    )(core, mine, other, feature, w_kv, level_queries, w_o, head)
+        "SVVVVVV",
+    )(core, mine, other, w_kv, level_queries, w_o, head)
     shape = latents.shape
     return (owned.reshape(shape), fields.reshape(shape[1], shape[2], PLEV * OUTS), kv, query, out, pixels.T)
 

time: 113 us -> 96.2 us (0.85)
  blocking collectives: 45.9 us -> 36.2 us
  starting transfers between devices: 26.9 us -> 21.2 us
  Pallas kernels: 26.7 us -> 25 us
    psum x1 -> x0, blocking collectives: 22.8 us -> none  [sum_over_all(): mine = lax.psum(mine, 'z')]
    all_to_all x0 -> x1, blocking collectives: none -> 12.8 us  [sum_over_all(): mine = add_up(lax.all_to_all(copies(mine, 'z'), 'z', 0, 0, tiled=True))]
    ppermute x2, starting transfers between devices: 11.5 us -> 5.82 us  [swap(): lax.ppermute(array, 'core', [(i, (i + 1) % count) for i in range(count)])]
    pallas_call x7, Pallas kernels: 26.7 us -> 25 us  [close(): return run(*held)]
where the time goes in v6:
time: 96.2 us; the launch traced here: 95.8 us
  blocking collectives  36.2 us (38%)
  Pallas kernels  25 us (26%)
  starting transfers between devices  21.2 us (22%)
  waiting for transfers between devices  11.7 us (12%)
    pallas_call x7, Pallas kernels, close(): return run(*held)  25 us
    ppermute x6, starting transfers between devices, move(): return lax.ppermute(array, LAT + LON, route)  15.4 us
    all_to_all x1, blocking collectives, sum_over_all(): mine = add_up(lax.all_to_all(copies(mine, 'z'), 'z', 0, 0, tiled=True))  12.8 us
    all_to_all x1, blocking collectives, sum_over_all(): lax.all_to_all(mine.reshape(chips, rows // chips, width), PLANE, 0, 0, ti...  11.9 us
    all_to_all x1, blocking collectives, sum_over_all(): lax.all_to_all(copies(mine, PLANE), PLANE, 0, 0, tiled=True)  11.4 us
    ppermute x6, waiting for transfers between devices, move(): return lax.ppermute(array, LAT + LON, route)  8.96 us
    ppermute x2, starting transfers between devices, swap(): lax.ppermute(array, 'core', [(i, (i + 1) % count) for i in range(count)])  5.82 us
    ppermute x2, waiting for transfers between devices, swap(): lax.ppermute(array, 'core', [(i, (i + 1) % count) for i in range(count)])  2.7 us
  transfers between devices with their start and end apart: 8, of which 4 were waited for; matrix products, arithmetic and copies ran while one was open for 1% of the time, Pallas kernels for 6%

profile of v6, /device:TPU:1, one launch (start us, length us, event | category | flops | bytes accessed | tf_op | source)
XLA Modules:
  0.0 95.8 jit_solution(4734116129574006823)
XLA Ops:
  0.6 0.0 copy-start.2
  0.6 2.6 %shard_map.209 = (bf16[224,512]{1,0:T(8,128)(2,1)}, bf16[80,512]{1,0:T(8,128)(2,1)}, bf16[80,512]{1,0:T(8,128)(2,1)}) custom-call(bf16[576,512]{1,0:T(8,128)(2,1)} %bitcast.14, s32[6,24]{1,0:T(8,128)} %ids_ref.3, bf16[384,576]{1,0:T(8,128)(2,1)} %constant.40.clone.perm_ref, bf16[24,2048]{1,0:T(8,128)(2,1)} %constant.41.clone.columns_ref, ...), custom_call_target="tpu_custom_call" | custom-call | tf_op jit(solution)/shard_map/pallas_call | solution.py:381
  3.2 8.9 %collective-permute-start = (bf16[224,512]{1,0:T(8,128)(2,1)}, bf16[224,512]{1,0:T(8,128)(2,1)}, u32[]{:S(2)}, u32[]{:S(2)}) collective-permute-start(bf16[224,512]{1,0:T(8,128)(2,1)} %get-tuple-element.27), channel_id=1, source_target_pairs={{0,240},{1,241},{2,242},{3,243},{4,244},{5,245},{6,246},{7,247},{8... | collective-permute-start | bytes 688136 | tf_op jit(solution)/shard_map/ppermute | solution.py:401
  12.1 1.0 collective-permute-start.1
  13.1 3.8 %collective-permute-start.2 = (bf16[80,512]{1,0:T(8,128)(2,1)}, bf16[80,512]{1,0:T(8,128)(2,1)}, u32[]{:S(2)}, u32[]{:S(2)}) collective-permute-start(bf16[80,512]{1,0:T(8,128)(2,1)} %get-tuple-element.29), channel_id=1, source_target_pairs={{0,255},{1,240},{2,241},{3,242},{4,243},{5,244},{6,245},{7,246},{8... | collective-permute-start | bytes 245768 | tf_op jit(solution)/shard_map/ppermute | solution.py:401
  16.9 2.4 %shard_map.208.main_ref = bf16[224,512]{1,0:T(8,128)(2,1)} custom-call(bf16[576,512]{1,0:T(8,128)(2,1)} %bitcast.15, s32[6,24]{1,0:T(8,128)} %ids_ref.3, bf16[224,576]{1,0:T(8,128)(2,1)} %constant.43.clone.perm_ref, bf16[24,1024]{1,0:T(8,128)(2,1)} %constant.44.clone.columns_ref, f32[8,1024]{1,0:T(8,128)} %constant.45.clone.rows_ref), custom_call_target="tpu_custom_call" | custom-call | tf_op jit(solution)/shard_map/pallas_call | solution.py:381
  19.3 0.0 collective-permute-done.1.west_ref
  19.3 0.7 collective-permute-done.2.corner_ref
  20.0 0.0 collective-permute-done.north_ref
  20.0 0.0 copy-done.2
  20.0 5.7 %shard_map.210 = (bf16[224,512]{1,0:T(8,128)(2,1)}, bf16[224,512]{1,0:T(8,128)(2,1)}, bf16[80,512]{1,0:T(8,128)(2,1)}, bf16[80,512]{1,0:T(8,128)(2,1)}) custom-call(s32[1,1]{1,0:T(1,128)} %bitcast.1.flag_ref, f32[8,256]{1,0:T(8,128)} %constant.46.clone.extra_ref, bf16[224,512]{1,0:T(8,128)(2,1)} %shard_map.208.main_ref, ...), custom_call_target="tpu_custom_call" | custom-call | tf_op jit(solution)/shard_map/pallas_call | solution.py:381
  25.7 0.6 collective-permute-start.3
  26.2 0.7 collective-permute-start.4
  26.9 0.5 collective-permute-start.5
  27.4 0.9 pad.4.whead_ref
  28.3 0.0 copy-done
  28.3 0.0 copy-done.1
  28.4 3.3 %shard_map.211 = (bf16[13,144,128]{2,1,0:T(8,128)(2,1)S(1)}, bf16[13,144,512]{2,1,0:T(8,128)(2,1)S(1)}, f32[144,512]{1,0:T(8,128)S(1)}, bf16[512,128]{1,0:T(8,12...) custom-call(bf16[144,1040]{1,0:T(8,128)(2,1)S(1)} %bitcast.13, bf16[13,512]{1,0:T(8,128)(2,1)S(1)} %copy-done.4, ...), custom_call_target="tpu_custom_call" | custom-call | tf_op jit(solution)/shard_map/pallas_call | solution.py:381
  31.7 0.0 collective-permute-done.4.west_ref
  31.7 8.3 %collective-permute-done.5.corner_ref = bf16[80,512]{1,0:T(8,128)(2,1)S(1)} collective-permute-done((bf16[80,512]{1,0:T(8,128)(2,1)}, bf16[80,512]{1,0:T(8,128)(2,1)S(1)}, u32[]{:S(2)}, u32[]{:S(2)}) %collective-permute-start.5) | collective-permute-done | bytes 81952 | tf_op jit(solution)/shard_map/ppermute | solution.py:401
  40.0 0.0 collective-permute-done.3.north_ref
  40.0 7.6 %shard_map.212 = (bf16[576,512]{1,0:T(8,128)(2,1)}, bf16[144,1040]{1,0:T(8,128)(2,1)}, bf16[384,512]{1,0:T(8,128)(2,1)S(1)}, bf16[384,512]{1,0:T(8,128)(2,1)S(1)}) custom-call(s32[1,1]{1,0:T(1,128)} %bitcast.flag_ref, bf16[224,512]{1,0:T(8,128)(2,1)} %get-tuple-element.30.main_ref, bf16[224,512]{1,0:T(8,128)(2,1)S(1)} %collective-permute-done.3.north_ref, ...), custom_call_target="tpu_custom_call" | custom-call | tf_op jit(solution)/shard_map/pallas_call | solution.py:381
  47.6 1.5 %collective-permute-start.6 = (bf16[384,512]{1,0:T(8,128)(2,1)S(1)}, bf16[384,512]{1,0:T(8,128)(2,1)S(1)}, u32[]{:S(2)}, u32[]{:S(2)}) collective-permute-start(bf16[384,512]{1,0:T(8,128)(2,1)S(1)} %get-tuple-element.43), channel_id=1, source_target_pairs={{0,1},{1,0},{2,3},{3,2},{4,5},{5,4},{6,7},{7,6},{8,9},{9,8},{10,11... | collective-permute-start | bytes 1179656 | tf_op jit(solution)/shard_map/ppermute | solution.py:406
  49.1 1.3 %collective-permute-done.6.right_ref = bf16[384,512]{1,0:T(8,128)(2,1)S(1)} collective-permute-done((bf16[384,512]{1,0:T(8,128)(2,1)S(1)}, bf16[384,512]{1,0:T(8,128)(2,1)S(1)}, u32[]{:S(2)}, u32[]{:S(2)}) %collective-permute-start.6) | collective-permute-done | bytes 393248 | tf_op jit(solution)/shard_map/ppermute | solution.py:406
  50.5 0.1 shard_map.213
  50.6 11.9 %all_to_all.15 = bf16[16,24,512]{2,1,0:T(8,128)(2,1)S(1)} all-to-all(bf16[16,24,512]{2,1,0:T(8,128)(2,1)S(1)} %bitcast.10), channel_id=1, replica_groups=mesh['z'=8,'x_hi'=2,'x_lo'=2,'y'=4,'core'=2] {'x_hi','x_lo','y'}, dimensions={0} | all-to-all | bytes 786432 | tf_op jit(solution)/shard_map/all_to_all | solution.py:421
  62.5 0.1 reduce_sum.24
  62.6 12.8 %all_to_all.16 = bf16[8,24,512]{2,1,0:T(8,128)(2,1)S(1)} all-to-all(bf16[8,24,512]{2,1,0:T(8,128)(2,1)S(1)} %broadcast_in_dim.4), channel_id=1, replica_groups=mesh['z'=8,'x_hi'=2,'x_lo'=2,'y'=4,'core'=2] {'z'}, dimensions={0} | all-to-all | bytes 393216 | tf_op jit(solution)/shard_map/all_to_all | solution.py:422
  75.4 11.4 %all_to_all.17 = bf16[16,24,512]{2,1,0:T(8,128)(2,1)S(1)} all-to-all(bf16[16,24,512]{2,1,0:T(8,128)(2,1)S(1)} %broadcast_in_dim.5), channel_id=1, replica_groups=mesh['z'=8,'x_hi'=2,'x_lo'=2,'y'=4,'core'=2] {'x_hi','x_lo','y'}, dimensions={0} | all-to-all | bytes 786432 | tf_op jit(solution)/shard_map/all_to_all | solution.py:423
  86.9 4.3 %collective-permute-start.7 = (bf16[384,512]{1,0:T(8,128)(2,1)S(1)}, bf16[384,512]{1,0:T(8,128)(2,1)S(1)}, u32[]{:S(2)}, u32[]{:S(2)}) collective-permute-start(bf16[384,512]{1,0:T(8,128)(2,1)S(1)} %bitcast.11), channel_id=1, source_target_pairs={{0,1},{1,0},{2,3},{3,2},{4,5},{5,4},{6,7},{7,6},{8,9},{9,8},{10,11... | collective-permute-start | bytes 1179656 | tf_op jit(solution)/shard_map/ppermute | solution.py:406
  91.2 1.3 %collective-permute-done.7.other_ref = bf16[384,512]{1,0:T(8,128)(2,1)S(1)} collective-permute-done((bf16[384,512]{1,0:T(8,128)(2,1)S(1)}, bf16[384,512]{1,0:T(8,128)(2,1)S(1)}, u32[]{:S(2)}, u32[]{:S(2)}) %collective-permute-start.7) | collective-permute-done | bytes 393248 | tf_op jit(solution)/shard_map/ppermute | solution.py:406
  92.5 3.3 %shard_map.214 = (f32[512,1024]{1,0:T(8,128)}, f32[13,512]{1,0:T(8,128)}, f32[512,512]{1,0:T(8,128)}, f32[80,512]{1,0:T(8,128)}) custom-call(s32[1,1]{1,0:T(1,128)} %bitcast.flag_ref, bf16[384,512]{1,0:T(8,128)(2,1)S(1)} %bitcast.12, bf16[384,512]{1,0:T(8,128)(2,1)S(1)} %collective-permute-done.7.other_ref, bf16[512,1024]{1,0:T(8,128)(2,1)S(1)} %copy-done, ...), custom_call_target="tpu_custom_call" | custom-call | tf_op jit(solution)/shard_map/pallas_call | solution.py:381
  (9 shorter events, 0.1 us)
Async XLA Ops:
  0.6 19.3 %copy-start.2 = (bf16[512,1536]{1,0:T(8,128)(2,1)S(1)}, bf16[512,1536]{1,0:T(8,128)(2,1)}, u32[]{:S(2)}) copy-start(bf16[512,1536]{1,0:T(8,128)(2,1)} %wqkv_ref.1) | copy-start | bytes 4718596
  3.2 16.7 %collective-permute-start = (bf16[224,512]{1,0:T(8,128)(2,1)}, bf16[224,512]{1,0:T(8,128)(2,1)}, u32[]{:S(2)}, u32[]{:S(2)}) collective-permute-start(bf16[224,512]{1,0:T(8,128)(2,1)} %get-tuple-element.27), channel_id=1, source_target_pairs={{0,240},{1,241},{2,242},{3,243},{4,244},{5,245},{6,246},{7,247},{8... | collective-permute-start | bytes 688136 | tf_op jit(solution)/shard_map/ppermute | solution.py:401
  12.1 7.2 %collective-permute-start.1 = (bf16[80,512]{1,0:T(8,128)(2,1)}, bf16[80,512]{1,0:T(8,128)(2,1)}, u32[]{:S(2)}, u32[]{:S(2)}) collective-permute-start(bf16[80,512]{1,0:T(8,128)(2,1)} %get-tuple-element.28), channel_id=1, source_target_pairs={{0,15},{1,0},{2,1},{3,2},{4,3},{5,4},{6,5},{7,6},{8,7},{9,8},{10,9... | collective-permute-start | bytes 245768 | tf_op jit(solution)/shard_map/ppermute | solution.py:401
  13.1 6.9 %collective-permute-start.2 = (bf16[80,512]{1,0:T(8,128)(2,1)}, bf16[80,512]{1,0:T(8,128)(2,1)}, u32[]{:S(2)}, u32[]{:S(2)}) collective-permute-start(bf16[80,512]{1,0:T(8,128)(2,1)} %get-tuple-element.29), channel_id=1, source_target_pairs={{0,255},{1,240},{2,241},{3,242},{4,243},{5,244},{6,245},{7,246},{8... | collective-permute-start | bytes 245768 | tf_op jit(solution)/shard_map/ppermute | solution.py:401
  16.9 11.4 %copy-start = (bf16[512,1024]{1,0:T(8,128)(2,1)S(1)}, bf16[512,1024]{1,0:T(8,128)(2,1)}, u32[]{:S(2)}) copy-start(bf16[512,1024]{1,0:T(8,128)(2,1)} %wkv_ref.5) | copy-start | bytes 3145732
  16.9 11.5 %copy-start.1 = (bf16[512,512]{1,0:T(8,128)(2,1)S(1)}, bf16[512,512]{1,0:T(8,128)(2,1)}, u32[]{:S(2)}) copy-start(bf16[512,512]{1,0:T(8,128)(2,1)} %wo_ref.3) | copy-start | bytes 1572868
  16.9 11.5 %copy-start.3 = (bf16[6,24,1040]{2,1,0:T(8,128)(2,1)S(1)}, bf16[6,24,1040]{2,1,0:T(8,128)(2,1)}, u32[]{:S(2)}) copy-start(bf16[6,24,1040]{2,1,0:T(8,128)(2,1)} %param.25) | copy-start | bytes 898564
  16.9 11.5 %copy-start.4 = (bf16[13,512]{1,0:T(8,128)(2,1)S(1)}, bf16[13,512]{1,0:T(8,128)(2,1)}, u32[]{:S(2)}) copy-start(bf16[13,512]{1,0:T(8,128)(2,1)} %queries_ref.5) | copy-start | bytes 39940
  25.7 14.3 %collective-permute-start.3 = (bf16[224,512]{1,0:T(8,128)(2,1)}, bf16[224,512]{1,0:T(8,128)(2,1)S(1)}, u32[]{:S(2)}, u32[]{:S(2)}) collective-permute-start(bf16[224,512]{1,0:T(8,128)(2,1)} %get-tuple-element.31), channel_id=1, source_target_pairs={{0,16},{1,17},{2,18},{3,19},{4,20},{5,21},{6,22},{7,23},{8,24},{9,... | collective-permute-start | bytes 688136 | tf_op jit(solution)/shard_map/ppermute | solution.py:401
  26.2 5.5 %collective-permute-start.4 = (bf16[80,512]{1,0:T(8,128)(2,1)}, bf16[80,512]{1,0:T(8,128)(2,1)S(1)}, u32[]{:S(2)}, u32[]{:S(2)}) collective-permute-start(bf16[80,512]{1,0:T(8,128)(2,1)} %get-tuple-element.32), channel_id=1, source_target_pairs={{0,1},{1,2},{2,3},{3,4},{4,5},{5,6},{6,7},{7,8},{8,9},{9,10},{10,1... | collective-permute-start | bytes 245768 | tf_op jit(solution)/shard_map/ppermute | solution.py:401
  26.9 13.1 %collective-permute-start.5 = (bf16[80,512]{1,0:T(8,128)(2,1)}, bf16[80,512]{1,0:T(8,128)(2,1)S(1)}, u32[]{:S(2)}, u32[]{:S(2)}) collective-permute-start(bf16[80,512]{1,0:T(8,128)(2,1)} %get-tuple-element.33), channel_id=1, source_target_pairs={{0,17},{1,18},{2,19},{3,20},{4,21},{5,22},{6,23},{7,24},{8,25},{9,... | collective-permute-start | bytes 245768 | tf_op jit(solution)/shard_map/ppermute | solution.py:401
  47.6 2.9 %collective-permute-start.6 = (bf16[384,512]{1,0:T(8,128)(2,1)S(1)}, bf16[384,512]{1,0:T(8,128)(2,1)S(1)}, u32[]{:S(2)}, u32[]{:S(2)}) collective-permute-start(bf16[384,512]{1,0:T(8,128)(2,1)S(1)} %get-tuple-element.43), channel_id=1, source_target_pairs={{0,1},{1,0},{2,3},{3,2},{4,5},{5,4},{6,7},{7,6},{8,9},{9,8},{10,11... | collective-permute-start | bytes 1179656 | tf_op jit(solution)/shard_map/ppermute | solution.py:406
  86.9 5.6 %collective-permute-start.7 = (bf16[384,512]{1,0:T(8,128)(2,1)S(1)}, bf16[384,512]{1,0:T(8,128)(2,1)S(1)}, u32[]{:S(2)}, u32[]{:S(2)}) collective-permute-start(bf16[384,512]{1,0:T(8,128)(2,1)S(1)} %bitcast.11), channel_id=1, source_target_pairs={{0,1},{1,0},{2,3},{3,2},{4,5},{5,4},{6,7},{7,6},{8,9},{9,8},{10,11... | collective-permute-start | bytes 1179656 | tf_op jit(solution)/shard_map/ppermute | solution.py:406

commit v7 on v6

--- a/solution.py
+++ b/solution.py
@@ -56,7 +56,7 @@
             order += rows_of(pair, rows, range(6, 18))
         for pair in level_pairs:
             order += rows_of(pair, rows, range(18, 24)) + [-1] * 4
-    for rows in ((3, 4, 5), (0, 1, 2)):
+    for rows in ((0, 1, 2), (3, 4, 5)):
         for pair in level_pairs:
             order += rows_of(pair, rows, range(0, 6)) + [-1] * 4
     return np.array(order)
@@ -74,7 +74,7 @@
     rows = np.zeros((8, 12 * SPAN), np.float32)
     extra = np.zeros((8, SPAN), np.float32)
     segment = 0
-    for starts, far in zip(PIECES, (False, True, False, True)):
+    for starts, far in zip(PIECES, (False, True, True, False)):
         for window, (at, count, place) in starts.items():
             for i in range(count):
                 lane, token = place + i, at + i
@@ -127,10 +127,10 @@
 
 
 def attention_kernel(
-    flag_ref, extra_ref, main_ref, north_ref, west_ref, corner_ref, wqkv_ref, wout_ref,
-    main_out, north_out, west_out, corner_out, proj, context,
+    flag_ref, extra_ref, main_ref, north_ref, corner_ref, west_ref, wqkv_ref, wout_ref,
+    main_out, north_out, corner_out, west_out, proj, context,
 ):
-    pieces = (main_ref, north_ref, west_ref, corner_ref)
+    pieces = (main_ref, north_ref, corner_ref, west_ref)
     wide = jnp.concatenate([ref[...].astype(F32) for ref in pieces], axis=0)
     proj[...] = mm(layer_norm(wide), wqkv_ref[...])
     lines = sum(ref[ref.shape[0] - 16 :, :SPAN].astype(F32) for ref in pieces)[12:]
@@ -159,13 +159,14 @@
             lane = pair * LANES
             query = take(lane).astype(BF).astype(F32) * 0.125
             key = take(D + lane).astype(BF)
-            value = take(2 * D + lane).astype(BF)
+            value = take(2 * D + lane).astype(BF).astype(F32)
             both = jnp.concatenate([jnp.where(low, query, 0.0), jnp.where(low, 0.0, query)], axis=0).astype(BF)
             scores = dot(both, key, ((1,), (1,))) + bias
-            weights = jnp.exp(scores - jnp.max(scores, axis=-1, keepdims=True))
-            scale = 1.0 / jnp.sum(weights, axis=-1, keepdims=True)
-            mixed = mm(weights.astype(BF), value) * scale
-            result = jnp.where(low, mixed[:size], mixed[size:])
+            weights = jnp.exp(scores - jnp.max(scores, axis=-1, keepdims=True)).astype(BF)
+            even = mm(weights[:size], jnp.where(low, value, 1.0).astype(BF))
+            odd = mm(weights[size:], jnp.where(low, 1.0, value).astype(BF))
+            sums = pltpu.roll(jnp.where(low, odd, even), LANES // 2, 1)
+            result = jnp.where(low, even, odd) / sums
             start = 0
             for at, count in parts:
                 context[at : at + count, lane : lane + LANES] = result[start : start + count]
@@ -174,8 +175,8 @@
     mixed = mixed.astype(BF)
     main_out[...] = mixed[:n]
     north_out[...] = mixed[n:w]
-    west_out[...] = mixed[w:c]
-    corner_out[...] = mixed[c:]
+    corner_out[...] = mixed[w:c]
+    west_out[...] = mixed[c:]
 
 
 def shift_matrix(offset, width):
@@ -242,12 +243,12 @@
 
 
 def decode_kernel(
-    flag_ref, main_ref, north_ref, west_ref, corner_ref, perm_ref, wkv_ref, queries_ref, up_ref, dctx_ref, dsum_ref,
+    flag_ref, main_ref, north_ref, corner_ref, west_ref, perm_ref, wkv_ref, queries_ref, up_ref, dctx_ref, dsum_ref,
     map_ref, base_ref, wv_ref,
     owned_ref, fields_ref, keep_ref, send_ref,
     value, weights, dvalues, context, products, fields, sums, owned, decoded_out, sems,
 ):
-    pieces = (main_ref, north_ref, west_ref, corner_ref)
+    pieces = (main_ref, north_ref, corner_ref, west_ref)
     packed = jnp.concatenate([ref[...] for ref in pieces], axis=0)
     wide = mm(perm_ref[...], packed)
     owned[...] = wide.astype(BF)
@@ -327,7 +328,7 @@
     out_ref[...] = (left_ref[...].astype(F32) + right_ref[...].astype(F32)).astype(BF)
 
 
-def final_kernel(flag_ref, mine_ref, other_ref, wkv_ref, queries_ref, wo_ref, whead_ref, kv_ref, query_ref, o_ref, head_ref):
+def final_kernel(flag_ref, mine_ref, other_ref, wkv_ref, queries_ref, wo_ref, whead_ref, kv_ref, query_ref, o_ref, head_ref, kv, o, sems):
     second = flag_ref[0, 0] > 0
     mine, other = mine_ref[...].astype(F32), other_ref[...].astype(F32)
     sums = jnp.concatenate([jnp.where(second, other, mine), jnp.where(second, mine, other)], axis=0).astype(BF)
@@ -353,11 +354,21 @@
     squares = squares + jnp.sum(out * out) + jnp.sum(pixels * pixels)
     limit = math.sqrt(2 * D * D + PLEV * D + D * D + D * OUTS)
     factor = jnp.minimum(1.0, limit * lax.rsqrt(jnp.full((1, 1), squares + clip_eps, F32)))
-    kv_ref[:, :D] = keys * factor
-    kv_ref[:, D:] = values * factor
+    values_half, keys_half = (slice(None), slice(D, None)), (slice(None), slice(None, D))
+    kv[values_half] = values * factor
+    values_copy = pltpu.make_async_copy(kv.at[values_half], kv_ref.at[values_half], sems.at[0])
+    values_copy.start()
+    kv[keys_half] = keys * factor
+    keys_copy = pltpu.make_async_copy(kv.at[keys_half], kv_ref.at[keys_half], sems.at[1])
+    keys_copy.start()
+    o[...] = out * factor
+    o_copy = pltpu.make_async_copy(o, o_ref, sems.at[2])
+    o_copy.start()
     query_ref[...] = level * factor
-    o_ref[...] = out * factor
     head_ref[...] = pixels * factor
+    values_copy.wait()
+    keys_copy.wait()
+    o_copy.wait()
 
 
 def call(kernel, outs, spaces, scratch=(), limit=40, out_specs=None):
@@ -431,13 +442,13 @@
     shapes = [far_struct((MAIN, D)), struct((MAIN, D)), struct((SIDE, D)), struct((SIDE, D))]
     split = 4 * SPAN
     flat = latents.reshape(TOKENS, D)
-    north, west, corner = call(functools.partial(pack_kernel, PIECES[1:]), shapes[1:], "HHHHH", limit=56)(
+    north, corner, west = call(functools.partial(pack_kernel, PIECES[1:]), shapes[1:], "HHHHH", limit=56)(
         flat, mask_ids, jnp.asarray(perm[MAIN:], BF), jnp.asarray(columns[:, split:], BF), jnp.asarray(rows[:, split:])
     )
     (main,) = call(functools.partial(pack_kernel, PIECES[:1]), shapes[:1], "HHHHH", limit=56)(
         flat, mask_ids, jnp.asarray(perm[:MAIN], BF), jnp.asarray(columns[:, :split], BF), jnp.asarray(rows[:, :split])
     )
-    north, west, corner = move(north, -1, 0), move(west, 0, -1), move(corner, -1, -1)
+    north, corner, west = move(north, -1, 0), move(corner, -1, -1), move(west, 0, -1)
     head = jnp.pad(w_head.T, ((0, LANES - OUTS), (0, 0)))
     up, dctx, dsum, both, base, wv = call(
         pre_kernel,
@@ -451,14 +462,14 @@
         ],
         "VVVVV",
     )(field_cotangent.reshape(PATCHES, PLEV * OUTS), level_queries, w_o, head, w_kv)
-    main, north, west, corner = call(
+    main, north, corner, west = call(
         attention_kernel,
         shapes,
         "SHHHHHVH",
         [pltpu.VMEM((PACKED, 3 * D), F32), pltpu.VMEM((PACKED, D), F32)],
         limit=48,
-    )(flag, jnp.asarray(extra), main, north, west, corner, w_qkv, w_out)
-    north, west, corner = move(north, 1, 0), move(west, 0, 1), move(corner, 1, 1)
+    )(flag, jnp.asarray(extra), main, north, corner, west, w_qkv, w_out)
+    north, corner, west = move(north, 1, 0), move(corner, 1, 1), move(west, 0, 1)
     core = lax.axis_index("core").astype(jnp.int32).reshape(1, 1)
     share = struct((ROWS // 2, D))
     owned, fields, keep, send = call(
@@ -478,12 +489,14 @@
             pltpu.SemaphoreType.DMA((2,)),
         ],
         out_specs=[pl.BlockSpec(memory_space=pl.ANY)] * 2 + [pl.BlockSpec(memory_space=pltpu.VMEM)] * 2,
-    )(core, main, north, west, corner, jnp.asarray(perm.T, BF), w_kv, level_queries, up, dctx, dsum, both, base, wv)
+    )(core, main, north, corner, west, jnp.asarray(perm.T, BF), w_kv, level_queries, up, dctx, dsum, both, base, wv)
     mine, other = sum_over_all(keep, send)
     kv, query, out, pixels = call(
         final_kernel,
         [struct((D, 2 * D), F32), struct((PLEV, D), F32), struct((D, D), F32), struct((OUTS, D), F32)],
         "SVVVVVV",
+        [pltpu.VMEM((D, 2 * D), F32), pltpu.VMEM((D, D), F32), pltpu.SemaphoreType.DMA((3,))],
+        out_specs=[pl.BlockSpec(memory_space=space) for space in (pl.ANY, pltpu.VMEM, pl.ANY, pltpu.VMEM)],
     )(core, mine, other, w_kv, level_queries, w_o, head)
     shape = latents.shape
     return (owned.reshape(shape), fields.reshape(shape[1], shape[2], PLEV * OUTS), kv, query, out, pixels.T)

time: 96.2 us -> 96.9 us (level)
  no operation moved by 1% of the time
where the time goes in v7:
time: 96.9 us; the launch traced here: 96.6 us
  blocking collectives  35.6 us (37%)
  Pallas kernels  25.6 us (26%)
  starting transfers between devices  21.9 us (23%)
  waiting for transfers between devices  11.5 us (12%)
    pallas_call x7, Pallas kernels, close(): return run(*held)  25.6 us
    ppermute x6, starting transfers between devices, move(): return lax.ppermute(array, LAT + LON, route)  15.4 us
    all_to_all x1, blocking collectives, sum_over_all(): mine = add_up(lax.all_to_all(copies(mine, 'z'), 'z', 0, 0, tiled=True))  12.3 us
    all_to_all x1, blocking collectives, sum_over_all(): lax.all_to_all(mine.reshape(chips, rows // chips, width), PLANE, 0, 0, ti...  11.9 us
    all_to_all x1, blocking collectives, sum_over_all(): lax.all_to_all(copies(mine, PLANE), PLANE, 0, 0, tiled=True)  11.4 us
    ppermute x6, waiting for transfers between devices, move(): return lax.ppermute(array, LAT + LON, route)  8.84 us
    ppermute x2, starting transfers between devices, swap(): lax.ppermute(array, 'core', [(i, (i + 1) % count) for i in range(count)])  6.47 us
    ppermute x2, waiting for transfers between devices, swap(): lax.ppermute(array, 'core', [(i, (i + 1) % count) for i in range(count)])  2.7 us
  transfers between devices with their start and end apart: 8, of which 4 were waited for; matrix products, arithmetic and copies ran while one was open for 1% of the time, Pallas kernels for 6%

profile of v7, /device:TPU:1, one launch (start us, length us, event | category | flops | bytes accessed | tf_op | source)
XLA Modules:
  0.0 96.6 jit_solution(3726115707754109219)
XLA Ops:
  0.6 0.0 copy-start.2
  0.6 2.6 %shard_map.209 = (bf16[224,512]{1,0:T(8,128)(2,1)}, bf16[80,512]{1,0:T(8,128)(2,1)}, bf16[80,512]{1,0:T(8,128)(2,1)}) custom-call(bf16[576,512]{1,0:T(8,128)(2,1)} %bitcast.14, s32[6,24]{1,0:T(8,128)} %ids_ref.3, bf16[384,576]{1,0:T(8,128)(2,1)} %constant.40.clone.perm_ref, bf16[24,2048]{1,0:T(8,128)(2,1)} %constant.41.clone.columns_ref, ...), custom_call_target="tpu_custom_call" | custom-call | tf_op jit(solution)/shard_map/pallas_call | solution.py:392
  3.2 8.9 %collective-permute-start = (bf16[224,512]{1,0:T(8,128)(2,1)}, bf16[224,512]{1,0:T(8,128)(2,1)}, u32[]{:S(2)}, u32[]{:S(2)}) collective-permute-start(bf16[224,512]{1,0:T(8,128)(2,1)} %get-tuple-element.27), channel_id=1, source_target_pairs={{0,240},{1,241},{2,242},{3,243},{4,244},{5,245},{6,246},{7,247},{8... | collective-permute-start | bytes 688136 | tf_op jit(solution)/shard_map/ppermute | solution.py:412
  12.1 1.1 %collective-permute-start.1 = (bf16[80,512]{1,0:T(8,128)(2,1)}, bf16[80,512]{1,0:T(8,128)(2,1)}, u32[]{:S(2)}, u32[]{:S(2)}) collective-permute-start(bf16[80,512]{1,0:T(8,128)(2,1)} %get-tuple-element.28), channel_id=1, source_target_pairs={{0,255},{1,240},{2,241},{3,242},{4,243},{5,244},{6,245},{7,246},{8... | collective-permute-start | bytes 245768 | tf_op jit(solution)/shard_map/ppermute | solution.py:412
  13.2 2.6 %collective-permute-start.2 = (bf16[80,512]{1,0:T(8,128)(2,1)}, bf16[80,512]{1,0:T(8,128)(2,1)}, u32[]{:S(2)}, u32[]{:S(2)}) collective-permute-start(bf16[80,512]{1,0:T(8,128)(2,1)} %get-tuple-element.29), channel_id=1, source_target_pairs={{0,15},{1,0},{2,1},{3,2},{4,3},{5,4},{6,5},{7,6},{8,7},{9,8},{10,9... | collective-permute-start | bytes 245768 | tf_op jit(solution)/shard_map/ppermute | solution.py:412
  15.8 2.4 %shard_map.208.main_ref = bf16[224,512]{1,0:T(8,128)(2,1)} custom-call(bf16[576,512]{1,0:T(8,128)(2,1)} %bitcast.15, s32[6,24]{1,0:T(8,128)} %ids_ref.3, bf16[224,576]{1,0:T(8,128)(2,1)} %constant.43.clone.perm_ref, bf16[24,1024]{1,0:T(8,128)(2,1)} %constant.44.clone.columns_ref, f32[8,1024]{1,0:T(8,128)} %constant.45.clone.rows_ref), custom_call_target="tpu_custom_call" | custom-call | tf_op jit(solution)/shard_map/pallas_call | solution.py:392
  18.2 1.1 %collective-permute-done.1.corner_ref = bf16[80,512]{1,0:T(8,128)(2,1)} collective-permute-done((bf16[80,512]{1,0:T(8,128)(2,1)}, bf16[80,512]{1,0:T(8,128)(2,1)}, u32[]{:S(2)}, u32[]{:S(2)}) %collective-permute-start.1) | collective-permute-done | bytes 81952 | tf_op jit(solution)/shard_map/ppermute | solution.py:412
  19.3 0.0 collective-permute-done.2.west_ref
  19.3 0.0 collective-permute-done.north_ref
  19.3 0.0 copy-done.2
  19.3 5.7 %shard_map.210 = (bf16[224,512]{1,0:T(8,128)(2,1)}, bf16[224,512]{1,0:T(8,128)(2,1)}, bf16[80,512]{1,0:T(8,128)(2,1)}, bf16[80,512]{1,0:T(8,128)(2,1)}) custom-call(s32[1,1]{1,0:T(1,128)} %bitcast.1.flag_ref, f32[8,256]{1,0:T(8,128)} %constant.46.clone.extra_ref, bf16[224,512]{1,0:T(8,128)(2,1)} %shard_map.208.main_ref, ...), custom_call_target="tpu_custom_call" | custom-call | tf_op jit(solution)/shard_map/pallas_call | solution.py:392
  25.0 1.2 %collective-permute-start.3 = (bf16[224,512]{1,0:T(8,128)(2,1)}, bf16[224,512]{1,0:T(8,128)(2,1)S(1)}, u32[]{:S(2)}, u32[]{:S(2)}) collective-permute-start(bf16[224,512]{1,0:T(8,128)(2,1)} %get-tuple-element.31), channel_id=1, source_target_pairs={{0,16},{1,17},{2,18},{3,19},{4,20},{5,21},{6,22},{7,23},{8,24},{9,... | collective-permute-start | bytes 688136 | tf_op jit(solution)/shard_map/ppermute | solution.py:412
  26.2 0.0 collective-permute-start.4
  26.2 1.6 %collective-permute-start.5 = (bf16[80,512]{1,0:T(8,128)(2,1)}, bf16[80,512]{1,0:T(8,128)(2,1)S(1)}, u32[]{:S(2)}, u32[]{:S(2)}) collective-permute-start(bf16[80,512]{1,0:T(8,128)(2,1)} %get-tuple-element.33), channel_id=1, source_target_pairs={{0,1},{1,2},{2,3},{3,4},{4,5},{5,6},{6,7},{7,8},{8,9},{9,10},{10,1... | collective-permute-start | bytes 245768 | tf_op jit(solution)/shard_map/ppermute | solution.py:412
  27.9 0.9 pad.4.whead_ref
  28.8 0.0 copy-done
  28.8 0.0 copy-done.1
  28.8 3.3 %shard_map.211 = (bf16[13,144,128]{2,1,0:T(8,128)(2,1)S(1)}, bf16[13,144,512]{2,1,0:T(8,128)(2,1)S(1)}, f32[144,512]{1,0:T(8,128)S(1)}, bf16[512,128]{1,0:T(8,12...) custom-call(bf16[144,1040]{1,0:T(8,128)(2,1)S(1)} %bitcast.13, bf16[13,512]{1,0:T(8,128)(2,1)S(1)} %copy-done.4, ...), custom_call_target="tpu_custom_call" | custom-call | tf_op jit(solution)/shard_map/pallas_call | solution.py:392
  32.1 7.8 %collective-permute-done.4.corner_ref = bf16[80,512]{1,0:T(8,128)(2,1)S(1)} collective-permute-done((bf16[80,512]{1,0:T(8,128)(2,1)}, bf16[80,512]{1,0:T(8,128)(2,1)S(1)}, u32[]{:S(2)}, u32[]{:S(2)}) %collective-permute-start.4) | collective-permute-done | bytes 81952 | tf_op jit(solution)/shard_map/ppermute | solution.py:412
  39.9 0.0 collective-permute-done.5.west_ref
  39.9 0.0 collective-permute-done.3.north_ref
  39.9 7.6 %shard_map.212 = (bf16[576,512]{1,0:T(8,128)(2,1)}, bf16[144,1040]{1,0:T(8,128)(2,1)}, bf16[384,512]{1,0:T(8,128)(2,1)S(1)}, bf16[384,512]{1,0:T(8,128)(2,1)S(1)}) custom-call(s32[1,1]{1,0:T(1,128)} %bitcast.flag_ref, bf16[224,512]{1,0:T(8,128)(2,1)} %get-tuple-element.30.main_ref, bf16[224,512]{1,0:T(8,128)(2,1)S(1)} %collective-permute-done.3.north_ref, ...), custom_call_target="tpu_custom_call" | custom-call | tf_op jit(solution)/shard_map/pallas_call | solution.py:392
  47.5 2.2 %collective-permute-start.6 = (bf16[384,512]{1,0:T(8,128)(2,1)S(1)}, bf16[384,512]{1,0:T(8,128)(2,1)S(1)}, u32[]{:S(2)}, u32[]{:S(2)}) collective-permute-start(bf16[384,512]{1,0:T(8,128)(2,1)S(1)} %get-tuple-element.43), channel_id=1, source_target_pairs={{0,1},{1,0},{2,3},{3,2},{4,5},{5,4},{6,7},{7,6},{8,9},{9,8},{10,11... | collective-permute-start | bytes 1179656 | tf_op jit(solution)/shard_map/ppermute | solution.py:417
  49.7 1.3 %collective-permute-done.6.right_ref = bf16[384,512]{1,0:T(8,128)(2,1)S(1)} collective-permute-done((bf16[384,512]{1,0:T(8,128)(2,1)S(1)}, bf16[384,512]{1,0:T(8,128)(2,1)S(1)}, u32[]{:S(2)}, u32[]{:S(2)}) %collective-permute-start.6) | collective-permute-done | bytes 393248 | tf_op jit(solution)/shard_map/ppermute | solution.py:417
  51.0 0.1 shard_map.213
  51.1 11.9 %all_to_all.15 = bf16[16,24,512]{2,1,0:T(8,128)(2,1)S(1)} all-to-all(bf16[16,24,512]{2,1,0:T(8,128)(2,1)S(1)} %bitcast.10), channel_id=1, replica_groups=mesh['z'=8,'x_hi'=2,'x_lo'=2,'y'=4,'core'=2] {'x_hi','x_lo','y'}, dimensions={0} | all-to-all | bytes 786432 | tf_op jit(solution)/shard_map/all_to_all | solution.py:432
  63.0 0.1 reduce_sum.24
  63.1 12.3 %all_to_all.16 = bf16[8,24,512]{2,1,0:T(8,128)(2,1)S(1)} all-to-all(bf16[8,24,512]{2,1,0:T(8,128)(2,1)S(1)} %broadcast_in_dim.4), channel_id=1, replica_groups=mesh['z'=8,'x_hi'=2,'x_lo'=2,'y'=4,'core'=2] {'z'}, dimensions={0} | all-to-all | bytes 393216 | tf_op jit(solution)/shard_map/all_to_all | solution.py:433
  75.5 11.4 %all_to_all.17 = bf16[16,24,512]{2,1,0:T(8,128)(2,1)S(1)} all-to-all(bf16[16,24,512]{2,1,0:T(8,128)(2,1)S(1)} %broadcast_in_dim.5), channel_id=1, replica_groups=mesh['z'=8,'x_hi'=2,'x_lo'=2,'y'=4,'core'=2] {'x_hi','x_lo','y'}, dimensions={0} | all-to-all | bytes 786432 | tf_op jit(solution)/shard_map/all_to_all | solution.py:434
  86.9 4.3 %collective-permute-start.7 = (bf16[384,512]{1,0:T(8,128)(2,1)S(1)}, bf16[384,512]{1,0:T(8,128)(2,1)S(1)}, u32[]{:S(2)}, u32[]{:S(2)}) collective-permute-start(bf16[384,512]{1,0:T(8,128)(2,1)S(1)} %bitcast.11), channel_id=1, source_target_pairs={{0,1},{1,0},{2,3},{3,2},{4,5},{5,4},{6,7},{7,6},{8,9},{9,8},{10,11... | collective-permute-start | bytes 1179656 | tf_op jit(solution)/shard_map/ppermute | solution.py:417
  91.2 1.3 %collective-permute-done.7.other_ref = bf16[384,512]{1,0:T(8,128)(2,1)S(1)} collective-permute-done((bf16[384,512]{1,0:T(8,128)(2,1)S(1)}, bf16[384,512]{1,0:T(8,128)(2,1)S(1)}, u32[]{:S(2)}, u32[]{:S(2)}) %collective-permute-start.7) | collective-permute-done | bytes 393248 | tf_op jit(solution)/shard_map/ppermute | solution.py:417
  92.5 3.9 %shard_map.214 = (f32[512,1024]{1,0:T(8,128)}, f32[13,512]{1,0:T(8,128)}, f32[512,512]{1,0:T(8,128)}, f32[80,512]{1,0:T(8,128)}) custom-call(s32[1,1]{1,0:T(1,128)} %bitcast.flag_ref, bf16[384,512]{1,0:T(8,128)(2,1)S(1)} %bitcast.12, bf16[384,512]{1,0:T(8,128)(2,1)S(1)} %collective-permute-done.7.other_ref, bf16[512,1024]{1,0:T(8,128)(2,1)S(1)} %copy-done, ...), custom_call_target="tpu_custom_call" | custom-call | tf_op jit(solution)/shard_map/pallas_call | solution.py:392
  (9 shorter events, 0.1 us)
Async XLA Ops:
  0.6 18.7 %copy-start.2 = (bf16[512,1536]{1,0:T(8,128)(2,1)S(1)}, bf16[512,1536]{1,0:T(8,128)(2,1)}, u32[]{:S(2)}) copy-start(bf16[512,1536]{1,0:T(8,128)(2,1)} %wqkv_ref.1) | copy-start | bytes 4718596
  3.2 16.0 %collective-permute-start = (bf16[224,512]{1,0:T(8,128)(2,1)}, bf16[224,512]{1,0:T(8,128)(2,1)}, u32[]{:S(2)}, u32[]{:S(2)}) collective-permute-start(bf16[224,512]{1,0:T(8,128)(2,1)} %get-tuple-element.27), channel_id=1, source_target_pairs={{0,240},{1,241},{2,242},{3,243},{4,244},{5,245},{6,246},{7,247},{8... | collective-permute-start | bytes 688136 | tf_op jit(solution)/shard_map/ppermute | solution.py:412
  12.1 7.2 %collective-permute-start.1 = (bf16[80,512]{1,0:T(8,128)(2,1)}, bf16[80,512]{1,0:T(8,128)(2,1)}, u32[]{:S(2)}, u32[]{:S(2)}) collective-permute-start(bf16[80,512]{1,0:T(8,128)(2,1)} %get-tuple-element.28), channel_id=1, source_target_pairs={{0,255},{1,240},{2,241},{3,242},{4,243},{5,244},{6,245},{7,246},{8... | collective-permute-start | bytes 245768 | tf_op jit(solution)/shard_map/ppermute | solution.py:412
  13.2 6.1 %collective-permute-start.2 = (bf16[80,512]{1,0:T(8,128)(2,1)}, bf16[80,512]{1,0:T(8,128)(2,1)}, u32[]{:S(2)}, u32[]{:S(2)}) collective-permute-start(bf16[80,512]{1,0:T(8,128)(2,1)} %get-tuple-element.29), channel_id=1, source_target_pairs={{0,15},{1,0},{2,1},{3,2},{4,3},{5,4},{6,5},{7,6},{8,7},{9,8},{10,9... | collective-permute-start | bytes 245768 | tf_op jit(solution)/shard_map/ppermute | solution.py:412
  15.8 12.9 %copy-start = (bf16[512,1024]{1,0:T(8,128)(2,1)S(1)}, bf16[512,1024]{1,0:T(8,128)(2,1)}, u32[]{:S(2)}) copy-start(bf16[512,1024]{1,0:T(8,128)(2,1)} %wkv_ref.5) | copy-start | bytes 3145732
  15.8 12.9 %copy-start.1 = (bf16[512,512]{1,0:T(8,128)(2,1)S(1)}, bf16[512,512]{1,0:T(8,128)(2,1)}, u32[]{:S(2)}) copy-start(bf16[512,512]{1,0:T(8,128)(2,1)} %wo_ref.3) | copy-start | bytes 1572868
  15.8 13.0 %copy-start.3 = (bf16[6,24,1040]{2,1,0:T(8,128)(2,1)S(1)}, bf16[6,24,1040]{2,1,0:T(8,128)(2,1)}, u32[]{:S(2)}) copy-start(bf16[6,24,1040]{2,1,0:T(8,128)(2,1)} %param.25) | copy-start | bytes 898564
  15.8 13.0 %copy-start.4 = (bf16[13,512]{1,0:T(8,128)(2,1)S(1)}, bf16[13,512]{1,0:T(8,128)(2,1)}, u32[]{:S(2)}) copy-start(bf16[13,512]{1,0:T(8,128)(2,1)} %queries_ref.5) | copy-start | bytes 39940
  25.0 14.9 %collective-permute-start.3 = (bf16[224,512]{1,0:T(8,128)(2,1)}, bf16[224,512]{1,0:T(8,128)(2,1)S(1)}, u32[]{:S(2)}, u32[]{:S(2)}) collective-permute-start(bf16[224,512]{1,0:T(8,128)(2,1)} %get-tuple-element.31), channel_id=1, source_target_pairs={{0,16},{1,17},{2,18},{3,19},{4,20},{5,21},{6,22},{7,23},{8,24},{9,... | collective-permute-start | bytes 688136 | tf_op jit(solution)/shard_map/ppermute | solution.py:412
  26.2 13.6 %collective-permute-start.4 = (bf16[80,512]{1,0:T(8,128)(2,1)}, bf16[80,512]{1,0:T(8,128)(2,1)S(1)}, u32[]{:S(2)}, u32[]{:S(2)}) collective-permute-start(bf16[80,512]{1,0:T(8,128)(2,1)} %get-tuple-element.32), channel_id=1, source_target_pairs={{0,17},{1,18},{2,19},{3,20},{4,21},{5,22},{6,23},{7,24},{8,25},{9,... | collective-permute-start | bytes 245768 | tf_op jit(solution)/shard_map/ppermute | solution.py:412
  26.2 13.6 %collective-permute-start.5 = (bf16[80,512]{1,0:T(8,128)(2,1)}, bf16[80,512]{1,0:T(8,128)(2,1)S(1)}, u32[]{:S(2)}, u32[]{:S(2)}) collective-permute-start(bf16[80,512]{1,0:T(8,128)(2,1)} %get-tuple-element.33), channel_id=1, source_target_pairs={{0,1},{1,2},{2,3},{3,4},{4,5},{5,6},{6,7},{7,8},{8,9},{9,10},{10,1... | collective-permute-start | bytes 245768 | tf_op jit(solution)/shard_map/ppermute | solution.py:412
  47.5 3.5 %collective-permute-start.6 = (bf16[384,512]{1,0:T(8,128)(2,1)S(1)}, bf16[384,512]{1,0:T(8,128)(2,1)S(1)}, u32[]{:S(2)}, u32[]{:S(2)}) collective-permute-start(bf16[384,512]{1,0:T(8,128)(2,1)S(1)} %get-tuple-element.43), channel_id=1, source_target_pairs={{0,1},{1,0},{2,3},{3,2},{4,5},{5,4},{6,7},{7,6},{8,9},{9,8},{10,11... | collective-permute-start | bytes 1179656 | tf_op jit(solution)/shard_map/ppermute | solution.py:417
  86.9 5.6 %collective-permute-start.7 = (bf16[384,512]{1,0:T(8,128)(2,1)S(1)}, bf16[384,512]{1,0:T(8,128)(2,1)S(1)}, u32[]{:S(2)}, u32[]{:S(2)}) collective-permute-start(bf16[384,512]{1,0:T(8,128)(2,1)S(1)} %bitcast.11), channel_id=1, source_target_pairs={{0,1},{1,0},{2,3},{3,2},{4,5},{5,4},{6,7},{7,6},{8,9},{9,8},{10,11... | collective-permute-start | bytes 1179656 | tf_op jit(solution)/shard_map/ppermute | solution.py:417

commit v8 on v7

--- a/solution.py
+++ b/solution.py
@@ -124,6 +124,11 @@
         bottom = jnp.concatenate([bottom, jnp.zeros((16, D - SPAN), F32)], axis=1)
         ref[: height - 16] = packed[: height - 16].astype(BF)
         ref[height - 16 :] = (packed[height - 16 :] + bottom).astype(BF)
+
+
+def own_kernel(x_ref, ids_ref, perm_ref, columns_ref, rows_ref, wout_ref, main_ref, wout_out):
+    wout_out[...] = wout_ref[...]
+    pack_kernel(PIECES[:1], x_ref, ids_ref, perm_ref, columns_ref, rows_ref, main_ref)
 
 
 def attention_kernel(
@@ -219,9 +224,11 @@
 
 
 def pre_kernel(
-    cot_ref, queries_ref, wo_ref, whead_ref, wkv_ref,
-    up_ref, dctx_ref, dsum_ref, map_ref, base_ref, wv_ref,
+    cot_ref, queries_ref, wo_ref, whead_ref, wkv_ref, main_ref, main_perm, far_perm,
+    up_ref, dctx_ref, dsum_ref, map_ref, base_ref, wv_ref, own_ref, far_perm_out,
 ):
+    own_ref[...] = mm(main_perm[...], main_ref[...]).astype(BF)
+    far_perm_out[...] = far_perm[...]
     order = feature_order()
     wv_ref[...] = mm(wkv_ref[:, D:], order).astype(BF)
     head = whead_ref[...]
@@ -243,14 +250,13 @@
 
 
 def decode_kernel(
-    flag_ref, main_ref, north_ref, corner_ref, west_ref, perm_ref, wkv_ref, queries_ref, up_ref, dctx_ref, dsum_ref,
+    flag_ref, own_ref, north_ref, corner_ref, west_ref, perm_ref, wkv_ref, queries_ref, up_ref, dctx_ref, dsum_ref,
     map_ref, base_ref, wv_ref,
     owned_ref, fields_ref, keep_ref, send_ref,
     value, weights, dvalues, context, products, fields, sums, owned, decoded_out, sems,
 ):
-    pieces = (main_ref, north_ref, corner_ref, west_ref)
-    packed = jnp.concatenate([ref[...] for ref in pieces], axis=0)
-    wide = mm(perm_ref[...], packed)
+    far = jnp.concatenate([ref[...] for ref in (north_ref, corner_ref, west_ref)], axis=0)
+    wide = own_ref[...].astype(F32) + mm(perm_ref[...], far)
     owned[...] = wide.astype(BF)
     owned_copy = pltpu.make_async_copy(owned, owned_ref, sems.at[0])
     owned_copy.start()
@@ -328,7 +334,7 @@
     out_ref[...] = (left_ref[...].astype(F32) + right_ref[...].astype(F32)).astype(BF)
 
 
-def final_kernel(flag_ref, mine_ref, other_ref, wkv_ref, queries_ref, wo_ref, whead_ref, kv_ref, query_ref, o_ref, head_ref, kv, o, sems):
+def final_kernel(flag_ref, mine_ref, other_ref, wkv_ref, queries_ref, wo_ref, whead_ref, kv_ref, query_ref, o_ref, head_ref):
     second = flag_ref[0, 0] > 0
     mine, other = mine_ref[...].astype(F32), other_ref[...].astype(F32)
     sums = jnp.concatenate([jnp.where(second, other, mine), jnp.where(second, mine, other)], axis=0).astype(BF)
@@ -354,21 +360,11 @@
     squares = squares + jnp.sum(out * out) + jnp.sum(pixels * pixels)
     limit = math.sqrt(2 * D * D + PLEV * D + D * D + D * OUTS)
     factor = jnp.minimum(1.0, limit * lax.rsqrt(jnp.full((1, 1), squares + clip_eps, F32)))
-    values_half, keys_half = (slice(None), slice(D, None)), (slice(None), slice(None, D))
-    kv[values_half] = values * factor
-    values_copy = pltpu.make_async_copy(kv.at[values_half], kv_ref.at[values_half], sems.at[0])
-    values_copy.start()
-    kv[keys_half] = keys * factor
-    keys_copy = pltpu.make_async_copy(kv.at[keys_half], kv_ref.at[keys_half], sems.at[1])
-    keys_copy.start()
-    o[...] = out * factor
-    o_copy = pltpu.make_async_copy(o, o_ref, sems.at[2])
-    o_copy.start()
+    kv_ref[:, :D] = keys * factor
+    kv_ref[:, D:] = values * factor
     query_ref[...] = level * factor
+    o_ref[...] = out * factor
     head_ref[...] = pixels * factor
-    values_copy.wait()
-    keys_copy.wait()
-    o_copy.wait()
 
 
 def call(kernel, outs, spaces, scratch=(), limit=40, out_specs=None):
@@ -445,12 +441,25 @@
     north, corner, west = call(functools.partial(pack_kernel, PIECES[1:]), shapes[1:], "HHHHH", limit=56)(
         flat, mask_ids, jnp.asarray(perm[MAIN:], BF), jnp.asarray(columns[:, split:], BF), jnp.asarray(rows[:, split:])
     )
-    (main,) = call(functools.partial(pack_kernel, PIECES[:1]), shapes[:1], "HHHHH", limit=56)(
-        flat, mask_ids, jnp.asarray(perm[:MAIN], BF), jnp.asarray(columns[:, :split], BF), jnp.asarray(rows[:, :split])
+    main, w_out = call(own_kernel, [struct((MAIN, D)), struct((D, D))], "HHHHHH", limit=40)(
+        flat,
+        mask_ids,
+        jnp.asarray(perm[:MAIN], BF),
+        jnp.asarray(columns[:, :split], BF),
+        jnp.asarray(rows[:, :split]),
+        w_out,
     )
     north, corner, west = move(north, -1, 0), move(corner, -1, -1), move(west, 0, -1)
     head = jnp.pad(w_head.T, ((0, LANES - OUTS), (0, 0)))
-    up, dctx, dsum, both, base, wv = call(
+    main, north, corner, west = call(
+        attention_kernel,
+        shapes,
+        "SHVHHHVV",
+        [pltpu.VMEM((PACKED, 3 * D), F32), pltpu.VMEM((PACKED, D), F32)],
+        limit=48,
+    )(flag, jnp.asarray(extra), main, north, corner, west, w_qkv, w_out)
+    north, corner, west = move(north, 1, 0), move(corner, 1, 1), move(west, 0, 1)
+    up, dctx, dsum, both, base, wv, own, far_perm = call(
         pre_kernel,
         [
             struct((PLEV, PATCHES, LANES)),
@@ -459,23 +468,26 @@
             struct((D, LANES)),
             struct((16, LANES), F32),
             struct((D, D)),
+            struct((TOKENS, D)),
+            struct((TOKENS, PACKED - MAIN)),
         ],
-        "VVVVV",
-    )(field_cotangent.reshape(PATCHES, PLEV * OUTS), level_queries, w_o, head, w_kv)
-    main, north, corner, west = call(
-        attention_kernel,
-        shapes,
-        "SHHHHHVH",
-        [pltpu.VMEM((PACKED, 3 * D), F32), pltpu.VMEM((PACKED, D), F32)],
-        limit=48,
-    )(flag, jnp.asarray(extra), main, north, corner, west, w_qkv, w_out)
-    north, corner, west = move(north, 1, 0), move(corner, 1, 1), move(west, 0, 1)
+        "VVVVVHHH",
+    )(
+        field_cotangent.reshape(PATCHES, PLEV * OUTS),
+        level_queries,
+        w_o,
+        head,
+        w_kv,
+        main,
+        jnp.asarray(perm[:MAIN].T, BF),
+        jnp.asarray(perm[MAIN:].T, BF),
+    )
     core = lax.axis_index("core").astype(jnp.int32).reshape(1, 1)
     share = struct((ROWS // 2, D))
     owned, fields, keep, send = call(
         decode_kernel,
         [struct((TOKENS, D)), struct((PATCHES, PLEV * OUTS)), share, share],
-        "SHVVVHVVVVVVVV",
+        "SVVVVVVVVVVVVV",
         [
             pltpu.VMEM((TOKENS, D), F32),
             pltpu.VMEM((TOKENS, LANES), F32),
@@ -489,14 +501,12 @@
             pltpu.SemaphoreType.DMA((2,)),
         ],
         out_specs=[pl.BlockSpec(memory_space=pl.ANY)] * 2 + [pl.BlockSpec(memory_space=pltpu.VMEM)] * 2,
-    )(core, main, north, corner, west, jnp.asarray(perm.T, BF), w_kv, level_queries, up, dctx, dsum, both, base, wv)
+    )(core, own, north, corner, west, far_perm, w_kv, level_queries, up, dctx, dsum, both, base, wv)
     mine, other = sum_over_all(keep, send)
     kv, query, out, pixels = call(
         final_kernel,
         [struct((D, 2 * D), F32), struct((PLEV, D), F32), struct((D, D), F32), struct((OUTS, D), F32)],
         "SVVVVVV",
-        [pltpu.VMEM((D, 2 * D), F32), pltpu.VMEM((D, D), F32), pltpu.SemaphoreType.DMA((3,))],
-        out_specs=[pl.BlockSpec(memory_space=space) for space in (pl.ANY, pltpu.VMEM, pl.ANY, pltpu.VMEM)],
     )(core, mine, other, w_kv, level_queries, w_o, head)
     shape = latents.shape
     return (owned.reshape(shape), fields.reshape(shape[1], shape[2], PLEV * OUTS), kv, query, out, pixels.T)

time: 96.9 us -> 94.7 us (0.977)
  Pallas kernels: 25.6 us -> 24.4 us
    pallas_call x7, Pallas kernels: 25.6 us -> 24.4 us  [close(): return run(*held)]
  transfers between devices with their start and end apart: 8 -> 8, of which waited for: 4 -> 4; matrix products, arithmetic and copies ran while one was open for 1% -> 1% of each run, Pallas kernels for 6% -> 7%
where the time goes in v8:
time: 94.7 us; the launch traced here: 94.4 us
  blocking collectives  35.7 us (38%)
  Pallas kernels  24.4 us (26%)
  starting transfers between devices  21.9 us (23%)
  waiting for transfers between devices  10.7 us (11%)
  local copies, waits for them, and re-layouts  0.96 us (1%)
    pallas_call x7, Pallas kernels, close(): return run(*held)  24.4 us
    ppermute x6, starting transfers between devices, move(): return lax.ppermute(array, LAT + LON, route)  15.4 us
    all_to_all x1, blocking collectives, sum_over_all(): mine = add_up(lax.all_to_all(copies(mine, 'z'), 'z', 0, 0, tiled=True))  12.3 us
    all_to_all x1, blocking collectives, sum_over_all(): lax.all_to_all(mine.reshape(chips, rows // chips, width), PLANE, 0, 0, ti...  11.9 us
    all_to_all x1, blocking collectives, sum_over_all(): lax.all_to_all(copies(mine, PLANE), PLANE, 0, 0, tiled=True)  11.4 us
    ppermute x6, waiting for transfers between devices, move(): return lax.ppermute(array, LAT + LON, route)  7.96 us
    ppermute x2, starting transfers between devices, swap(): lax.ppermute(array, 'core', [(i, (i + 1) % count) for i in range(count)])  6.47 us
    ppermute x2, waiting for transfers between devices, swap(): lax.ppermute(array, 'core', [(i, (i + 1) % count) for i in range(count)])  2.7 us
  transfers between devices with their start and end apart: 8, of which 4 were waited for; matrix products, arithmetic and copies ran while one was open for 1% of the time, Pallas kernels for 7%

profile of v8, /device:TPU:1, one launch (start us, length us, event | category | flops | bytes accessed | tf_op | source)
XLA Modules:
  0.0 94.4 jit_solution(13160385357690556743)
XLA Ops:
  0.6 0.0 copy-start.2
  0.6 2.6 %shard_map.218 = (bf16[224,512]{1,0:T(8,128)(2,1)}, bf16[80,512]{1,0:T(8,128)(2,1)}, bf16[80,512]{1,0:T(8,128)(2,1)}) custom-call(bf16[576,512]{1,0:T(8,128)(2,1)} %bitcast.14, s32[6,24]{1,0:T(8,128)} %ids_ref.3, bf16[384,576]{1,0:T(8,128)(2,1)} %constant.42.clone.perm_ref, bf16[24,2048]{1,0:T(8,128)(2,1)} %constant.43.clone.columns_ref, ...), custom_call_target="tpu_custom_call" | custom-call | tf_op jit(solution)/shard_map/pallas_call | solution.py:388
  3.2 8.9 %collective-permute-start = (bf16[224,512]{1,0:T(8,128)(2,1)}, bf16[224,512]{1,0:T(8,128)(2,1)}, u32[]{:S(2)}, u32[]{:S(2)}) collective-permute-start(bf16[224,512]{1,0:T(8,128)(2,1)} %get-tuple-element.32), channel_id=1, source_target_pairs={{0,240},{1,241},{2,242},{3,243},{4,244},{5,245},{6,246},{7,247},{8... | collective-permute-start | bytes 688136 | tf_op jit(solution)/shard_map/ppermute | solution.py:408
  12.1 1.1 %collective-permute-start.1 = (bf16[80,512]{1,0:T(8,128)(2,1)}, bf16[80,512]{1,0:T(8,128)(2,1)}, u32[]{:S(2)}, u32[]{:S(2)}) collective-permute-start(bf16[80,512]{1,0:T(8,128)(2,1)} %get-tuple-element.33), channel_id=1, source_target_pairs={{0,255},{1,240},{2,241},{3,242},{4,243},{5,244},{6,245},{7,246},{8... | collective-permute-start | bytes 245768 | tf_op jit(solution)/shard_map/ppermute | solution.py:408
  13.2 2.6 %collective-permute-start.2 = (bf16[80,512]{1,0:T(8,128)(2,1)}, bf16[80,512]{1,0:T(8,128)(2,1)}, u32[]{:S(2)}, u32[]{:S(2)}) collective-permute-start(bf16[80,512]{1,0:T(8,128)(2,1)} %get-tuple-element.34), channel_id=1, source_target_pairs={{0,15},{1,0},{2,1},{3,2},{4,3},{5,4},{6,5},{7,6},{8,7},{9,8},{10,9... | collective-permute-start | bytes 245768 | tf_op jit(solution)/shard_map/ppermute | solution.py:408
  15.8 1.9 %shard_map.217 = (bf16[224,512]{1,0:T(8,128)(2,1)S(1)}, bf16[512,512]{1,0:T(8,128)(2,1)S(1)}) custom-call(bf16[576,512]{1,0:T(8,128)(2,1)} %bitcast.15, s32[6,24]{1,0:T(8,128)} %ids_ref.3, bf16[224,576]{1,0:T(8,128)(2,1)} %constant.45.clone.perm_ref, bf16[24,1024]{1,0:T(8,128)(2,1)} %constant.46.clone.columns_ref, f32[8,1024]{1,0:T(8,128)} %constant.47.clone.rows_ref, ...), custom_call_target="tpu_custom_call" | custom-call | tf_op jit(solution)/shard_map/pallas_call | solution.py:388
  17.7 1.6 %collective-permute-done.1.corner_ref = bf16[80,512]{1,0:T(8,128)(2,1)} collective-permute-done((bf16[80,512]{1,0:T(8,128)(2,1)}, bf16[80,512]{1,0:T(8,128)(2,1)}, u32[]{:S(2)}, u32[]{:S(2)}) %collective-permute-start.1) | collective-permute-done | bytes 81952 | tf_op jit(solution)/shard_map/ppermute | solution.py:408
  19.3 0.0 collective-permute-done.2.west_ref
  19.3 0.0 collective-permute-done.north_ref
  19.3 0.0 copy-done.2
  19.3 5.4 %shard_map.219 = (bf16[224,512]{1,0:T(8,128)(2,1)}, bf16[224,512]{1,0:T(8,128)(2,1)}, bf16[80,512]{1,0:T(8,128)(2,1)}, bf16[80,512]{1,0:T(8,128)(2,1)}) custom-call(s32[1,1]{1,0:T(1,128)} %bitcast.3.flag_ref, f32[8,256]{1,0:T(8,128)} %constant.48.clone.extra_ref, bf16[224,512]{1,0:T(8,128)(2,1)S(1)} %get-tuple-element.31.main_ref, ...), custom_call_target="tpu_custom_call" | custom-call | tf_op jit(solution)/shard_map/pallas_call | solution.py:388
  24.7 1.2 %collective-permute-start.3 = (bf16[224,512]{1,0:T(8,128)(2,1)}, bf16[224,512]{1,0:T(8,128)(2,1)S(1)}, u32[]{:S(2)}, u32[]{:S(2)}) collective-permute-start(bf16[224,512]{1,0:T(8,128)(2,1)} %get-tuple-element.38), channel_id=1, source_target_pairs={{0,16},{1,17},{2,18},{3,19},{4,20},{5,21},{6,22},{7,23},{8,24},{9,... | collective-permute-start | bytes 688136 | tf_op jit(solution)/shard_map/ppermute | solution.py:408
  25.9 0.0 collective-permute-start.4
  25.9 1.6 %collective-permute-start.5 = (bf16[80,512]{1,0:T(8,128)(2,1)}, bf16[80,512]{1,0:T(8,128)(2,1)S(1)}, u32[]{:S(2)}, u32[]{:S(2)}) collective-permute-start(bf16[80,512]{1,0:T(8,128)(2,1)} %get-tuple-element.40), channel_id=1, source_target_pairs={{0,1},{1,2},{2,3},{3,4},{4,5},{5,6},{6,7},{7,8},{8,9},{9,10},{10,1... | collective-permute-start | bytes 245768 | tf_op jit(solution)/shard_map/ppermute | solution.py:408
  27.5 0.9 pad.4.whead_ref
  28.4 0.0 copy-done
  28.5 0.0 copy-done.1
  28.5 4.7 %shard_map.220 = (bf16[13,144,128]{2,1,0:T(8,128)(2,1)S(1)}, bf16[13,144,512]{2,1,0:T(8,128)(2,1)S(1)}, f32[144,512]{1,0:T(8,128)S(1)}, bf16[512,128]{1,0:T(8,12...) custom-call(bf16[144,1040]{1,0:T(8,128)(2,1)S(1)} %bitcast.13, ...), custom_call_target="tpu_custom_call" | custom-call | tf_op jit(solution)/shard_map/pallas_call | solution.py:388
  33.2 6.4 %collective-permute-done.4.corner_ref = bf16[80,512]{1,0:T(8,128)(2,1)S(1)} collective-permute-done((bf16[80,512]{1,0:T(8,128)(2,1)}, bf16[80,512]{1,0:T(8,128)(2,1)S(1)}, u32[]{:S(2)}, u32[]{:S(2)}) %collective-permute-start.4) | collective-permute-done | bytes 81952 | tf_op jit(solution)/shard_map/ppermute | solution.py:408
  39.6 0.0 collective-permute-done.5.west_ref
  39.6 0.0 collective-permute-done.3.north_ref
  39.6 6.4 %shard_map.221 = (bf16[576,512]{1,0:T(8,128)(2,1)}, bf16[144,1040]{1,0:T(8,128)(2,1)}, bf16[384,512]{1,0:T(8,128)(2,1)S(1)}, bf16[384,512]{1,0:T(8,128)(2,1)S(1)}) custom-call(s32[1,1]{1,0:T(1,128)} %bitcast.flag_ref, bf16[576,512]{1,0:T(8,128)(2,1)S(1)} %get-tuple-element.37.own_ref, bf16[224,512]{1,0:T(8,128)(2,1)S(1)} %collective-permute-done.3.north_ref, ...), custom_call_target="tpu_custom_call" | custom-call | tf_op jit(solution)/shard_map/pallas_call | solution.py:388
  46.0 2.2 %collective-permute-start.6 = (bf16[384,512]{1,0:T(8,128)(2,1)S(1)}, bf16[384,512]{1,0:T(8,128)(2,1)S(1)}, u32[]{:S(2)}, u32[]{:S(2)}) collective-permute-start(bf16[384,512]{1,0:T(8,128)(2,1)S(1)} %get-tuple-element.51), channel_id=1, source_target_pairs={{0,1},{1,0},{2,3},{3,2},{4,5},{5,4},{6,7},{7,6},{8,9},{9,8},{10,11... | collective-permute-start | bytes 1179656 | tf_op jit(solution)/shard_map/ppermute | solution.py:413
  48.2 1.3 %collective-permute-done.6.right_ref = bf16[384,512]{1,0:T(8,128)(2,1)S(1)} collective-permute-done((bf16[384,512]{1,0:T(8,128)(2,1)S(1)}, bf16[384,512]{1,0:T(8,128)(2,1)S(1)}, u32[]{:S(2)}, u32[]{:S(2)}) %collective-permute-start.6) | collective-permute-done | bytes 393248 | tf_op jit(solution)/shard_map/ppermute | solution.py:413
  49.5 0.1 shard_map.222
  49.6 11.9 %all_to_all.15 = bf16[16,24,512]{2,1,0:T(8,128)(2,1)S(1)} all-to-all(bf16[16,24,512]{2,1,0:T(8,128)(2,1)S(1)} %bitcast.10), channel_id=1, replica_groups=mesh['z'=8,'x_hi'=2,'x_lo'=2,'y'=4,'core'=2] {'x_hi','x_lo','y'}, dimensions={0} | all-to-all | bytes 786432 | tf_op jit(solution)/shard_map/all_to_all | solution.py:428
  61.6 0.1 reduce_sum.24
  61.7 12.3 %all_to_all.16 = bf16[8,24,512]{2,1,0:T(8,128)(2,1)S(1)} all-to-all(bf16[8,24,512]{2,1,0:T(8,128)(2,1)S(1)} %broadcast_in_dim.4), channel_id=1, replica_groups=mesh['z'=8,'x_hi'=2,'x_lo'=2,'y'=4,'core'=2] {'z'}, dimensions={0} | all-to-all | bytes 393216 | tf_op jit(solution)/shard_map/all_to_all | solution.py:429
  74.0 11.4 %all_to_all.17 = bf16[16,24,512]{2,1,0:T(8,128)(2,1)S(1)} all-to-all(bf16[16,24,512]{2,1,0:T(8,128)(2,1)S(1)} %broadcast_in_dim.5), channel_id=1, replica_groups=mesh['z'=8,'x_hi'=2,'x_lo'=2,'y'=4,'core'=2] {'x_hi','x_lo','y'}, dimensions={0} | all-to-all | bytes 786432 | tf_op jit(solution)/shard_map/all_to_all | solution.py:430
  85.4 4.3 %collective-permute-start.7 = (bf16[384,512]{1,0:T(8,128)(2,1)S(1)}, bf16[384,512]{1,0:T(8,128)(2,1)S(1)}, u32[]{:S(2)}, u32[]{:S(2)}) collective-permute-start(bf16[384,512]{1,0:T(8,128)(2,1)S(1)} %bitcast.11), channel_id=1, source_target_pairs={{0,1},{1,0},{2,3},{3,2},{4,5},{5,4},{6,7},{7,6},{8,9},{9,8},{10,11... | collective-permute-start | bytes 1179656 | tf_op jit(solution)/shard_map/ppermute | solution.py:413
  89.7 1.3 %collective-permute-done.7.other_ref = bf16[384,512]{1,0:T(8,128)(2,1)S(1)} collective-permute-done((bf16[384,512]{1,0:T(8,128)(2,1)S(1)}, bf16[384,512]{1,0:T(8,128)(2,1)S(1)}, u32[]{:S(2)}, u32[]{:S(2)}) %collective-permute-start.7) | collective-permute-done | bytes 393248 | tf_op jit(solution)/shard_map/ppermute | solution.py:413
  91.1 3.3 %shard_map.223 = (f32[512,1024]{1,0:T(8,128)}, f32[13,512]{1,0:T(8,128)}, f32[512,512]{1,0:T(8,128)}, f32[80,512]{1,0:T(8,128)}) custom-call(s32[1,1]{1,0:T(1,128)} %bitcast.flag_ref, bf16[384,512]{1,0:T(8,128)(2,1)S(1)} %bitcast.12, bf16[384,512]{1,0:T(8,128)(2,1)S(1)} %collective-permute-done.7.other_ref, bf16[512,1024]{1,0:T(8,128)(2,1)S(1)} %copy-done, ...), custom_call_target="tpu_custom_call" | custom-call | tf_op jit(solution)/shard_map/pallas_call | solution.py:388
  (9 shorter events, 0.1 us)
Async XLA Ops:
  0.6 18.7 %copy-start.2 = (bf16[512,1536]{1,0:T(8,128)(2,1)S(1)}, bf16[512,1536]{1,0:T(8,128)(2,1)}, u32[]{:S(2)}) copy-start(bf16[512,1536]{1,0:T(8,128)(2,1)} %wqkv_ref.1) | copy-start | bytes 4718596
  3.2 16.0 %collective-permute-start = (bf16[224,512]{1,0:T(8,128)(2,1)}, bf16[224,512]{1,0:T(8,128)(2,1)}, u32[]{:S(2)}, u32[]{:S(2)}) collective-permute-start(bf16[224,512]{1,0:T(8,128)(2,1)} %get-tuple-element.32), channel_id=1, source_target_pairs={{0,240},{1,241},{2,242},{3,243},{4,244},{5,245},{6,246},{7,247},{8... | collective-permute-start | bytes 688136 | tf_op jit(solution)/shard_map/ppermute | solution.py:408
  12.1 7.2 %collective-permute-start.1 = (bf16[80,512]{1,0:T(8,128)(2,1)}, bf16[80,512]{1,0:T(8,128)(2,1)}, u32[]{:S(2)}, u32[]{:S(2)}) collective-permute-start(bf16[80,512]{1,0:T(8,128)(2,1)} %get-tuple-element.33), channel_id=1, source_target_pairs={{0,255},{1,240},{2,241},{3,242},{4,243},{5,244},{6,245},{7,246},{8... | collective-permute-start | bytes 245768 | tf_op jit(solution)/shard_map/ppermute | solution.py:408
  13.2 6.1 %collective-permute-start.2 = (bf16[80,512]{1,0:T(8,128)(2,1)}, bf16[80,512]{1,0:T(8,128)(2,1)}, u32[]{:S(2)}, u32[]{:S(2)}) collective-permute-start(bf16[80,512]{1,0:T(8,128)(2,1)} %get-tuple-element.34), channel_id=1, source_target_pairs={{0,15},{1,0},{2,1},{3,2},{4,3},{5,4},{6,5},{7,6},{8,7},{9,8},{10,9... | collective-permute-start | bytes 245768 | tf_op jit(solution)/shard_map/ppermute | solution.py:408
  15.8 12.6 %copy-start = (bf16[512,1024]{1,0:T(8,128)(2,1)S(1)}, bf16[512,1024]{1,0:T(8,128)(2,1)}, u32[]{:S(2)}) copy-start(bf16[512,1024]{1,0:T(8,128)(2,1)} %wkv_ref.5) | copy-start | bytes 3145732
  15.8 12.6 %copy-start.1 = (bf16[512,512]{1,0:T(8,128)(2,1)S(1)}, bf16[512,512]{1,0:T(8,128)(2,1)}, u32[]{:S(2)}) copy-start(bf16[512,512]{1,0:T(8,128)(2,1)} %wo_ref.3) | copy-start | bytes 1572868
  15.8 12.6 %copy-start.3 = (bf16[6,24,1040]{2,1,0:T(8,128)(2,1)S(1)}, bf16[6,24,1040]{2,1,0:T(8,128)(2,1)}, u32[]{:S(2)}) copy-start(bf16[6,24,1040]{2,1,0:T(8,128)(2,1)} %param.26) | copy-start | bytes 898564
  15.8 12.6 %copy-start.4 = (bf16[13,512]{1,0:T(8,128)(2,1)S(1)}, bf16[13,512]{1,0:T(8,128)(2,1)}, u32[]{:S(2)}) copy-start(bf16[13,512]{1,0:T(8,128)(2,1)} %queries_ref.5) | copy-start | bytes 39940
  24.7 14.9 %collective-permute-start.3 = (bf16[224,512]{1,0:T(8,128)(2,1)}, bf16[224,512]{1,0:T(8,128)(2,1)S(1)}, u32[]{:S(2)}, u32[]{:S(2)}) collective-permute-start(bf16[224,512]{1,0:T(8,128)(2,1)} %get-tuple-element.38), channel_id=1, source_target_pairs={{0,16},{1,17},{2,18},{3,19},{4,20},{5,21},{6,22},{7,23},{8,24},{9,... | collective-permute-start | bytes 688136 | tf_op jit(solution)/shard_map/ppermute | solution.py:408
  25.9 13.6 %collective-permute-start.4 = (bf16[80,512]{1,0:T(8,128)(2,1)}, bf16[80,512]{1,0:T(8,128)(2,1)S(1)}, u32[]{:S(2)}, u32[]{:S(2)}) collective-permute-start(bf16[80,512]{1,0:T(8,128)(2,1)} %get-tuple-element.39), channel_id=1, source_target_pairs={{0,17},{1,18},{2,19},{3,20},{4,21},{5,22},{6,23},{7,24},{8,25},{9,... | collective-permute-start | bytes 245768 | tf_op jit(solution)/shard_map/ppermute | solution.py:408
  25.9 13.6 %collective-permute-start.5 = (bf16[80,512]{1,0:T(8,128)(2,1)}, bf16[80,512]{1,0:T(8,128)(2,1)S(1)}, u32[]{:S(2)}, u32[]{:S(2)}) collective-permute-start(bf16[80,512]{1,0:T(8,128)(2,1)} %get-tuple-element.40), channel_id=1, source_target_pairs={{0,1},{1,2},{2,3},{3,4},{4,5},{5,6},{6,7},{7,8},{8,9},{9,10},{10,1... | collective-permute-start | bytes 245768 | tf_op jit(solution)/shard_map/ppermute | solution.py:408
  46.0 3.5 %collective-permute-start.6 = (bf16[384,512]{1,0:T(8,128)(2,1)S(1)}, bf16[384,512]{1,0:T(8,128)(2,1)S(1)}, u32[]{:S(2)}, u32[]{:S(2)}) collective-permute-start(bf16[384,512]{1,0:T(8,128)(2,1)S(1)} %get-tuple-element.51), channel_id=1, source_target_pairs={{0,1},{1,0},{2,3},{3,2},{4,5},{5,4},{6,7},{7,6},{8,9},{9,8},{10,11... | collective-permute-start | bytes 1179656 | tf_op jit(solution)/shard_map/ppermute | solution.py:413
  85.4 5.6 %collective-permute-start.7 = (bf16[384,512]{1,0:T(8,128)(2,1)S(1)}, bf16[384,512]{1,0:T(8,128)(2,1)S(1)}, u32[]{:S(2)}, u32[]{:S(2)}) collective-permute-start(bf16[384,512]{1,0:T(8,128)(2,1)S(1)} %bitcast.11), channel_id=1, source_target_pairs={{0,1},{1,0},{2,3},{3,2},{4,5},{5,4},{6,7},{7,6},{8,9},{9,8},{10,11... | collective-permute-start | bytes 1179656 | tf_op jit(solution)/shard_map/ppermute | solution.py:413

commit v9 on v8

--- a/solution.py
+++ b/solution.py
@@ -226,7 +226,13 @@
 def pre_kernel(
     cot_ref, queries_ref, wo_ref, whead_ref, wkv_ref, main_ref, main_perm, far_perm,
     up_ref, dctx_ref, dsum_ref, map_ref, base_ref, wv_ref, own_ref, far_perm_out,
+    spread_ref, gather_ref, shift_ref, totals_ref,
 ):
+    spread_ref[...] = spread_queries(queries_ref[...].astype(F32)).astype(BF)
+    row = lax.broadcasted_iota(jnp.int32, (PLEV * LANES, LANES), 0)
+    c = lax.broadcasted_iota(jnp.int32, (PLEV * LANES, LANES), 1)
+    gather_ref[...] = jnp.where(row // 16 == c, 1.0, 0.0).astype(BF)
+    shift_ref[...] = shift_matrix(LANES, 3 * LANES)
     own_ref[...] = mm(main_perm[...], main_ref[...]).astype(BF)
     far_perm_out[...] = far_perm[...]
     order = feature_order()
@@ -238,20 +244,25 @@
     base_ref[...] = jnp.concatenate(
         [dot(queries_ref[...], head, ((1,), (1,))), jnp.zeros((16 - PLEV, LANES), F32)], axis=0
     )
+    totals = []
     dsum = jnp.zeros((PATCHES, D), F32)
     for level in range(PLEV):
         first, offset, width = spot(level)
-        up = mm(cot_ref[:, first : first + width], shift_matrix(offset, width)).astype(BF)
-        up_ref[level] = up
+        up = mm(cot_ref[:, first : first + width], shift_ref[LANES - offset : LANES - offset + width])
+        totals.append(jnp.sum(up, axis=0, keepdims=True))
+        up = up.astype(BF)
+        up_ref[level * PATCHES : (level + 1) * PATCHES] = up
         dctx = dot(up, both, ((1,), (1,))).astype(BF)
         dctx_ref[level] = dctx
         dsum = dsum + dctx.astype(F32)
     dsum_ref[...] = dsum
+    totals.append(jnp.zeros((LANES - OUTS - PLEV, LANES), F32))
+    totals_ref[...] = jnp.concatenate(totals, axis=0)
 
 
 def decode_kernel(
-    flag_ref, own_ref, north_ref, corner_ref, west_ref, perm_ref, wkv_ref, queries_ref, up_ref, dctx_ref, dsum_ref,
-    map_ref, base_ref, wv_ref,
+    flag_ref, own_ref, north_ref, corner_ref, west_ref, perm_ref, wkv_ref, up_ref, dctx_ref, dsum_ref,
+    map_ref, base_ref, wv_ref, spread_ref, gather_ref, shift_ref, totals_ref,
     owned_ref, fields_ref, keep_ref, send_ref,
     value, weights, dvalues, context, products, fields, sums, owned, decoded_out, sems,
 ):
@@ -263,8 +274,7 @@
     normed = layer_norm(wide)
     key = mm(normed, wkv_ref[:, :D]).astype(BF)
     value[...] = mm(normed, wv_ref[...]).astype(BF).astype(F32)
-    queries = spread_queries(queries_ref[...].astype(F32)).astype(BF)
-    scores = dot(key, queries, ((1,), (1,))) * 0.125
+    scores = dot(key, spread_ref[...], ((1,), (1,))) * 0.125
     slabs = [scores[l * PATCHES : (l + 1) * PATCHES] for l in range(LEV)]
     top = jnp.maximum(jnp.maximum(slabs[0], slabs[1]), jnp.maximum(slabs[2], slabs[3]))
     slabs = [jnp.exp(s - top) for s in slabs]
@@ -298,13 +308,12 @@
             dvalues[at[l]] = found[l]
         dvalues[at[LEV - 1]] = dsum_ref[start : start + BLOCK] - (found[0] + found[1] + found[2])
     fields[...] = jnp.zeros_like(fields)
-    row = lax.broadcasted_iota(jnp.int32, (PLEV * LANES, LANES), 0)
-    c = lax.broadcasted_iota(jnp.int32, (PLEV * LANES, LANES), 1)
-    slopes = mm(products[...], jnp.where(row // 16 == c, 1.0, 0.0).astype(BF))
+    slopes = mm(products[...], gather_ref[...])
     for level in range(PLEV):
         first, offset, width = spot(level)
         decoded = mm(context[level * PATCHES : (level + 1) * PATCHES], map_ref[...]) + base_ref[level : level + 1]
-        fields[:, first : first + width] += dot(decoded.astype(BF), shift_matrix(offset, width), ((1,), (1,)))
+        shift = shift_ref[LANES - offset : LANES - offset + width]
+        fields[:, first : first + width] += dot(decoded.astype(BF), shift, ((1,), (1,)))
     decoded_out[...] = fields[...].astype(BF)
     fields_copy = pltpu.make_async_copy(decoded_out, fields_ref, sems.at[1])
     fields_copy.start()
@@ -315,13 +324,9 @@
     dscores = jnp.concatenate(dscores, axis=0).astype(BF)
     sums[:D] = dot(normed, dvalues[...].astype(BF), ((0,), (0,)))
     sums[D : D + LANES] = dot(dscores, normed, ((0,), (0,)))
-    up = jnp.concatenate([up_ref[a] for a in range(PLEV)], axis=0)
-    outer = dot(up, context[...], ((0,), (0,)))
+    outer = dot(up_ref[...], context[...], ((0,), (0,)))
     sums[D + LANES : D + LANES + OUTS] = outer[:OUTS]
-    totals = [jnp.sum(up_ref[a].astype(F32), axis=0, keepdims=True) for a in range(PLEV)]
-    totals.append(jnp.zeros((LANES - OUTS - PLEV, LANES), F32))
-    totals = jnp.concatenate(totals, axis=0)
-    sums[D + LANES + OUTS :] = jnp.concatenate([totals, jnp.zeros((LANES - OUTS, D - LANES), F32)], axis=1)
+    sums[D + LANES + OUTS :] = jnp.concatenate([totals_ref[...], jnp.zeros((LANES - OUTS, D - LANES), F32)], axis=1)
     second = flag_ref[0, 0] > 0
     top, bottom = sums[: ROWS // 2], sums[ROWS // 2 :]
     keep_ref[...] = jnp.where(second, bottom, top).astype(BF)
@@ -459,10 +464,10 @@
         limit=48,
     )(flag, jnp.asarray(extra), main, north, corner, west, w_qkv, w_out)
     north, corner, west = move(north, 1, 0), move(corner, 1, 1), move(west, 0, 1)
-    up, dctx, dsum, both, base, wv, own, far_perm = call(
+    up, dctx, dsum, both, base, wv, own, far_perm, spread, gather, shift, totals = call(
         pre_kernel,
         [
-            struct((PLEV, PATCHES, LANES)),
+            struct((PLEV * PATCHES, LANES)),
             struct((PLEV, PATCHES, D)),
             struct((PATCHES, D), F32),
             struct((D, LANES)),
@@ -470,6 +475,10 @@
             struct((D, D)),
             struct((TOKENS, D)),
             struct((TOKENS, PACKED - MAIN)),
+            struct((LANES, D)),
+            struct((PLEV * LANES, LANES)),
+            struct((3 * LANES, LANES)),
+            struct((LANES - OUTS, LANES), F32),
         ],
         "VVVVVHHH",
     )(
@@ -487,7 +496,7 @@
     owned, fields, keep, send = call(
         decode_kernel,
         [struct((TOKENS, D)), struct((PATCHES, PLEV * OUTS)), share, share],
-        "SVVVVVVVVVVVVV",
+        "S" + "V" * 16,
         [
             pltpu.VMEM((TOKENS, D), F32),
             pltpu.VMEM((TOKENS, LANES), F32),
@@ -501,7 +510,7 @@
             pltpu.SemaphoreType.DMA((2,)),
         ],
         out_specs=[pl.BlockSpec(memory_space=pl.ANY)] * 2 + [pl.BlockSpec(memory_space=pltpu.VMEM)] * 2,
-    )(core, own, north, corner, west, far_perm, w_kv, level_queries, up, dctx, dsum, both, base, wv)
+    )(core, own, north, corner, west, far_perm, w_kv, up, dctx, dsum, both, base, wv, spread, gather, shift, totals)
     mine, other = sum_over_all(keep, send)
     kv, query, out, pixels = call(
         final_kernel,

time: 94.7 us -> 94.9 us (level)
  no operation moved by 1% of the time
where the time goes in v9:
time: 94.9 us; the launch traced here: 94.6 us
  blocking collectives  35.6 us (38%)
  Pallas kernels  24.7 us (26%)
  starting transfers between devices  21.9 us (23%)
  waiting for transfers between devices  10.6 us (11%)
  local copies, waits for them, and re-layouts  0.96 us (1%)
    pallas_call x7, Pallas kernels, close(): return run(*held)  24.7 us
    ppermute x6, starting transfers between devices, move(): return lax.ppermute(array, LAT + LON, route)  15.4 us
    all_to_all x1, blocking collectives, sum_over_all(): mine = add_up(lax.all_to_all(copies(mine, 'z'), 'z', 0, 0, tiled=True))  12.3 us
    all_to_all x1, blocking collectives, sum_over_all(): lax.all_to_all(mine.reshape(chips, rows // chips, width), PLANE, 0, 0, ti...  11.9 us
    all_to_all x1, blocking collectives, sum_over_all(): lax.all_to_all(copies(mine, PLANE), PLANE, 0, 0, tiled=True)  11.4 us
    ppermute x6, waiting for transfers between devices, move(): return lax.ppermute(array, LAT + LON, route)  7.88 us
    ppermute x2, starting transfers between devices, swap(): lax.ppermute(array, 'core', [(i, (i + 1) % count) for i in range(count)])  6.47 us
    ppermute x2, waiting for transfers between devices, swap(): lax.ppermute(array, 'core', [(i, (i + 1) % count) for i in range(count)])  2.7 us
  transfers between devices with their start and end apart: 8, of which 4 were waited for; matrix products, arithmetic and copies ran while one was open for 1% of the time, Pallas kernels for 7%

profile of v9, /device:TPU:1, one launch (start us, length us, event | category | flops | bytes accessed | tf_op | source)
XLA Modules:
  0.0 94.6 jit_solution(12024940071491017703)
XLA Ops:
  0.6 0.0 copy-start.2
  0.6 2.6 %shard_map.218 = (bf16[224,512]{1,0:T(8,128)(2,1)}, bf16[80,512]{1,0:T(8,128)(2,1)}, bf16[80,512]{1,0:T(8,128)(2,1)}) custom-call(bf16[576,512]{1,0:T(8,128)(2,1)} %bitcast.14, s32[6,24]{1,0:T(8,128)} %ids_ref.3, bf16[384,576]{1,0:T(8,128)(2,1)} %constant.42.clone.perm_ref, bf16[24,2048]{1,0:T(8,128)(2,1)} %constant.43.clone.columns_ref, ...), custom_call_target="tpu_custom_call" | custom-call | tf_op jit(solution)/shard_map/pallas_call | solution.py:393
  3.2 8.9 %collective-permute-start = (bf16[224,512]{1,0:T(8,128)(2,1)}, bf16[224,512]{1,0:T(8,128)(2,1)}, u32[]{:S(2)}, u32[]{:S(2)}) collective-permute-start(bf16[224,512]{1,0:T(8,128)(2,1)} %get-tuple-element.36), channel_id=1, source_target_pairs={{0,240},{1,241},{2,242},{3,243},{4,244},{5,245},{6,246},{7,247},{8... | collective-permute-start | bytes 688136 | tf_op jit(solution)/shard_map/ppermute | solution.py:413
  12.1 1.1 %collective-permute-start.1 = (bf16[80,512]{1,0:T(8,128)(2,1)}, bf16[80,512]{1,0:T(8,128)(2,1)}, u32[]{:S(2)}, u32[]{:S(2)}) collective-permute-start(bf16[80,512]{1,0:T(8,128)(2,1)} %get-tuple-element.37), channel_id=1, source_target_pairs={{0,255},{1,240},{2,241},{3,242},{4,243},{5,244},{6,245},{7,246},{8... | collective-permute-start | bytes 245768 | tf_op jit(solution)/shard_map/ppermute | solution.py:413
  13.2 2.6 %collective-permute-start.2 = (bf16[80,512]{1,0:T(8,128)(2,1)}, bf16[80,512]{1,0:T(8,128)(2,1)}, u32[]{:S(2)}, u32[]{:S(2)}) collective-permute-start(bf16[80,512]{1,0:T(8,128)(2,1)} %get-tuple-element.38), channel_id=1, source_target_pairs={{0,15},{1,0},{2,1},{3,2},{4,3},{5,4},{6,5},{7,6},{8,7},{9,8},{10,9... | collective-permute-start | bytes 245768 | tf_op jit(solution)/shard_map/ppermute | solution.py:413
  15.8 1.9 %shard_map.217 = (bf16[224,512]{1,0:T(8,128)(2,1)S(1)}, bf16[512,512]{1,0:T(8,128)(2,1)S(1)}) custom-call(bf16[576,512]{1,0:T(8,128)(2,1)} %bitcast.15, s32[6,24]{1,0:T(8,128)} %ids_ref.3, bf16[224,576]{1,0:T(8,128)(2,1)} %constant.45.clone.perm_ref, bf16[24,1024]{1,0:T(8,128)(2,1)} %constant.46.clone.columns_ref, f32[8,1024]{1,0:T(8,128)} %constant.47.clone.rows_ref, ...), custom_call_target="tpu_custom_call" | custom-call | tf_op jit(solution)/shard_map/pallas_call | solution.py:393
  17.7 1.6 %collective-permute-done.1.corner_ref = bf16[80,512]{1,0:T(8,128)(2,1)} collective-permute-done((bf16[80,512]{1,0:T(8,128)(2,1)}, bf16[80,512]{1,0:T(8,128)(2,1)}, u32[]{:S(2)}, u32[]{:S(2)}) %collective-permute-start.1) | collective-permute-done | bytes 81952 | tf_op jit(solution)/shard_map/ppermute | solution.py:413
  19.3 0.0 collective-permute-done.2.west_ref
  19.3 0.0 collective-permute-done.north_ref
  19.3 0.0 copy-done.2
  19.3 5.4 %shard_map.219 = (bf16[224,512]{1,0:T(8,128)(2,1)}, bf16[224,512]{1,0:T(8,128)(2,1)}, bf16[80,512]{1,0:T(8,128)(2,1)}, bf16[80,512]{1,0:T(8,128)(2,1)}) custom-call(s32[1,1]{1,0:T(1,128)} %bitcast.3.flag_ref, f32[8,256]{1,0:T(8,128)} %constant.48.clone.extra_ref, bf16[224,512]{1,0:T(8,128)(2,1)S(1)} %get-tuple-element.35.main_ref, ...), custom_call_target="tpu_custom_call" | custom-call | tf_op jit(solution)/shard_map/pallas_call | solution.py:393
  24.7 1.2 %collective-permute-start.3 = (bf16[224,512]{1,0:T(8,128)(2,1)}, bf16[224,512]{1,0:T(8,128)(2,1)S(1)}, u32[]{:S(2)}, u32[]{:S(2)}) collective-permute-start(bf16[224,512]{1,0:T(8,128)(2,1)} %get-tuple-element.42), channel_id=1, source_target_pairs={{0,16},{1,17},{2,18},{3,19},{4,20},{5,21},{6,22},{7,23},{8,24},{9,... | collective-permute-start | bytes 688136 | tf_op jit(solution)/shard_map/ppermute | solution.py:413
  25.9 0.0 collective-permute-start.4
  25.9 1.6 %collective-permute-start.5 = (bf16[80,512]{1,0:T(8,128)(2,1)}, bf16[80,512]{1,0:T(8,128)(2,1)S(1)}, u32[]{:S(2)}, u32[]{:S(2)}) collective-permute-start(bf16[80,512]{1,0:T(8,128)(2,1)} %get-tuple-element.44), channel_id=1, source_target_pairs={{0,1},{1,2},{2,3},{3,4},{4,5},{5,6},{6,7},{7,8},{8,9},{9,10},{10,1... | collective-permute-start | bytes 245768 | tf_op jit(solution)/shard_map/ppermute | solution.py:413
  27.5 0.9 pad.4.whead_ref
  28.4 0.0 copy-done
  28.5 0.0 copy-done.1
  28.5 4.8 %shard_map.220 = (bf16[1872,128]{1,0:T(8,128)(2,1)S(1)}, bf16[13,144,512]{2,1,0:T(8,128)(2,1)S(1)}, f32[144,512]{1,0:T(8,128)S(1)}, bf16[512,128]{1,0:T(8,128)(2...) custom-call(bf16[144,1040]{1,0:T(8,128)(2,1)S(1)} %bitcast.13, ...), custom_call_target="tpu_custom_call" | custom-call | tf_op jit(solution)/shard_map/pallas_call | solution.py:393
  33.3 6.3 %collective-permute-done.4.corner_ref = bf16[80,512]{1,0:T(8,128)(2,1)S(1)} collective-permute-done((bf16[80,512]{1,0:T(8,128)(2,1)}, bf16[80,512]{1,0:T(8,128)(2,1)S(1)}, u32[]{:S(2)}, u32[]{:S(2)}) %collective-permute-start.4) | collective-permute-done | bytes 81952 | tf_op jit(solution)/shard_map/ppermute | solution.py:413
  39.6 0.0 collective-permute-done.5.west_ref
  39.6 0.0 collective-permute-done.3.north_ref
  39.6 6.6 %shard_map.221 = (bf16[576,512]{1,0:T(8,128)(2,1)}, bf16[144,1040]{1,0:T(8,128)(2,1)}, bf16[384,512]{1,0:T(8,128)(2,1)S(1)}, bf16[384,512]{1,0:T(8,128)(2,1)S(1)}) custom-call(s32[1,1]{1,0:T(1,128)} %bitcast.flag_ref, bf16[576,512]{1,0:T(8,128)(2,1)S(1)} %get-tuple-element.41.own_ref, bf16[224,512]{1,0:T(8,128)(2,1)S(1)} %collective-permute-done.3.north_ref, ...), custom_call_target="tpu_custom_call" | custom-call | tf_op jit(solution)/shard_map/pallas_call | solution.py:393
  46.2 2.2 %collective-permute-start.6 = (bf16[384,512]{1,0:T(8,128)(2,1)S(1)}, bf16[384,512]{1,0:T(8,128)(2,1)S(1)}, u32[]{:S(2)}, u32[]{:S(2)}) collective-permute-start(bf16[384,512]{1,0:T(8,128)(2,1)S(1)} %get-tuple-element.59), channel_id=1, source_target_pairs={{0,1},{1,0},{2,3},{3,2},{4,5},{5,4},{6,7},{7,6},{8,9},{9,8},{10,11... | collective-permute-start | bytes 1179656 | tf_op jit(solution)/shard_map/ppermute | solution.py:418
  48.4 1.3 %collective-permute-done.6.right_ref = bf16[384,512]{1,0:T(8,128)(2,1)S(1)} collective-permute-done((bf16[384,512]{1,0:T(8,128)(2,1)S(1)}, bf16[384,512]{1,0:T(8,128)(2,1)S(1)}, u32[]{:S(2)}, u32[]{:S(2)}) %collective-permute-start.6) | collective-permute-done | bytes 393248 | tf_op jit(solution)/shard_map/ppermute | solution.py:418
  49.7 0.1 shard_map.222
  49.8 11.9 %all_to_all.15 = bf16[16,24,512]{2,1,0:T(8,128)(2,1)S(1)} all-to-all(bf16[16,24,512]{2,1,0:T(8,128)(2,1)S(1)} %bitcast.10), channel_id=1, replica_groups=mesh['z'=8,'x_hi'=2,'x_lo'=2,'y'=4,'core'=2] {'x_hi','x_lo','y'}, dimensions={0} | all-to-all | bytes 786432 | tf_op jit(solution)/shard_map/all_to_all | solution.py:433
  61.8 0.1 reduce_sum.24
  61.9 12.3 %all_to_all.16 = bf16[8,24,512]{2,1,0:T(8,128)(2,1)S(1)} all-to-all(bf16[8,24,512]{2,1,0:T(8,128)(2,1)S(1)} %broadcast_in_dim.4), channel_id=1, replica_groups=mesh['z'=8,'x_hi'=2,'x_lo'=2,'y'=4,'core'=2] {'z'}, dimensions={0} | all-to-all | bytes 393216 | tf_op jit(solution)/shard_map/all_to_all | solution.py:434
  74.2 11.4 %all_to_all.17 = bf16[16,24,512]{2,1,0:T(8,128)(2,1)S(1)} all-to-all(bf16[16,24,512]{2,1,0:T(8,128)(2,1)S(1)} %broadcast_in_dim.5), channel_id=1, replica_groups=mesh['z'=8,'x_hi'=2,'x_lo'=2,'y'=4,'core'=2] {'x_hi','x_lo','y'}, dimensions={0} | all-to-all | bytes 786432 | tf_op jit(solution)/shard_map/all_to_all | solution.py:435
  85.6 4.3 %collective-permute-start.7 = (bf16[384,512]{1,0:T(8,128)(2,1)S(1)}, bf16[384,512]{1,0:T(8,128)(2,1)S(1)}, u32[]{:S(2)}, u32[]{:S(2)}) collective-permute-start(bf16[384,512]{1,0:T(8,128)(2,1)S(1)} %bitcast.11), channel_id=1, source_target_pairs={{0,1},{1,0},{2,3},{3,2},{4,5},{5,4},{6,7},{7,6},{8,9},{9,8},{10,11... | collective-permute-start | bytes 1179656 | tf_op jit(solution)/shard_map/ppermute | solution.py:418
  89.9 1.3 %collective-permute-done.7.other_ref = bf16[384,512]{1,0:T(8,128)(2,1)S(1)} collective-permute-done((bf16[384,512]{1,0:T(8,128)(2,1)S(1)}, bf16[384,512]{1,0:T(8,128)(2,1)S(1)}, u32[]{:S(2)}, u32[]{:S(2)}) %collective-permute-start.7) | collective-permute-done | bytes 393248 | tf_op jit(solution)/shard_map/ppermute | solution.py:418
  91.3 3.3 %shard_map.223 = (f32[512,1024]{1,0:T(8,128)}, f32[13,512]{1,0:T(8,128)}, f32[512,512]{1,0:T(8,128)}, f32[80,512]{1,0:T(8,128)}) custom-call(s32[1,1]{1,0:T(1,128)} %bitcast.flag_ref, bf16[384,512]{1,0:T(8,128)(2,1)S(1)} %bitcast.12, bf16[384,512]{1,0:T(8,128)(2,1)S(1)} %collective-permute-done.7.other_ref, bf16[512,1024]{1,0:T(8,128)(2,1)S(1)} %copy-done, ...), custom_call_target="tpu_custom_call" | custom-call | tf_op jit(solution)/shard_map/pallas_call | solution.py:393
  (9 shorter events, 0.1 us)
Async XLA Ops:
  0.6 18.7 %copy-start.2 = (bf16[512,1536]{1,0:T(8,128)(2,1)S(1)}, bf16[512,1536]{1,0:T(8,128)(2,1)}, u32[]{:S(2)}) copy-start(bf16[512,1536]{1,0:T(8,128)(2,1)} %wqkv_ref.1) | copy-start | bytes 4718596
  3.2 16.0 %collective-permute-start = (bf16[224,512]{1,0:T(8,128)(2,1)}, bf16[224,512]{1,0:T(8,128)(2,1)}, u32[]{:S(2)}, u32[]{:S(2)}) collective-permute-start(bf16[224,512]{1,0:T(8,128)(2,1)} %get-tuple-element.36), channel_id=1, source_target_pairs={{0,240},{1,241},{2,242},{3,243},{4,244},{5,245},{6,246},{7,247},{8... | collective-permute-start | bytes 688136 | tf_op jit(solution)/shard_map/ppermute | solution.py:413
  12.1 7.2 %collective-permute-start.1 = (bf16[80,512]{1,0:T(8,128)(2,1)}, bf16[80,512]{1,0:T(8,128)(2,1)}, u32[]{:S(2)}, u32[]{:S(2)}) collective-permute-start(bf16[80,512]{1,0:T(8,128)(2,1)} %get-tuple-element.37), channel_id=1, source_target_pairs={{0,255},{1,240},{2,241},{3,242},{4,243},{5,244},{6,245},{7,246},{8... | collective-permute-start | bytes 245768 | tf_op jit(solution)/shard_map/ppermute | solution.py:413
  13.2 6.1 %collective-permute-start.2 = (bf16[80,512]{1,0:T(8,128)(2,1)}, bf16[80,512]{1,0:T(8,128)(2,1)}, u32[]{:S(2)}, u32[]{:S(2)}) collective-permute-start(bf16[80,512]{1,0:T(8,128)(2,1)} %get-tuple-element.38), channel_id=1, source_target_pairs={{0,15},{1,0},{2,1},{3,2},{4,3},{5,4},{6,5},{7,6},{8,7},{9,8},{10,9... | collective-permute-start | bytes 245768 | tf_op jit(solution)/shard_map/ppermute | solution.py:413
  15.8 12.6 %copy-start = (bf16[512,1024]{1,0:T(8,128)(2,1)S(1)}, bf16[512,1024]{1,0:T(8,128)(2,1)}, u32[]{:S(2)}) copy-start(bf16[512,1024]{1,0:T(8,128)(2,1)} %wkv_ref.5) | copy-start | bytes 3145732
  15.8 12.6 %copy-start.1 = (bf16[512,512]{1,0:T(8,128)(2,1)S(1)}, bf16[512,512]{1,0:T(8,128)(2,1)}, u32[]{:S(2)}) copy-start(bf16[512,512]{1,0:T(8,128)(2,1)} %wo_ref.3) | copy-start | bytes 1572868
  15.8 12.6 %copy-start.3 = (bf16[6,24,1040]{2,1,0:T(8,128)(2,1)S(1)}, bf16[6,24,1040]{2,1,0:T(8,128)(2,1)}, u32[]{:S(2)}) copy-start(bf16[6,24,1040]{2,1,0:T(8,128)(2,1)} %param.26) | copy-start | bytes 898564
  15.8 12.6 %copy-start.4 = (bf16[13,512]{1,0:T(8,128)(2,1)S(1)}, bf16[13,512]{1,0:T(8,128)(2,1)}, u32[]{:S(2)}) copy-start(bf16[13,512]{1,0:T(8,128)(2,1)} %queries_ref.3) | copy-start | bytes 39940
  24.7 14.9 %collective-permute-start.3 = (bf16[224,512]{1,0:T(8,128)(2,1)}, bf16[224,512]{1,0:T(8,128)(2,1)S(1)}, u32[]{:S(2)}, u32[]{:S(2)}) collective-permute-start(bf16[224,512]{1,0:T(8,128)(2,1)} %get-tuple-element.42), channel_id=1, source_target_pairs={{0,16},{1,17},{2,18},{3,19},{4,20},{5,21},{6,22},{7,23},{8,24},{9,... | collective-permute-start | bytes 688136 | tf_op jit(solution)/shard_map/ppermute | solution.py:413
  25.9 13.6 %collective-permute-start.4 = (bf16[80,512]{1,0:T(8,128)(2,1)}, bf16[80,512]{1,0:T(8,128)(2,1)S(1)}, u32[]{:S(2)}, u32[]{:S(2)}) collective-permute-start(bf16[80,512]{1,0:T(8,128)(2,1)} %get-tuple-element.43), channel_id=1, source_target_pairs={{0,17},{1,18},{2,19},{3,20},{4,21},{5,22},{6,23},{7,24},{8,25},{9,... | collective-permute-start | bytes 245768 | tf_op jit(solution)/shard_map/ppermute | solution.py:413
  25.9 13.6 %collective-permute-start.5 = (bf16[80,512]{1,0:T(8,128)(2,1)}, bf16[80,512]{1,0:T(8,128)(2,1)S(1)}, u32[]{:S(2)}, u32[]{:S(2)}) collective-permute-start(bf16[80,512]{1,0:T(8,128)(2,1)} %get-tuple-element.44), channel_id=1, source_target_pairs={{0,1},{1,2},{2,3},{3,4},{4,5},{5,6},{6,7},{7,8},{8,9},{9,10},{10,1... | collective-permute-start | bytes 245768 | tf_op jit(solution)/shard_map/ppermute | solution.py:413
  46.2 3.5 %collective-permute-start.6 = (bf16[384,512]{1,0:T(8,128)(2,1)S(1)}, bf16[384,512]{1,0:T(8,128)(2,1)S(1)}, u32[]{:S(2)}, u32[]{:S(2)}) collective-permute-start(bf16[384,512]{1,0:T(8,128)(2,1)S(1)} %get-tuple-element.59), channel_id=1, source_target_pairs={{0,1},{1,0},{2,3},{3,2},{4,5},{5,4},{6,7},{7,6},{8,9},{9,8},{10,11... | collective-permute-start | bytes 1179656 | tf_op jit(solution)/shard_map/ppermute | solution.py:418
  85.6 5.6 %collective-permute-start.7 = (bf16[384,512]{1,0:T(8,128)(2,1)S(1)}, bf16[384,512]{1,0:T(8,128)(2,1)S(1)}, u32[]{:S(2)}, u32[]{:S(2)}) collective-permute-start(bf16[384,512]{1,0:T(8,128)(2,1)S(1)} %bitcast.11), channel_id=1, source_target_pairs={{0,1},{1,0},{2,3},{3,2},{4,5},{5,4},{6,7},{7,6},{8,9},{9,8},{10,11... | collective-permute-start | bytes 1179656 | tf_op jit(solution)/shard_map/ppermute | solution.py:418

commit v10 on v8

--- a/solution.py
+++ b/solution.py
@@ -36,7 +36,7 @@
 
 LAT = ("z", "x_hi")
 LON = ("x_lo", "y", "core")
-PLANE = ("x_hi", "x_lo", "y")
+PLANE = ("y", "x_hi", "x_lo")
 
 norm_eps = 1e-05
 clip_eps = 1e-06

time: 94.7 us -> 94.8 us (level)
  no operation moved by 1% of the time
where the time goes in v10:
time: 94.8 us; the launch traced here: 94.5 us
  blocking collectives  35.8 us (38%)
  Pallas kernels  24.4 us (26%)
  starting transfers between devices  21.8 us (23%)
  waiting for transfers between devices  10.7 us (11%)
  local copies, waits for them, and re-layouts  0.96 us (1%)
    pallas_call x7, Pallas kernels, close(): return run(*held)  24.4 us
    ppermute x6, starting transfers between devices, move(): return lax.ppermute(array, LAT + LON, route)  15.4 us
    all_to_all x1, blocking collectives, sum_over_all(): mine = add_up(lax.all_to_all(copies(mine, 'z'), 'z', 0, 0, tiled=True))  12.4 us
    all_to_all x1, blocking collectives, sum_over_all(): lax.all_to_all(mine.reshape(chips, rows // chips, width), PLANE, 0, 0, ti...  12.2 us
    all_to_all x1, blocking collectives, sum_over_all(): lax.all_to_all(copies(mine, PLANE), PLANE, 0, 0, tiled=True)  11.3 us
    ppermute x6, waiting for transfers between devices, move(): return lax.ppermute(array, LAT + LON, route)  7.96 us
    ppermute x2, starting transfers between devices, swap(): lax.ppermute(array, 'core', [(i, (i + 1) % count) for i in range(count)])  6.39 us
    ppermute x2, waiting for transfers between devices, swap(): lax.ppermute(array, 'core', [(i, (i + 1) % count) for i in range(count)])  2.7 us
  transfers between devices with their start and end apart: 8, of which 4 were waited for; matrix products, arithmetic and copies ran while one was open for 1% of the time, Pallas kernels for 7%

profile of v10, /device:TPU:1, one launch (start us, length us, event | category | flops | bytes accessed | tf_op | source)
XLA Modules:
  0.0 94.5 jit_solution(15182220176756390139)
XLA Ops:
  0.6 0.0 copy-start.2
  0.6 2.6 %shard_map.218 = (bf16[224,512]{1,0:T(8,128)(2,1)}, bf16[80,512]{1,0:T(8,128)(2,1)}, bf16[80,512]{1,0:T(8,128)(2,1)}) custom-call(bf16[576,512]{1,0:T(8,128)(2,1)} %bitcast.14, s32[6,24]{1,0:T(8,128)} %ids_ref.3, bf16[384,576]{1,0:T(8,128)(2,1)} %constant.42.clone.perm_ref, bf16[24,2048]{1,0:T(8,128)(2,1)} %constant.43.clone.columns_ref, ...), custom_call_target="tpu_custom_call" | custom-call | tf_op jit(solution)/shard_map/pallas_call | solution.py:388
  3.2 8.9 %collective-permute-start = (bf16[224,512]{1,0:T(8,128)(2,1)}, bf16[224,512]{1,0:T(8,128)(2,1)}, u32[]{:S(2)}, u32[]{:S(2)}) collective-permute-start(bf16[224,512]{1,0:T(8,128)(2,1)} %get-tuple-element.32), channel_id=1, source_target_pairs={{0,240},{1,241},{2,242},{3,243},{4,244},{5,245},{6,246},{7,247},{8... | collective-permute-start | bytes 688136 | tf_op jit(solution)/shard_map/ppermute | solution.py:408
  12.1 1.1 %collective-permute-start.1 = (bf16[80,512]{1,0:T(8,128)(2,1)}, bf16[80,512]{1,0:T(8,128)(2,1)}, u32[]{:S(2)}, u32[]{:S(2)}) collective-permute-start(bf16[80,512]{1,0:T(8,128)(2,1)} %get-tuple-element.33), channel_id=1, source_target_pairs={{0,255},{1,240},{2,241},{3,242},{4,243},{5,244},{6,245},{7,246},{8... | collective-permute-start | bytes 245768 | tf_op jit(solution)/shard_map/ppermute | solution.py:408
  13.2 2.6 %collective-permute-start.2 = (bf16[80,512]{1,0:T(8,128)(2,1)}, bf16[80,512]{1,0:T(8,128)(2,1)}, u32[]{:S(2)}, u32[]{:S(2)}) collective-permute-start(bf16[80,512]{1,0:T(8,128)(2,1)} %get-tuple-element.34), channel_id=1, source_target_pairs={{0,15},{1,0},{2,1},{3,2},{4,3},{5,4},{6,5},{7,6},{8,7},{9,8},{10,9... | collective-permute-start | bytes 245768 | tf_op jit(solution)/shard_map/ppermute | solution.py:408
  15.8 1.9 %shard_map.217 = (bf16[224,512]{1,0:T(8,128)(2,1)S(1)}, bf16[512,512]{1,0:T(8,128)(2,1)S(1)}) custom-call(bf16[576,512]{1,0:T(8,128)(2,1)} %bitcast.15, s32[6,24]{1,0:T(8,128)} %ids_ref.3, bf16[224,576]{1,0:T(8,128)(2,1)} %constant.45.clone.perm_ref, bf16[24,1024]{1,0:T(8,128)(2,1)} %constant.46.clone.columns_ref, f32[8,1024]{1,0:T(8,128)} %constant.47.clone.rows_ref, ...), custom_call_target="tpu_custom_call" | custom-call | tf_op jit(solution)/shard_map/pallas_call | solution.py:388
  17.7 1.6 %collective-permute-done.1.corner_ref = bf16[80,512]{1,0:T(8,128)(2,1)} collective-permute-done((bf16[80,512]{1,0:T(8,128)(2,1)}, bf16[80,512]{1,0:T(8,128)(2,1)}, u32[]{:S(2)}, u32[]{:S(2)}) %collective-permute-start.1) | collective-permute-done | bytes 81952 | tf_op jit(solution)/shard_map/ppermute | solution.py:408
  19.3 0.0 collective-permute-done.2.west_ref
  19.3 0.0 collective-permute-done.north_ref
  19.3 0.0 copy-done.2
  19.3 5.4 %shard_map.219 = (bf16[224,512]{1,0:T(8,128)(2,1)}, bf16[224,512]{1,0:T(8,128)(2,1)}, bf16[80,512]{1,0:T(8,128)(2,1)}, bf16[80,512]{1,0:T(8,128)(2,1)}) custom-call(s32[1,1]{1,0:T(1,128)} %bitcast.3.flag_ref, f32[8,256]{1,0:T(8,128)} %constant.48.clone.extra_ref, bf16[224,512]{1,0:T(8,128)(2,1)S(1)} %get-tuple-element.31.main_ref, ...), custom_call_target="tpu_custom_call" | custom-call | tf_op jit(solution)/shard_map/pallas_call | solution.py:388
  24.7 1.2 %collective-permute-start.3 = (bf16[224,512]{1,0:T(8,128)(2,1)}, bf16[224,512]{1,0:T(8,128)(2,1)S(1)}, u32[]{:S(2)}, u32[]{:S(2)}) collective-permute-start(bf16[224,512]{1,0:T(8,128)(2,1)} %get-tuple-element.38), channel_id=1, source_target_pairs={{0,16},{1,17},{2,18},{3,19},{4,20},{5,21},{6,22},{7,23},{8,24},{9,... | collective-permute-start | bytes 688136 | tf_op jit(solution)/shard_map/ppermute | solution.py:408
  25.9 0.0 collective-permute-start.4
  25.9 1.6 %collective-permute-start.5 = (bf16[80,512]{1,0:T(8,128)(2,1)}, bf16[80,512]{1,0:T(8,128)(2,1)S(1)}, u32[]{:S(2)}, u32[]{:S(2)}) collective-permute-start(bf16[80,512]{1,0:T(8,128)(2,1)} %get-tuple-element.40), channel_id=1, source_target_pairs={{0,1},{1,2},{2,3},{3,4},{4,5},{5,6},{6,7},{7,8},{8,9},{9,10},{10,1... | collective-permute-start | bytes 245768 | tf_op jit(solution)/shard_map/ppermute | solution.py:408
  27.5 0.9 pad.4.whead_ref
  28.4 0.0 copy-done
  28.5 0.0 copy-done.1
  28.5 4.7 %shard_map.220 = (bf16[13,144,128]{2,1,0:T(8,128)(2,1)S(1)}, bf16[13,144,512]{2,1,0:T(8,128)(2,1)S(1)}, f32[144,512]{1,0:T(8,128)S(1)}, bf16[512,128]{1,0:T(8,12...) custom-call(bf16[144,1040]{1,0:T(8,128)(2,1)S(1)} %bitcast.13, ...), custom_call_target="tpu_custom_call" | custom-call | tf_op jit(solution)/shard_map/pallas_call | solution.py:388
  33.2 6.4 %collective-permute-done.4.corner_ref = bf16[80,512]{1,0:T(8,128)(2,1)S(1)} collective-permute-done((bf16[80,512]{1,0:T(8,128)(2,1)}, bf16[80,512]{1,0:T(8,128)(2,1)S(1)}, u32[]{:S(2)}, u32[]{:S(2)}) %collective-permute-start.4) | collective-permute-done | bytes 81952 | tf_op jit(solution)/shard_map/ppermute | solution.py:408
  39.6 0.0 collective-permute-done.5.west_ref
  39.6 0.0 collective-permute-done.3.north_ref
  39.6 6.4 %shard_map.221 = (bf16[576,512]{1,0:T(8,128)(2,1)}, bf16[144,1040]{1,0:T(8,128)(2,1)}, bf16[384,512]{1,0:T(8,128)(2,1)S(1)}, bf16[384,512]{1,0:T(8,128)(2,1)S(1)}) custom-call(s32[1,1]{1,0:T(1,128)} %bitcast.flag_ref, bf16[576,512]{1,0:T(8,128)(2,1)S(1)} %get-tuple-element.37.own_ref, bf16[224,512]{1,0:T(8,128)(2,1)S(1)} %collective-permute-done.3.north_ref, ...), custom_call_target="tpu_custom_call" | custom-call | tf_op jit(solution)/shard_map/pallas_call | solution.py:388
  46.0 2.2 %collective-permute-start.6 = (bf16[384,512]{1,0:T(8,128)(2,1)S(1)}, bf16[384,512]{1,0:T(8,128)(2,1)S(1)}, u32[]{:S(2)}, u32[]{:S(2)}) collective-permute-start(bf16[384,512]{1,0:T(8,128)(2,1)S(1)} %get-tuple-element.51), channel_id=1, source_target_pairs={{0,1},{1,0},{2,3},{3,2},{4,5},{5,4},{6,7},{7,6},{8,9},{9,8},{10,11... | collective-permute-start | bytes 1179656 | tf_op jit(solution)/shard_map/ppermute | solution.py:413
  48.2 1.3 %collective-permute-done.6.right_ref = bf16[384,512]{1,0:T(8,128)(2,1)S(1)} collective-permute-done((bf16[384,512]{1,0:T(8,128)(2,1)S(1)}, bf16[384,512]{1,0:T(8,128)(2,1)S(1)}, u32[]{:S(2)}, u32[]{:S(2)}) %collective-permute-start.6) | collective-permute-done | bytes 393248 | tf_op jit(solution)/shard_map/ppermute | solution.py:413
  49.5 0.1 shard_map.222
  49.6 12.2 %all_to_all.15 = bf16[16,24,512]{2,1,0:T(8,128)(2,1)S(1)} all-to-all(bf16[16,24,512]{2,1,0:T(8,128)(2,1)S(1)} %bitcast.10), channel_id=1, replica_groups=mesh['z'=8,'x_hi'=2,'x_lo'=2,'y'=4,'core'=2] {'y','x_hi','x_lo'}, dimensions={0} | all-to-all | bytes 786432 | tf_op jit(solution)/shard_map/all_to_all | solution.py:428
  61.8 0.1 reduce_sum.24
  61.9 12.4 %all_to_all.16 = bf16[8,24,512]{2,1,0:T(8,128)(2,1)S(1)} all-to-all(bf16[8,24,512]{2,1,0:T(8,128)(2,1)S(1)} %broadcast_in_dim.4), channel_id=1, replica_groups=mesh['z'=8,'x_hi'=2,'x_lo'=2,'y'=4,'core'=2] {'z'}, dimensions={0} | all-to-all | bytes 393216 | tf_op jit(solution)/shard_map/all_to_all | solution.py:429
  74.3 11.3 %all_to_all.17 = bf16[16,24,512]{2,1,0:T(8,128)(2,1)S(1)} all-to-all(bf16[16,24,512]{2,1,0:T(8,128)(2,1)S(1)} %broadcast_in_dim.5), channel_id=1, replica_groups=mesh['z'=8,'x_hi'=2,'x_lo'=2,'y'=4,'core'=2] {'y','x_hi','x_lo'}, dimensions={0} | all-to-all | bytes 786432 | tf_op jit(solution)/shard_map/all_to_all | solution.py:430
  85.6 4.2 %collective-permute-start.7 = (bf16[384,512]{1,0:T(8,128)(2,1)S(1)}, bf16[384,512]{1,0:T(8,128)(2,1)S(1)}, u32[]{:S(2)}, u32[]{:S(2)}) collective-permute-start(bf16[384,512]{1,0:T(8,128)(2,1)S(1)} %bitcast.11), channel_id=1, source_target_pairs={{0,1},{1,0},{2,3},{3,2},{4,5},{5,4},{6,7},{7,6},{8,9},{9,8},{10,11... | collective-permute-start | bytes 1179656 | tf_op jit(solution)/shard_map/ppermute | solution.py:413
  89.8 1.3 %collective-permute-done.7.other_ref = bf16[384,512]{1,0:T(8,128)(2,1)S(1)} collective-permute-done((bf16[384,512]{1,0:T(8,128)(2,1)S(1)}, bf16[384,512]{1,0:T(8,128)(2,1)S(1)}, u32[]{:S(2)}, u32[]{:S(2)}) %collective-permute-start.7) | collective-permute-done | bytes 393248 | tf_op jit(solution)/shard_map/ppermute | solution.py:413
  91.2 3.3 %shard_map.223 = (f32[512,1024]{1,0:T(8,128)}, f32[13,512]{1,0:T(8,128)}, f32[512,512]{1,0:T(8,128)}, f32[80,512]{1,0:T(8,128)}) custom-call(s32[1,1]{1,0:T(1,128)} %bitcast.flag_ref, bf16[384,512]{1,0:T(8,128)(2,1)S(1)} %bitcast.12, bf16[384,512]{1,0:T(8,128)(2,1)S(1)} %collective-permute-done.7.other_ref, bf16[512,1024]{1,0:T(8,128)(2,1)S(1)} %copy-done, ...), custom_call_target="tpu_custom_call" | custom-call | tf_op jit(solution)/shard_map/pallas_call | solution.py:388
  (9 shorter events, 0.1 us)
Async XLA Ops:
  0.6 18.7 %copy-start.2 = (bf16[512,1536]{1,0:T(8,128)(2,1)S(1)}, bf16[512,1536]{1,0:T(8,128)(2,1)}, u32[]{:S(2)}) copy-start(bf16[512,1536]{1,0:T(8,128)(2,1)} %wqkv_ref.1) | copy-start | bytes 4718596
  3.2 16.0 %collective-permute-start = (bf16[224,512]{1,0:T(8,128)(2,1)}, bf16[224,512]{1,0:T(8,128)(2,1)}, u32[]{:S(2)}, u32[]{:S(2)}) collective-permute-start(bf16[224,512]{1,0:T(8,128)(2,1)} %get-tuple-element.32), channel_id=1, source_target_pairs={{0,240},{1,241},{2,242},{3,243},{4,244},{5,245},{6,246},{7,247},{8... | collective-permute-start | bytes 688136 | tf_op jit(solution)/shard_map/ppermute | solution.py:408
  12.1 7.2 %collective-permute-start.1 = (bf16[80,512]{1,0:T(8,128)(2,1)}, bf16[80,512]{1,0:T(8,128)(2,1)}, u32[]{:S(2)}, u32[]{:S(2)}) collective-permute-start(bf16[80,512]{1,0:T(8,128)(2,1)} %get-tuple-element.33), channel_id=1, source_target_pairs={{0,255},{1,240},{2,241},{3,242},{4,243},{5,244},{6,245},{7,246},{8... | collective-permute-start | bytes 245768 | tf_op jit(solution)/shard_map/ppermute | solution.py:408
  13.2 6.1 %collective-permute-start.2 = (bf16[80,512]{1,0:T(8,128)(2,1)}, bf16[80,512]{1,0:T(8,128)(2,1)}, u32[]{:S(2)}, u32[]{:S(2)}) collective-permute-start(bf16[80,512]{1,0:T(8,128)(2,1)} %get-tuple-element.34), channel_id=1, source_target_pairs={{0,15},{1,0},{2,1},{3,2},{4,3},{5,4},{6,5},{7,6},{8,7},{9,8},{10,9... | collective-permute-start | bytes 245768 | tf_op jit(solution)/shard_map/ppermute | solution.py:408
  15.8 12.6 %copy-start = (bf16[512,1024]{1,0:T(8,128)(2,1)S(1)}, bf16[512,1024]{1,0:T(8,128)(2,1)}, u32[]{:S(2)}) copy-start(bf16[512,1024]{1,0:T(8,128)(2,1)} %wkv_ref.5) | copy-start | bytes 3145732
  15.8 12.6 %copy-start.1 = (bf16[512,512]{1,0:T(8,128)(2,1)S(1)}, bf16[512,512]{1,0:T(8,128)(2,1)}, u32[]{:S(2)}) copy-start(bf16[512,512]{1,0:T(8,128)(2,1)} %wo_ref.3) | copy-start | bytes 1572868
  15.8 12.6 %copy-start.3 = (bf16[6,24,1040]{2,1,0:T(8,128)(2,1)S(1)}, bf16[6,24,1040]{2,1,0:T(8,128)(2,1)}, u32[]{:S(2)}) copy-start(bf16[6,24,1040]{2,1,0:T(8,128)(2,1)} %param.26) | copy-start | bytes 898564
  15.8 12.6 %copy-start.4 = (bf16[13,512]{1,0:T(8,128)(2,1)S(1)}, bf16[13,512]{1,0:T(8,128)(2,1)}, u32[]{:S(2)}) copy-start(bf16[13,512]{1,0:T(8,128)(2,1)} %queries_ref.5) | copy-start | bytes 39940
  24.7 14.9 %collective-permute-start.3 = (bf16[224,512]{1,0:T(8,128)(2,1)}, bf16[224,512]{1,0:T(8,128)(2,1)S(1)}, u32[]{:S(2)}, u32[]{:S(2)}) collective-permute-start(bf16[224,512]{1,0:T(8,128)(2,1)} %get-tuple-element.38), channel_id=1, source_target_pairs={{0,16},{1,17},{2,18},{3,19},{4,20},{5,21},{6,22},{7,23},{8,24},{9,... | collective-permute-start | bytes 688136 | tf_op jit(solution)/shard_map/ppermute | solution.py:408
  25.9 13.6 %collective-permute-start.4 = (bf16[80,512]{1,0:T(8,128)(2,1)}, bf16[80,512]{1,0:T(8,128)(2,1)S(1)}, u32[]{:S(2)}, u32[]{:S(2)}) collective-permute-start(bf16[80,512]{1,0:T(8,128)(2,1)} %get-tuple-element.39), channel_id=1, source_target_pairs={{0,17},{1,18},{2,19},{3,20},{4,21},{5,22},{6,23},{7,24},{8,25},{9,... | collective-permute-start | bytes 245768 | tf_op jit(solution)/shard_map/ppermute | solution.py:408
  25.9 13.6 %collective-permute-start.5 = (bf16[80,512]{1,0:T(8,128)(2,1)}, bf16[80,512]{1,0:T(8,128)(2,1)S(1)}, u32[]{:S(2)}, u32[]{:S(2)}) collective-permute-start(bf16[80,512]{1,0:T(8,128)(2,1)} %get-tuple-element.40), channel_id=1, source_target_pairs={{0,1},{1,2},{2,3},{3,4},{4,5},{5,6},{6,7},{7,8},{8,9},{9,10},{10,1... | collective-permute-start | bytes 245768 | tf_op jit(solution)/shard_map/ppermute | solution.py:408
  46.0 3.5 %collective-permute-start.6 = (bf16[384,512]{1,0:T(8,128)(2,1)S(1)}, bf16[384,512]{1,0:T(8,128)(2,1)S(1)}, u32[]{:S(2)}, u32[]{:S(2)}) collective-permute-start(bf16[384,512]{1,0:T(8,128)(2,1)S(1)} %get-tuple-element.51), channel_id=1, source_target_pairs={{0,1},{1,0},{2,3},{3,2},{4,5},{5,4},{6,7},{7,6},{8,9},{9,8},{10,11... | collective-permute-start | bytes 1179656 | tf_op jit(solution)/shard_map/ppermute | solution.py:413
  85.6 5.6 %collective-permute-start.7 = (bf16[384,512]{1,0:T(8,128)(2,1)S(1)}, bf16[384,512]{1,0:T(8,128)(2,1)S(1)}, u32[]{:S(2)}, u32[]{:S(2)}) collective-permute-start(bf16[384,512]{1,0:T(8,128)(2,1)S(1)} %bitcast.11), channel_id=1, source_target_pairs={{0,1},{1,0},{2,3},{3,2},{4,5},{5,4},{6,7},{7,6},{8,9},{9,8},{10,11... | collective-permute-start | bytes 1179656 | tf_op jit(solution)/shard_map/ppermute | solution.py:413
